TPU v7x, 128 devices: a whole 4x4x4 slice. The times are simulated.
128 devices in a mesh: fsdp: 16 (over y, x), tp: 8 (over z, core).
Axes of the slice: x: 4, y: 4, z: 4, core: 2. Of those that a mesh axis runs over, the one named last changes fastest.
Arguments:
- grad: bfloat16 [8192, 15360], P('fsdp', 'tp'), may hold values from -6 to 6
- start_basis: bfloat16 [8192, 512], P('fsdp'), may hold values from -6 to 6
- weight: bfloat16 [8192, 15360], P('fsdp', 'tp'), may hold values from -1.1953125 to 1.1953125
- first_moment: float32 [512, 15360], P('fsdp', 'tp'), may hold values from -3 to 3
- second_moment: float32 [512, 15360], P('fsdp', 'tp'), may hold values from 0.2 to 8
Outputs:
- first_basis: bfloat16 [8192, 512], P('fsdp')
- new_basis: bfloat16 [8192, 512], P('fsdp')
- moment_one: float32 [512, 15360], P('fsdp', 'tp')
- moment_two: float32 [512, 15360], P('fsdp', 'tp')
- new_weight: bfloat16 [8192, 15360], P('fsdp', 'tp')
All inputs are finite; a program needn't handle non-finite values.
Results may differ from a plain program's by a relative error of at most 0.022.
Values may be sent and summed in bfloat16 or wider, within the bound.
No kernel may reach another device: no remote copies, remote signals or barrier semaphores. Data moves between devices by JAX's collectives and lax.ppermute only.
A program may use at most 128 MiB of HBM per device.

v0:
```python
import math

import jax
import jax.numpy as jnp
from jax import lax
from jax.sharding import PartitionSpec as P

M = 8192


BETA_ONE = 0.9
BETA_TWO = 0.95
ADAM_EPS = 1e-06
STEP_SIZE = 2.0


def contract_rows(left, right, exact_mode):
    if exact_mode:
        return lax.dot_general(
            left,
            right,
            (((0,), (0,)), ((), ())),
            precision=lax.Precision.HIGHEST,
            preferred_element_type=jnp.float32,
        )
    return lax.dot_general(
        left, right, (((0,), (0,)), ((), ())), preferred_element_type=jnp.float32
    )


def range_image(grad, basis_b, inv_sqrt):
    grad_block = grad
    summed = lax.psum_scatter(
        contract_rows(grad_block, basis_b, False), "fsdp", scatter_dimension=0, tiled=True
    )
    panel_rows = (summed * inv_sqrt).astype(jnp.bfloat16)
    grad_block = grad
    partial_image = jnp.dot(
        grad_block,
        lax.all_gather(panel_rows, "fsdp", axis=0, tiled=True),
        preferred_element_type=jnp.float32,
    )
    return lax.psum(partial_image, "tp")


def solve_basis(image_rows, factor):
    return lax.linalg.triangular_solve(
        factor, image_rows, left_side=False, lower=True, transpose_a=True
    )


def per_device(grad, start_basis, weight, first_moment, second_moment):
    share_rows = first_moment.shape[0]
    inv_sqrt = 1.0 / math.sqrt(M)
    start_f32 = start_basis.astype(jnp.float32)
    basis_b = start_basis
    image_rows = range_image(grad, basis_b, inv_sqrt)
    gram_whole = (
        lax.psum(contract_rows(image_rows, image_rows, True).astype(jnp.bfloat16), "fsdp").astype(
            jnp.float32
        )
        / M
    )
    factor = jnp.linalg.cholesky(gram_whole)
    basis_b = solve_basis(image_rows, factor).astype(jnp.bfloat16)
    first_basis = basis_b
    image_rows = range_image(grad, basis_b, inv_sqrt)
    gram_whole = lax.psum(contract_rows(image_rows, image_rows, True), "fsdp") / M
    factor = jnp.linalg.cholesky(gram_whole)
    exact = solve_basis(image_rows, factor)
    margin = (
        lax.psum(contract_rows(exact, start_f32, True).astype(jnp.bfloat16), "fsdp").astype(
            jnp.float32
        )
        / M
    )
    basis_b = exact.astype(jnp.bfloat16)
    my_offset = lax.axis_index("fsdp") * share_rows
    basis_cols = basis_b
    reduced = (
        lax.psum_scatter(
            contract_rows(basis_cols, grad, False).astype(jnp.bfloat16),
            "fsdp",
            scatter_dimension=0,
            tiled=True,
        ).astype(jnp.float32)
        * inv_sqrt
    )
    moment_all, second_all = (
        lax.all_gather(first_moment.astype(jnp.bfloat16), "fsdp", axis=0, tiled=True).astype(
            first_moment.dtype
        ),
        lax.all_gather(second_moment.astype(jnp.bfloat16), "fsdp", axis=0, tiled=True).astype(
            second_moment.dtype
        ),
    )
    margin_rows = lax.dynamic_slice_in_dim(margin, my_offset, share_rows, 0)
    rotated_one = jnp.dot(margin_rows, moment_all, precision=lax.Precision.HIGHEST)
    rotated_two = jnp.dot(margin_rows * margin_rows, second_all, precision=lax.Precision.HIGHEST)
    moment_one = BETA_ONE * rotated_one + (1.0 - BETA_ONE) * reduced
    moment_two = BETA_TWO * rotated_two + (1.0 - BETA_TWO) * reduced * reduced
    direction = (moment_one / (jnp.sqrt(moment_two) + ADAM_EPS)).astype(jnp.bfloat16)
    basis_cols = basis_b
    expanded = jnp.dot(
        basis_cols,
        lax.all_gather(direction, "fsdp", axis=0, tiled=True),
        preferred_element_type=jnp.float32,
    )
    new_weight = (weight.astype(jnp.float32) - STEP_SIZE * inv_sqrt * expanded).astype(jnp.bfloat16)
    return (first_basis, basis_b, moment_one, moment_two, new_weight)


def solution(mesh):
    in_specs = (P("fsdp", "tp"), P("fsdp", None), P("fsdp", "tp"), P("fsdp", "tp"), P("fsdp", "tp"))
    out_specs = (
        P("fsdp", None),
        P("fsdp", None),
        P("fsdp", "tp"),
        P("fsdp", "tp"),
        P("fsdp", "tp"),
    )
    return jax.shard_map(
        per_device, mesh=mesh, in_specs=in_specs, out_specs=out_specs, check_vma=False
    )
```

profile of v0, /device:TPU:0, one launch (start us, length us, event | category | flops | bytes accessed | tf_op | source)
XLA Modules:
  0.0 1165.2 jit_solution(15331760740006657409)
XLA Ops:
  12.9 79.2 %reduce-scatter.10.cloned.1.call-done = f32[120,512]{1,0:T(8,128)} async-done(((f32[1920,512]{1,0:T(8,128)}), f32[120,512]{1,0:T(8,128)}) %reduce-scatter.10.cloned.1.call-update) | async-done | bytes 245776
  93.9 44.9 %all-gather.6.cloned.1.call-done = bf16[1920,512]{1,0:T(8,128)(2,1)} async-done(((bf16[120,512]{1,0:T(8,128)(2,1)}), bf16[1920,512]{1,0:T(8,128)(2,1)}) %all-gather.6.cloned.1.call-update) | async-done | bytes 1966096 | tf_op jit(solution)/shard_map/all_gather | solution.py:40
  142.6 62.2 %all-reduce.9.cloned.1.call-done = f32[512,512]{0,1:T(8,128)} async-done(((f32[512,512]{0,1:T(8,128)}), f32[512,512]{0,1:T(8,128)}) %all-reduce.9.cloned.1.call-update) | async-done | bytes 1048592 | tf_op jit(solution)/shard_map/psum | solution.py:43
  209.3 84.1 %all-reduce.11.cloned.1.call-done = bf16[512,512]{0,1:T(8,128)(2,1)} async-done(((bf16[512,512]{0,1:T(8,128)(2,1)}), bf16[512,512]{0,1:T(8,128)(2,1)}) %all-reduce.11.cloned.1.call-update) | async-done | bytes 524304 | tf_op jit(solution)/shard_map/psum | solution.py:59
  298.4 11.7 %cholesky.286 = f32[128,128]{1,0:T(8,128)S(1)} custom-call(f32[128,128]{1,0:T(8,128)S(1)} %cholesky.426), custom_call_target="Cholesky" | custom-call | tf_op jit(solution)/shard_map/jit(cholesky)/cholesky | solution.py:64
  310.2 9.8 custom-call.27
  324.3 11.7 %cholesky.305 = f32[128,128]{1,0:T(8,128)S(1)} custom-call(f32[128,128]{1,0:T(8,128)S(1)} %cholesky.430), custom_call_target="Cholesky" | custom-call | tf_op jit(solution)/shard_map/jit(cholesky)/cholesky | solution.py:64
  336.6 10.0 custom-call.28
  349.0 11.7 %cholesky.326 = f32[128,128]{1,0:T(8,128)S(1)} custom-call(f32[128,128]{1,0:T(8,128)S(1)} %cholesky.435), custom_call_target="Cholesky" | custom-call | tf_op jit(solution)/shard_map/jit(cholesky)/cholesky | solution.py:64
  362.0 9.8 custom-call.29
  374.0 11.7 %cholesky.343 = f32[128,128]{1,0:T(8,128)S(1)} custom-call(f32[128,128]{1,0:T(8,128)S(1)} %convolution_subtract_fusion.11), custom_call_target="Cholesky" | custom-call | tf_op jit(solution)/shard_map/jit(cholesky)/cholesky | solution.py:64
  393.1 11.6 while.4
  404.7 39.3 %custom-call.30 = f32[4,128,128]{1,2,0:T(8,128)S(1)} custom-call(f32[4,128,128]{2,1,0:T(8,128)S(1)} %get-tuple-element.21), custom_call_target="InvertDiagBlocksLowerTriangular" | custom-call | tf_op jit(solution)/shard_map/triangular_solve/custom-call.3 | solution.py:47
  453.9 76.2 %reduce-scatter.12.cloned.1.call-done = f32[120,512]{1,0:T(8,128)} async-done(((f32[1920,512]{1,0:T(8,128)}), f32[120,512]{1,0:T(8,128)}) %reduce-scatter.12.cloned.1.call-update) | async-done | bytes 245776
  531.8 45.0 %all-gather.8.cloned.1.call-done = bf16[1920,512]{1,0:T(8,128)(2,1)} async-done(((bf16[120,512]{1,0:T(8,128)(2,1)}), bf16[1920,512]{1,0:T(8,128)(2,1)}) %all-gather.8.cloned.1.call-update) | async-done | bytes 1966096 | tf_op jit(solution)/shard_map/all_gather | solution.py:40
  580.7 62.1 %all-reduce.13.cloned.1.call-done = f32[512,512]{0,1:T(8,128)} async-done(((f32[512,512]{0,1:T(8,128)}), f32[512,512]{0,1:T(8,128)}) %all-reduce.13.cloned.1.call-update) | async-done | bytes 1048592 | tf_op jit(solution)/shard_map/psum | solution.py:43
  642.8 4.4 fusion.77
  648.2 85.2 %all-reduce.15.cloned.1.call-done = f32[512,512]{0,1:T(8,128)} async-done(((f32[512,512]{0,1:T(8,128)}), f32[512,512]{0,1:T(8,128)}) %all-reduce.15.cloned.1.call-update) | async-done | bytes 1048592 | tf_op jit(solution)/shard_map/psum | solution.py:68
  740.8 11.7 %cholesky.358 = f32[128,128]{1,0:T(8,128)S(1)} custom-call(f32[128,128]{1,0:T(8,128)S(1)} %cholesky.439), custom_call_target="Cholesky" | custom-call | tf_op jit(solution)/shard_map/jit(cholesky)/cholesky | solution.py:69
  753.6 9.8 custom-call.31
  766.7 11.7 %cholesky.377 = f32[128,128]{1,0:T(8,128)S(1)} custom-call(f32[128,128]{1,0:T(8,128)S(1)} %cholesky.443), custom_call_target="Cholesky" | custom-call | tf_op jit(solution)/shard_map/jit(cholesky)/cholesky | solution.py:69
  780.4 10.0 custom-call.32
  792.8 11.7 %cholesky.398 = f32[128,128]{1,0:T(8,128)S(1)} custom-call(f32[128,128]{1,0:T(8,128)S(1)} %cholesky.448), custom_call_target="Cholesky" | custom-call | tf_op jit(solution)/shard_map/jit(cholesky)/cholesky | solution.py:69
  805.1 9.8 custom-call.33
  817.2 11.7 %cholesky.415 = f32[128,128]{1,0:T(8,128)S(1)} custom-call(f32[128,128]{1,0:T(8,128)S(1)} %convolution_subtract_fusion.10), custom_call_target="Cholesky" | custom-call | tf_op jit(solution)/shard_map/jit(cholesky)/cholesky | solution.py:69
  836.0 11.7 %while.5 = (s32[]{:T(128)}, f32[512,512]{1,0:T(8,128)}, s32[4,2]{0,1:T(2,128)S(1)}, f32[4,128,128]{2,1,0:T(8,128)S(1)}, s32[]{:T(128)}) while((s32[]{:T(128)}, f32[512,512]{1,0:T(8,128)}, s32[4,2]{0,1:T(2,128)S(1)}, f32[4,128,128]{2,1,0:T(8,128)S(1)}, s32[]{:T(128)}) %tuple.90), condition=%wide.while_cond.clone, body=%wide.while_body.clone.sunk | while | flops 2 | bytes 131181 | solution.py:47
  847.7 39.3 %custom-call.34 = f32[4,128,128]{1,2,0:T(8,128)S(1)} custom-call(f32[4,128,128]{2,1,0:T(8,128)S(1)} %get-tuple-element.22), custom_call_target="InvertDiagBlocksLowerTriangular" | custom-call | tf_op jit(solution)/shard_map/triangular_solve/custom-call.3 | solution.py:47
  903.1 79.1 %all-reduce.17.cloned.1.call-done = bf16[512,512]{0,1:T(8,128)(2,1)} async-done(((bf16[512,512]{0,1:T(8,128)(2,1)}), bf16[512,512]{0,1:T(8,128)(2,1)}) %all-reduce.17.cloned.1.call-update) | async-done | bytes 524304 | tf_op jit(solution)/shard_map/psum | solution.py:72
  982.1 77.3 %reduce-scatter.8.cloned.1.call-done = bf16[32,1920]{1,0:T(8,128)(2,1)} async-done(((bf16[512,1920]{1,0:T(8,128)(2,1)}), bf16[32,1920]{1,0:T(8,128)(2,1)}) %reduce-scatter.8.cloned.1.call-update) | async-done | bytes 122896 | tf_op jit(solution)/shard_map/reduce_scatter | solution.py:81
  1062.1 43.9 %all-gather.10.cloned.1.call-done = bf16[512,1920]{1,0:T(8,128)(2,1)} async-done(((bf16[32,1920]{1,0:T(8,128)(2,1)}), bf16[512,1920]{1,0:T(8,128)(2,1)}) %all-gather.10.cloned.1.call-update) | async-done | bytes 1966096 | tf_op jit(solution)/shard_map/all_gather | solution.py:90
  1111.5 42.0 %all-gather.14.cloned.1.call-done = bf16[512,1920]{1,0:T(8,128)(2,1)} async-done(((bf16[32,1920]{1,0:T(8,128)(2,1)}), bf16[512,1920]{1,0:T(8,128)(2,1)}) %all-gather.14.cloned.1.call-update) | async-done | bytes 1966096 | tf_op jit(solution)/shard_map/all_gather | solution.py:106
  1153.6 4.7 subtract_convert_fusion
  (161 shorter events, 123.2 us)
Async XLA Ops:
  7.2 1.6 copy-start
  7.2 85.0 %reduce-scatter.10.cloned.1.call-start = ((), (), s32[]{:S(2)}) async-start(), calls=%async_computation.14 | async-start | bytes 4177920
  12.9 125.9 %all-gather.6.cloned.1.call-start = ((), (), s32[]{:S(2)}) async-start(), calls=%async_computation.3 | async-start | bytes 2088960 | tf_op jit(solution)/shard_map/all_gather | solution.py:40
  93.8 111.0 %all-reduce.9.cloned.1.call-start = ((), (), s32[]{:S(2)}) async-start(), calls=%async_computation.4 | async-start | bytes 2097152 | tf_op jit(solution)/shard_map/psum | solution.py:43
  142.6 150.8 %all-reduce.11.cloned.1.call-start = ((), (), s32[]{:S(2)}) async-start(), calls=%async_computation.5 | async-start | bytes 1048576 | tf_op jit(solution)/shard_map/psum | solution.py:59
  209.0 321.1 %reduce-scatter.12.cloned.1.call-start = ((), (), s32[]{:S(2)}) async-start(), calls=%async_computation.15 | async-start | bytes 4177920
  293.4 3.8 copy-start.9
  297.4 1.0 copy-start.7
  361.3 82.7 %copy-start.2 = (f32[512,512]{0,1:T(8,128)S(1)}, f32[512,512]{0,1:T(8,128)}, u32[]{:S(2)}) copy-start(f32[512,512]{0,1:T(8,128)} %all-reduce.9.cloned.1.call-done) | copy-start | bytes 3145732
  450.0 0.8 copy-start.3
  453.9 122.9 %all-gather.8.cloned.1.call-start = ((), (), s32[]{:S(2)}) async-start(), calls=%async_computation.6 | async-start | bytes 2088960 | tf_op jit(solution)/shard_map/all_gather | solution.py:40
  531.8 111.0 %all-reduce.13.cloned.1.call-start = ((), (), s32[]{:S(2)}) async-start(), calls=%async_computation.7 | async-start | bytes 2097152 | tf_op jit(solution)/shard_map/psum | solution.py:43
  580.6 66.6 %copy-start.14 = (f32[32,1920]{1,0:T(8,128)S(1)}, f32[32,1920]{1,0:T(8,128)}, u32[]{:S(2)}) copy-start(f32[32,1920]{1,0:T(8,128)} %param.12) | copy-start | bytes 737284
  580.7 152.8 %all-reduce.15.cloned.1.call-start = ((), (), s32[]{:S(2)}) async-start(), calls=%async_computation.8 | async-start | bytes 2097152 | tf_op jit(solution)/shard_map/psum | solution.py:68
  647.2 255.9 %all-gather.12.cloned.1.call-start = ((), (), s32[]{:S(2)}) async-start(), calls=%async_computation.12 | async-start | bytes 2088960 | tf_op jit(solution)/shard_map/all_gather | solution.py:93
  648.0 334.2 %all-reduce.17.cloned.1.call-start = ((), (), s32[]{:S(2)}) async-start(), calls=%async_computation.9 | async-start | bytes 1048576 | tf_op jit(solution)/shard_map/psum | solution.py:72
  733.4 4.9 copy-start.5
  739.8 1.0 copy-start.6
  805.1 81.9 %copy-start.1 = (f32[512,512]{0,1:T(8,128)S(1)}, f32[512,512]{0,1:T(8,128)}, u32[]{:S(2)}) copy-start(f32[512,512]{0,1:T(8,128)} %all-reduce.13.cloned.1.call-done) | copy-start | bytes 3145732
  887.0 0.7 copy-start.13
  890.2 5.6 copy-start.11
  892.9 3.0 copy-start.8
  897.8 161.7 %reduce-scatter.8.cloned.1.call-start = ((), (), s32[]{:S(2)}) async-start(), calls=%async_computation.11 | async-start | bytes 2088960 | tf_op jit(solution)/shard_map/reduce_scatter | solution.py:81
  901.4 0.9 copy-start.15
  901.4 204.7 %all-gather.10.cloned.1.call-start = ((), (), s32[]{:S(2)}) async-start(), calls=%async_computation.10 | async-start | bytes 2088960 | tf_op jit(solution)/shard_map/all_gather | solution.py:90
  903.0 250.6 %all-gather.14.cloned.1.call-start = ((), (), s32[]{:S(2)}) async-start(), calls=%async_computation.13 | async-start | bytes 2088960 | tf_op jit(solution)/shard_map/all_gather | solution.py:106
  1059.5 46.6 %copy-start.12 = (bf16[32,1920]{1,0:T(8,128)(2,1)S(1)}, bf16[32,1920]{1,0:T(8,128)(2,1)}, u32[]{:S(2)}) copy-start(bf16[32,1920]{1,0:T(8,128)(2,1)} %reduce-scatter.8.cloned.1.call-done) | copy-start | bytes 368644
  1062.1 48.4 %copy-start.10 = (f32[32,1920]{1,0:T(8,128)}, f32[32,1920]{1,0:T(8,128)S(1)}, u32[]{:S(2)}) copy-start(f32[32,1920]{1,0:T(8,128)S(1)} %fusion) | copy-start | bytes 737284
  1062.1 47.4 %copy-start.4 = (bf16[512,512]{0,1:T(8,128)(2,1)S(1)}, bf16[512,512]{0,1:T(8,128)(2,1)}, u32[]{:S(2)}) copy-start(bf16[512,512]{0,1:T(8,128)(2,1)} %copy-done.3) | copy-start | bytes 1572868
Sparse Core Ops, SparseCore 0:
  13.0 79.1 reduce-scatter.9
  94.9 43.8 all-gather.5
  142.7 62.0 all-reduce.8
  209.1 84.1 all-reduce.10
  454.0 76.0 reduce-scatter.11
  532.9 43.8 all-gather.7
  580.8 62.0 all-reduce.12
  647.3 86.0 all-reduce.14
  736.3 44.4 all-gather.11
  897.9 84.2 all-reduce.16
  986.0 73.4 reduce-scatter.7
  1062.3 43.7 all-gather.9
  1109.6 43.8 all-gather.13
where the time goes:
time: 1170 us
  waiting for transfers between devices  781 us (67%)
  other arithmetic  257 us (22%)
  matrix products  68.5 us (6%)
  local copies, waits for them, and re-layouts  36.9 us (3%)
  between operations  20 us (2%)
    another operation x29, other arithmetic, per_device(): factor = jnp.linalg.cholesky(gram_whole)  162 us
    unnamed x15, waiting for transfers between devices  156 us
    psum x2, waiting for transfers between devices, range_image(): return lax.psum(partial_image, 'tp')  124 us
    all_gather x2, waiting for transfers between devices, range_image(): lax.all_gather(panel_rows, 'fsdp', axis=0, tiled=True)  89.9 us
    psum x1, waiting for transfers between devices, per_device(): lax.psum(contract_rows(image_rows, image_rows, True), 'fsdp') / M  85.2 us
    psum x1, waiting for transfers between devices, per_device(): lax.psum(contract_rows(image_rows, image_rows, True).astype(jnp.bfloat16)...  84.1 us
    another operation x5, other arithmetic, solve_basis(): lax.linalg.triangular_solve(factor, image_rows, left_side=False, lower=Tr...  83.7 us
    psum x1, waiting for transfers between devices, per_device(): lax.psum(contract_rows(exact, start_f32, True).astype(jnp.bfloat16), 'fsdp')  79.1 us
  transfers between devices with their start and end apart: 13, of which 12 were waited for; matrix products, arithmetic and copies ran while one was open for 15% of the time, Pallas kernels for 0%

commit v1 on v0

v1 whole, which is shorter than its diff:
```python
import math

import jax
import jax.numpy as jnp
from jax import lax
from jax.experimental import pallas as pl
from jax.experimental.pallas import tpu as pltpu
from jax.sharding import PartitionSpec as P

M = 8192

BETA_ONE = 0.9
BETA_TWO = 0.95
ADAM_EPS = 1e-06
STEP_SIZE = 2.0

BF = jnp.bfloat16
F32 = jnp.float32

def elim(read, n=128):
    lane = lax.broadcasted_iota(jnp.int32, (8, n), 1)
    sub = lax.broadcasted_iota(jnp.int32, (8, n), 0)
    G = [read(g) for g in range(n // 8)]
    out = []
    for g0 in range(n // 8):
        acc = jnp.zeros((8, n), jnp.float32)
        for s0 in range(8):
            j = g0 * 8 + s0
            hit = lane == j
            r = jnp.broadcast_to(G[g0][s0:s0 + 1, :], (8, n))
            p = jnp.broadcast_to(r[:, j:j + 1], (8, n))
            row = jnp.where(lane < j, r, jnp.where(hit, 1.0, 0.0)) * lax.rsqrt(p)
            acc = jnp.where(sub == s0, row, acc)
            rr = jnp.where(hit, 1.0, r) * (1.0 / p)
            for g in range(g0, n // 8):
                c = jnp.broadcast_to(G[g][:, j:j + 1], (8, n))
                new = jnp.where(hit, 0.0, G[g]) - c * rr
                G[g] = jnp.where(sub > s0, new, G[g]) if g == g0 else new
        out.append(acc)
    return out

def dot(a, b, dims):
    return lax.dot_general(a, b, (dims, ((), ())), precision=lax.Precision.HIGHEST, preferred_element_type=jnp.float32)

NB = 128
def chol_kernel(a_ref, x_ref, w_ref, s_ref, b_ref):
    n = a_ref.shape[0]
    s_ref[...] = a_ref[...]
    b_ref[...] = jnp.zeros_like(b_ref)
    nb = n // NB
    for k in range(nb):
        lo = k * NB
        for g, v in enumerate(elim(lambda g: s_ref[pl.ds(lo + 8 * g, 8), pl.ds(lo, NB)])):
            w_ref[pl.ds(8 * g, 8), :] = v
        w = w_ref[...]
        if k:
            xk = dot(w, b_ref[lo:lo + NB, :lo], ((1,), (0,)))
            x_ref[lo:lo + NB, :lo] = xk
        x_ref[lo:lo + NB, lo:lo + NB] = w
        if lo + NB < n:
            x_ref[lo:lo + NB, lo + NB:] = jnp.zeros((NB, n - lo - NB), jnp.float32)
            hi = lo + NB
            u = dot(w, s_ref[lo:hi, hi:], ((1,), (0,)))
            s_ref[hi:, hi:] -= dot(u, u, ((0,), (0,)))
            b_ref[hi:, :hi] -= dot(u, x_ref[lo:hi, :hi], ((0,), (0,)))

def chol_inv(a):
    n = a.shape[0]
    return pl.pallas_call(
        chol_kernel,
        out_shape=jax.ShapeDtypeStruct((n, n), jnp.float32),
        in_specs=[pl.BlockSpec(memory_space=pltpu.VMEM)],
        out_specs=pl.BlockSpec(memory_space=pltpu.VMEM),
        scratch_shapes=[pltpu.VMEM((NB, NB), jnp.float32), pltpu.VMEM((n, n), jnp.float32), pltpu.VMEM((n, n), jnp.float32)],
        compiler_params=pltpu.CompilerParams(vmem_limit_bytes=32 * 2**20),
    )(a)


def mm(a, b, ca, cb):
    return lax.dot_general(a, b, (((ca,), (cb,)), ((), ())), preferred_element_type=F32)


def mm_split(a, b, ca, cb):
    hi = b.astype(BF)
    lo = (b - hi.astype(F32)).astype(BF)
    return mm(a, hi, ca, cb) + mm(a, lo, ca, cb)


def mm_split2(a, b, ca, cb):
    hi = a.astype(BF)
    lo = (a - hi.astype(F32)).astype(BF)
    return mm_split(hi, b, ca, cb) + mm(lo, b.astype(BF), ca, cb)


def scatter_sum(x, axis, n):
    parts = lax.all_to_all(x.astype(BF).reshape(n, x.shape[0] // n, x.shape[1]), axis, 0, 0, tiled=True)
    return jnp.sum(parts.astype(F32), axis=0)


def gather(x, axis, n):
    parts = lax.all_to_all(jnp.broadcast_to(x[None], (n,) + x.shape), axis, 0, 0, tiled=True)
    return parts.reshape(n * x.shape[0], x.shape[1])


def per_device(nf, nt, grad, start_basis, weight, first_moment, second_moment):
    inv_sqrt = 1.0 / math.sqrt(M)
    share_rows, cols = first_moment.shape
    share_cols = cols // nf
    rank = start_basis.shape[1]

    moments = jnp.concatenate([first_moment.astype(BF), second_moment.astype(BF)], axis=0)
    moments = moments.T.reshape(nf, share_cols, 2 * share_rows)
    moments = lax.all_to_all(moments, "fsdp", 0, 0, tiled=True).transpose(1, 0, 2)
    first_t = moments[:, :, :share_rows].reshape(share_cols, rank)
    second_t = moments[:, :, share_rows:].reshape(share_cols, rank)

    panel = (scatter_sum(mm(grad, start_basis, 0, 0), "fsdp", nf) * inv_sqrt).astype(BF)
    panel = gather(panel, "fsdp", nf)
    image = scatter_sum(mm(grad, panel, 1, 0), "tp", nt).astype(BF)
    image = lax.all_gather(image, "tp", axis=0, tiled=True)
    gram = scatter_sum(mm(image, image, 0, 0), "fsdp", nf)
    gram = lax.all_gather(gram.astype(BF), "fsdp", axis=0, tiled=True).astype(F32) / M
    inverse = chol_inv(gram)
    first_basis = mm_split(image, inverse, 1, 1).astype(BF)
    raw = scatter_sum(mm(grad, image, 0, 0), "fsdp", nf)
    panel = (mm_split2(raw, inverse, 1, 1) * inv_sqrt).astype(BF)

    panel = gather(panel, "fsdp", nf)
    image = scatter_sum(mm(grad, panel, 1, 0), "tp", nt).astype(BF)
    image = lax.all_gather(image, "tp", axis=0, tiled=True)
    both = mm(image, jnp.concatenate([image, start_basis], axis=1), 0, 0)
    both = scatter_sum(both, "fsdp", nf)
    both = lax.all_gather(both.astype(BF), "fsdp", axis=0, tiled=True)
    inverse = chol_inv(both[:, :rank].astype(F32) / M)
    margin = mm_split(both[:, rank:], inverse, 0, 1) / M
    new_basis = mm_split(image, inverse, 1, 1).astype(BF)
    raw = scatter_sum(mm(grad, image, 0, 0), "fsdp", nf)
    reduced = mm_split2(raw, inverse, 1, 1) * inv_sqrt

    rotated_one = mm(first_t, margin.astype(BF), 1, 0)
    rotated_two = mm(second_t, (margin * margin).astype(BF), 1, 0)
    moment_one = BETA_ONE * rotated_one + (1.0 - BETA_ONE) * reduced
    moment_two = BETA_TWO * rotated_two + (1.0 - BETA_TWO) * reduced * reduced
    direction = (moment_one / (jnp.sqrt(moment_two) + ADAM_EPS)).astype(BF)

    back = jnp.concatenate(
        [moment_one.astype(BF).reshape(share_cols, nf, share_rows), moment_two.astype(BF).reshape(share_cols, nf, share_rows)], axis=2
    ).transpose(1, 0, 2)
    sent = jnp.concatenate([jnp.broadcast_to(direction[None], (nf, share_cols, rank)), back], axis=2)
    got = lax.all_to_all(sent, "fsdp", 0, 0, tiled=True).reshape(cols, rank + 2 * share_rows)
    expanded = mm(new_basis, got[:, :rank], 1, 1)
    new_weight = (weight.astype(F32) - STEP_SIZE * inv_sqrt * expanded).astype(BF)
    moment_one = got[:, rank : rank + share_rows].astype(F32).T
    moment_two = got[:, rank + share_rows :].astype(F32).T
    return (first_basis, new_basis, moment_one, moment_two, new_weight)


def solution(mesh):
    specs = (P("fsdp", "tp"), P("fsdp", None), P("fsdp", "tp"), P("fsdp", "tp"), P("fsdp", "tp"))
    out_specs = (P("fsdp", None), P("fsdp", None), P("fsdp", "tp"), P("fsdp", "tp"), P("fsdp", "tp"))
    nf, nt = mesh.shape["fsdp"], mesh.shape["tp"]

    def body(*args):
        return per_device(nf, nt, *args)

    return jax.shard_map(body, mesh=mesh, in_specs=specs, out_specs=out_specs, check_vma=False)
```

time: 1170 us -> 545 us (0.47)
  waiting for transfers between devices: 781 us -> 94.8 us
  other arithmetic: 257 us -> 16.5 us
  blocking collectives: 0 us -> 177 us
  Pallas kernels: 0 us -> 143 us
  matrix products: 68.5 us -> 27.5 us
  starting transfers between devices: 0.88 us -> 32.7 us
    psum x5 -> x0, waiting for transfers between devices: 373 us -> none  [the longest x2 124 us: range_image(): return lax.psum(partial_image, 'tp')]
    another operation x34 -> x0, other arithmetic: 245 us -> none  [the longest x29 162 us: per_device(): factor = jnp.linalg.cholesky(gram_whole)]
    unnamed x15 -> x1, waiting for transfers between devices: 156 us -> 0.02 us
    all_gather x5 -> x1, waiting for transfers between devices: 176 us -> 20.3 us  [per_device(): both = lax.all_gather(both.astype(BF), 'fsdp', axis=0, tiled=True)]
    pallas_call x0 -> x2, Pallas kernels: none -> 143 us  [chol_inv(): pl.pallas_call(chol_kernel, out_shape=jax.ShapeDtypeStruct((n, n), jnp.fl...]
    all_to_all x0 -> x4, blocking collectives: none -> 107 us  [the longest x2 57.9 us: gather(): lax.all_to_all(jnp.broadcast_to(x[None], (n,) + x.shape), axis, 0, 0, til...]
    reduce_scatter x1 -> x0, waiting for transfers between devices: 77.3 us -> none  [per_device(): lax.psum_scatter(contract_rows(basis_cols, grad, False).astype(jnp.bfloat...]
    all_to_all x0 -> x7, waiting for transfers between devices: none -> 74.6 us  [the longest x5 45.3 us: scatter_sum(): lax.all_to_all(x.astype(BF).reshape(n, x.shape[0] // n, x.shape[1]), axis...]
  transfers between devices with their start and end apart: 13 -> 8, of which waited for: 12 -> 6; matrix products, arithmetic and copies ran while one was open for 15% -> 6% of each run, Pallas kernels for 0% -> 13%
where the time goes in v1:
time: 545 us; the launch traced here: 539 us
  blocking collectives  177 us (32%)
  Pallas kernels  143 us (26%)
  waiting for transfers between devices  94.8 us (17%)
  starting transfers between devices  32.7 us (6%)
  local copies, waits for them, and re-layouts  32.5 us (6%)
  matrix products  27.5 us (5%)
  other arithmetic  16.5 us (3%)
  between operations  14.9 us (3%)
    pallas_call x2, Pallas kernels, chol_inv(): pl.pallas_call(chol_kernel, out_shape=jax.ShapeDtypeStruct((n, n), jnp.fl...  143 us
    all_to_all x2, blocking collectives, gather(): lax.all_to_all(jnp.broadcast_to(x[None], (n,) + x.shape), axis, 0, 0, til...  57.9 us
    all_to_all x2, blocking collectives, scatter_sum(): lax.all_to_all(x.astype(BF).reshape(n, x.shape[0] // n, x.shape[1]), axis...  49.4 us
    all_to_all x5, waiting for transfers between devices, scatter_sum(): lax.all_to_all(x.astype(BF).reshape(n, x.shape[0] // n, x.shape[1]), axis...  45.3 us
    all_gather x1, blocking collectives, per_device(): lax.all_gather(gram.astype(BF), 'fsdp', axis=0, tiled=True).astype(F32) / M  43 us
    all_to_all x1, waiting for transfers between devices, per_device(): lax.all_to_all(sent, 'fsdp', 0, 0, tiled=True)  29.2 us
    dot_general x22, matrix products, mm(): lax.dot_general(a, b, (((ca,), (cb,)), ((), ())), preferred_element_type=...  27.5 us
    all_gather x2, blocking collectives, per_device(): image = lax.all_gather(image, 'tp', axis=0, tiled=True)  26.4 us
  transfers between devices with their start and end apart: 8, of which 6 were waited for; matrix products, arithmetic and copies ran while one was open for 6% of the time, Pallas kernels for 13%

profile of v1, /device:TPU:0, one launch (start us, length us, event | category | flops | bytes accessed | tf_op | source)
XLA Modules:
  0.0 539.0 jit_solution(18196370721823179778)
XLA Ops:
  8.7 2.3 convolution_convert_fusion.2
  11.0 33.9 %all_to_all.55 = bf16[16,120,512]{2,1,0:T(8,128)(2,1)S(1)} all-to-all(bf16[16,120,512]{2,1,0:T(8,128)(2,1)S(1)} %bitcast.65), channel_id=1, replica_groups=mesh['fsdp'=16,'tp'=8] {'fsdp'}, dimensions={0} | all-to-all | bytes 3932160 | tf_op jit(solution)/shard_map/all_to_all | solution.py:96
  45.3 29.4 %all_to_all.56 = bf16[16,120,512]{2,1,0:T(8,128)(2,1)S(1)} all-to-all(bf16[16,120,512]{2,1,0:T(8,128)(2,1)S(1)} %broadcast_in_dim.6), channel_id=1, replica_groups=mesh['fsdp'=16,'tp'=8] {'fsdp'}, dimensions={0} | all-to-all | bytes 3932160 | tf_op jit(solution)/shard_map/all_to_all | solution.py:101
  76.0 15.5 %all_to_all.57 = bf16[8,64,512]{2,1,0:T(8,128)(2,1)S(1)} all-to-all(bf16[8,64,512]{2,1,0:T(8,128)(2,1)S(1)} %bitcast.68), channel_id=1, replica_groups=mesh['fsdp'=16,'tp'=8] {'tp'}, dimensions={0} | all-to-all | bytes 1048576 | tf_op jit(solution)/shard_map/all_to_all | solution.py:96
  91.6 13.1 %all_gather.12 = bf16[512,512]{1,0:T(8,128)(2,1)S(1)} all-gather(bf16[64,512]{1,0:T(8,128)(2,1)S(1)} %reduce_sum.76), channel_id=1, replica_groups=mesh['fsdp'=16,'tp'=8] {'tp'}, dimensions={0}, use_global_device_ids=true | all-gather | bytes 589824 | tf_op jit(solution)/shard_map/all_gather | solution.py:120
  106.0 3.6 all-to-all-start.3
  109.6 2.6 fusion
  112.1 4.0 copy.25
  116.1 5.7 %all-to-all-done.3 = bf16[16,32,512]{2,1,0:T(8,128)(2,1)S(1)} async-done(((bf16[16,32,512]{2,1,0:T(8,128)(2,1)}), bf16[16,32,512]{2,1,0:T(8,128)(2,1)S(1)}, u32[]{:S(2)}, u32[]{:S(2)}) %all-to-all-start.3) | async-done | bytes 524320 | tf_op jit(solution)/shard_map/all_to_all | solution.py:96
  121.9 4.4 all-to-all-start.4
  126.4 43.0 %all_gather.13 = bf16[512,512]{1,0:T(8,128)(2,1)S(1)} all-gather(bf16[32,512]{1,0:T(8,128)(2,1)S(1)} %reduce_sum.77), channel_id=1, replica_groups=mesh['fsdp'=16,'tp'=8] {'fsdp'}, dimensions={0}, use_global_device_ids=true | all-gather | bytes 557056 | tf_op jit(solution)/shard_map/all_gather | solution.py:122
  169.6 71.6 %shard_map.92 = f32[512,512]{1,0:T(8,128)S(1)} custom-call(f32[512,512]{1,0:T(8,128)S(1)} %convert_multiply_fusion.1.a_ref), custom_call_target="tpu_custom_call" | custom-call | tf_op jit(solution)/shard_map/pallas_call | solution.py:69
  244.2 28.5 %all_to_all.58 = bf16[16,120,512]{2,1,0:T(8,128)(2,1)S(1)} all-to-all(bf16[16,120,512]{2,1,0:T(8,128)(2,1)S(1)} %broadcast_in_dim.7), channel_id=1, replica_groups=mesh['fsdp'=16,'tp'=8] {'fsdp'}, dimensions={0} | all-to-all | bytes 3932160 | tf_op jit(solution)/shard_map/all_to_all | solution.py:101
  274.7 3.5 all-to-all-start.6
  284.8 3.7 all-to-all-done.6
  288.5 4.2 all-to-all-start.8
  293.4 13.3 %all_gather.14 = bf16[512,512]{1,0:T(8,128)(2,1)S(1)} all-gather(bf16[64,512]{1,0:T(8,128)(2,1)} %reduce_sum.79), channel_id=1, replica_groups=mesh['fsdp'=16,'tp'=8] {'tp'}, dimensions={0}, use_global_device_ids=true | all-gather | bytes 589824 | tf_op jit(solution)/shard_map/all_gather | solution.py:130
  306.7 3.0 convolution_convert_fusion.3
  309.7 7.1 %all-to-all-start.7 = ((bf16[16,32,1024]{2,1,0:T(8,128)(2,1)}), bf16[16,32,1024]{2,1,0:T(8,128)(2,1)}, u32[]{:S(2)}, u32[]{:S(2)}) async-start(bf16[16,32,1024]{2,1,0:T(8,128)(2,1)} %bitcast.66), calls=%async_computation.7 | async-start | bytes 2097152 | tf_op jit(solution)/shard_map/all_to_all | solution.py:96
  316.8 2.6 fusion.1
  319.4 4.0 copy.27
  323.3 11.7 %all-to-all-done.7 = bf16[16,32,1024]{2,1,0:T(8,128)(2,1)} async-done(((bf16[16,32,1024]{2,1,0:T(8,128)(2,1)}), bf16[16,32,1024]{2,1,0:T(8,128)(2,1)}, u32[]{:S(2)}, u32[]{:S(2)}) %all-to-all-start.7) | async-done | bytes 1048608 | tf_op jit(solution)/shard_map/all_to_all | solution.py:96
  335.0 4.4 all-to-all-start.9
  343.5 24.2 %all-to-all-done.9 = bf16[16,120,512]{2,1,0:T(8,128)(2,1)} async-done(((bf16[16,120,512]{2,1,0:T(8,128)(2,1)}), bf16[16,120,512]{2,1,0:T(8,128)(2,1)}, u32[]{:S(2)}, u32[]{:S(2)}) %all-to-all-start.9) | async-done | bytes 1966112 | tf_op jit(solution)/shard_map/all_to_all | solution.py:96
  367.7 2.6 convert_reduce_fusion
  370.3 20.3 %all-gather.2.cloned.1.call-done = bf16[512,1024]{1,0:T(8,128)(2,1)} async-done(((bf16[32,1024]{1,0:T(8,128)(2,1)}), bf16[512,1024]{1,0:T(8,128)(2,1)}) %all-gather.2.cloned.1.call-update) | async-done | bytes 1048592 | tf_op jit(solution)/shard_map/all_gather | solution.py:133
  391.7 71.7 %shard_map.93 = f32[512,512]{1,0:T(8,128)S(1)} custom-call(f32[512,512]{1,0:T(8,128)S(1)} %convert_multiply_fusion.a_ref), custom_call_target="tpu_custom_call" | custom-call | tf_op jit(solution)/shard_map/pallas_call | solution.py:69
  477.0 5.1 all-to-all-start.10
  486.0 29.2 %all-to-all-done.10 = bf16[16,120,576]{1,2,0:T(8,128)(2,1)} async-done(((bf16[16,120,576]{1,2,0:T(8,128)(2,1)}), bf16[16,120,576]{1,2,0:T(8,128)(2,1)}, u32[]{:S(2)}, u32[]{:S(2)}) %all-to-all-start.10) | async-done | bytes 2211872 | tf_op jit(solution)/shard_map/all_to_all | solution.py:150
  515.3 4.6 copy.31
  519.9 5.4 reshape.75
  527.0 4.7 subtract_convert_fusion
  (70 shorter events, 41.3 us)
Async XLA Ops:
  7.2 1.6 copy-start
  104.7 7.4 %copy-start.3 = (bf16[512,512]{1,0:T(8,128)(2,1)}, bf16[512,512]{1,0:T(8,128)(2,1)S(1)}, u32[]{:S(2)}) copy-start(bf16[512,512]{1,0:T(8,128)(2,1)S(1)} %all_gather.12) | copy-start | bytes 1572868
  106.0 15.9 %all-to-all-start.3 = ((bf16[16,32,512]{2,1,0:T(8,128)(2,1)}), bf16[16,32,512]{2,1,0:T(8,128)(2,1)S(1)}, u32[]{:S(2)}, u32[]{:S(2)}) async-start(bf16[16,32,512]{2,1,0:T(8,128)(2,1)} %bitcast.4), calls=%async_computation.3 | async-start | bytes 1048576 | tf_op jit(solution)/shard_map/all_to_all | solution.py:96
  121.9 119.3 %all-to-all-start.4 = ((bf16[16,120,512]{2,1,0:T(8,128)(2,1)}), bf16[16,120,512]{2,1,0:T(8,128)(2,1)}, u32[]{:S(2)}, u32[]{:S(2)}) async-start(bf16[16,120,512]{2,1,0:T(8,128)(2,1)} %bitcast.62), calls=%async_computation.4 | async-start | bytes 3932160 | tf_op jit(solution)/shard_map/all_to_all | solution.py:96
  274.7 13.8 %all-to-all-start.6 = ((bf16[8,64,512]{2,1,0:T(8,128)(2,1)}), bf16[8,64,512]{2,1,0:T(8,128)(2,1)S(1)}, u32[]{:S(2)}, u32[]{:S(2)}) async-start(bf16[8,64,512]{2,1,0:T(8,128)(2,1)} %bitcast.67), calls=%async_computation.6 | async-start | bytes 1048576 | tf_op jit(solution)/shard_map/all_to_all | solution.py:96
  288.5 21.2 %all-to-all-start.8 = ((bf16[16,120,64]{1,2,0:T(8,128)(2,1)}), bf16[16,120,64]{1,2,0:T(8,128)(2,1)}, u32[]{:S(2)}, u32[]{:S(2)}) async-start(bf16[16,120,64]{1,2,0:T(8,128)(2,1)} %copy.26), calls=%async_computation.8 | async-start | bytes 524288 | tf_op jit(solution)/shard_map/all_to_all | solution.py:113
  306.7 10.1 %copy-start.5 = (bf16[512,512]{1,0:T(8,128)(2,1)}, bf16[512,512]{1,0:T(8,128)(2,1)S(1)}, u32[]{:S(2)}) copy-start(bf16[512,512]{1,0:T(8,128)(2,1)S(1)} %all_gather.14) | copy-start | bytes 1572868
  309.7 25.4 %all-to-all-start.7 = ((bf16[16,32,1024]{2,1,0:T(8,128)(2,1)}), bf16[16,32,1024]{2,1,0:T(8,128)(2,1)}, u32[]{:S(2)}, u32[]{:S(2)}) async-start(bf16[16,32,1024]{2,1,0:T(8,128)(2,1)} %bitcast.66), calls=%async_computation.7 | async-start | bytes 2097152 | tf_op jit(solution)/shard_map/all_to_all | solution.py:96
  335.0 32.7 %all-to-all-start.9 = ((bf16[16,120,512]{2,1,0:T(8,128)(2,1)}), bf16[16,120,512]{2,1,0:T(8,128)(2,1)}, u32[]{:S(2)}, u32[]{:S(2)}) async-start(bf16[16,120,512]{2,1,0:T(8,128)(2,1)} %bitcast.61), calls=%async_computation.9 | async-start | bytes 3932160 | tf_op jit(solution)/shard_map/all_to_all | solution.py:96
  339.5 51.1 %all-gather.2.cloned.1.call-start = ((), (), s32[]{:S(2)}) async-start(), calls=%async_computation.11 | async-start | bytes 1114112 | tf_op jit(solution)/shard_map/all_gather | solution.py:133
  391.7 71.9 %copy-start.7 = (f32[120,512]{1,0:T(8,128)S(1)}, f32[120,512]{1,0:T(8,128)}, u32[]{:S(2)}) copy-start(f32[120,512]{1,0:T(8,128)} %convert_reduce_fusion) | copy-start | bytes 737284
  463.6 1.9 copy-start.1
  463.6 1.4 copy-start.8
  465.5 0.9 copy-start.11
  465.5 1.2 copy-start.10
  477.0 38.3 %all-to-all-start.10 = ((bf16[16,120,576]{1,2,0:T(8,128)(2,1)}), bf16[16,120,576]{1,2,0:T(8,128)(2,1)}, u32[]{:S(2)}, u32[]{:S(2)}) async-start(bf16[16,120,576]{1,2,0:T(8,128)(2,1)} %pad_maximum_fusion), calls=%async_computation.10 | async-start | bytes 4718592 | tf_op jit(solution)/shard_map/all_to_all | solution.py:150
  482.2 1.6 copy-start.4
  483.8 1.3 copy-start.6
  483.8 1.8 copy-start.2
  486.0 41.0 %copy-start.9 = (bf16[512,512]{1,0:T(8,128)(2,1)}, bf16[512,512]{1,0:T(8,128)(2,1)S(1)}, u32[]{:S(2)}) copy-start(bf16[512,512]{1,0:T(8,128)(2,1)S(1)} %fusion.5) | copy-start | bytes 1572868
Sparse Core Ops, SparseCore 0:
  343.0 47.4 all-gather.1

commit v2 on v1

--- a/solution.py
+++ b/solution.py
@@ -72,6 +72,7 @@
         in_specs=[pl.BlockSpec(memory_space=pltpu.VMEM)],
         out_specs=pl.BlockSpec(memory_space=pltpu.VMEM),
         scratch_shapes=[pltpu.VMEM((NB, NB), jnp.float32), pltpu.VMEM((n, n), jnp.float32), pltpu.VMEM((n, n), jnp.float32)],
+        cost_estimate=pl.CostEstimate(flops=60 * 10**9, bytes_accessed=2 * 2**20, transcendentals=0),
         compiler_params=pltpu.CompilerParams(vmem_limit_bytes=32 * 2**20),
     )(a)
 
@@ -119,22 +120,27 @@
     image = scatter_sum(mm(grad, panel, 1, 0), "tp", nt).astype(BF)
     image = lax.all_gather(image, "tp", axis=0, tiled=True)
     gram = scatter_sum(mm(image, image, 0, 0), "fsdp", nf)
-    gram = lax.all_gather(gram.astype(BF), "fsdp", axis=0, tiled=True).astype(F32) / M
-    inverse = chol_inv(gram)
+    gram = lax.all_gather(gram.astype(BF), "fsdp", axis=0, tiled=True)
+    raw, gram = lax.optimization_barrier((mm(grad, image, 0, 0).astype(BF), gram))
+    inverse = chol_inv(gram.astype(F32) / M)
     first_basis = mm_split(image, inverse, 1, 1).astype(BF)
-    raw = scatter_sum(mm(grad, image, 0, 0), "fsdp", nf)
+    raw = scatter_sum(raw, "fsdp", nf)
     panel = (mm_split2(raw, inverse, 1, 1) * inv_sqrt).astype(BF)
 
     panel = gather(panel, "fsdp", nf)
     image = scatter_sum(mm(grad, panel, 1, 0), "tp", nt).astype(BF)
     image = lax.all_gather(image, "tp", axis=0, tiled=True)
-    both = mm(image, jnp.concatenate([image, start_basis], axis=1), 0, 0)
-    both = scatter_sum(both, "fsdp", nf)
-    both = lax.all_gather(both.astype(BF), "fsdp", axis=0, tiled=True)
-    inverse = chol_inv(both[:, :rank].astype(F32) / M)
-    margin = mm_split(both[:, rank:], inverse, 0, 1) / M
+    gram = scatter_sum(mm(image, image, 0, 0), "fsdp", nf)
+    gram = lax.all_gather(gram.astype(BF), "fsdp", axis=0, tiled=True)
+    raw, cross, gram = lax.optimization_barrier(
+        (mm(grad, image, 0, 0).astype(BF), mm(image, start_basis, 0, 0).astype(BF), gram)
+    )
+    inverse = chol_inv(gram.astype(F32) / M)
+    cross = scatter_sum(cross, "fsdp", nf)
+    cross = gather(cross.astype(BF), "fsdp", nf)
+    margin = mm_split(cross, inverse, 0, 1) / M
     new_basis = mm_split(image, inverse, 1, 1).astype(BF)
-    raw = scatter_sum(mm(grad, image, 0, 0), "fsdp", nf)
+    raw = scatter_sum(raw, "fsdp", nf)
     reduced = mm_split2(raw, inverse, 1, 1) * inv_sqrt
 
     rotated_one = mm(first_t, margin.astype(BF), 1, 0)
@@ -146,12 +152,12 @@
     back = jnp.concatenate(
         [moment_one.astype(BF).reshape(share_cols, nf, share_rows), moment_two.astype(BF).reshape(share_cols, nf, share_rows)], axis=2
     ).transpose(1, 0, 2)
-    sent = jnp.concatenate([jnp.broadcast_to(direction[None], (nf, share_cols, rank)), back], axis=2)
-    got = lax.all_to_all(sent, "fsdp", 0, 0, tiled=True).reshape(cols, rank + 2 * share_rows)
-    expanded = mm(new_basis, got[:, :rank], 1, 1)
+    direction = gather(direction, "fsdp", nf)
+    back = lax.all_to_all(back, "fsdp", 0, 0, tiled=True).reshape(cols, 2 * share_rows)
+    expanded = mm(new_basis, direction, 1, 1)
     new_weight = (weight.astype(F32) - STEP_SIZE * inv_sqrt * expanded).astype(BF)
-    moment_one = got[:, rank : rank + share_rows].astype(F32).T
-    moment_two = got[:, rank + share_rows :].astype(F32).T
+    moments = back.astype(F32).T
+    moment_one, moment_two = moments[:share_rows], moments[share_rows:]
     return (first_basis, new_basis, moment_one, moment_two, new_weight)
 
 

time: 545 us -> 511 us (0.938)
  waiting for transfers between devices: 94.8 us -> 46.6 us
  blocking collectives: 177 us -> 208 us
  between operations: 14.9 us -> 1.49 us
    all_to_all x5, waiting for transfers between devices: 45.3 us -> 20.8 us  [scatter_sum(): lax.all_to_all(x.astype(BF).reshape(n, x.shape[0] // n, x.shape[1]), axis...]
    all_gather x1 -> x0, waiting for transfers between devices: 20.3 us -> none  [per_device(): both = lax.all_gather(both.astype(BF), 'fsdp', axis=0, tiled=True)]
    all_to_all x0 -> x1, blocking collectives: none -> 15.8 us  [per_device(): lax.all_to_all(back, 'fsdp', 0, 0, tiled=True).reshape(cols, 2 * share_rows)]
    all_to_all x2 -> x3, blocking collectives: 49.4 us -> 62.3 us  [scatter_sum(): lax.all_to_all(x.astype(BF).reshape(n, x.shape[0] // n, x.shape[1]), axis...]
    all_to_all x1 -> x2, waiting for transfers between devices: 29.2 us -> 17.9 us  [gather(): lax.all_to_all(jnp.broadcast_to(x[None], (n,) + x.shape), axis, 0, 0, til...]
    convert_element_type x3 -> x0, local copies, waits for them, and re-layouts: 9.62 us -> none  [the longest x2 7.96 us: scatter_sum(): x.astype(BF).reshape(n, x.shape[0] // n, x.shape[1])]
    all_to_all x1, waiting for transfers between devices: 0.01 us -> 8 us  [per_device(): lax.all_to_all(moments, 'fsdp', 0, 0, tiled=True).transpose(1, 0, 2)]
    optimization_barrier x0 -> x2, local copies, waits for them, and re-layouts: none -> 7.97 us  [the longest x1 3.99 us: per_device(): lax.optimization_barrier((mm(grad, image, 0, 0).astype(BF), gram))]
  transfers between devices with their start and end apart: 8 -> 8, of which waited for: 6 -> 6; matrix products, arithmetic and copies ran while one was open for 6% -> 6% of each run, Pallas kernels for 13% -> 28%
where the time goes in v2:
time: 511 us; the launch traced here: 504 us
  blocking collectives  208 us (41%)
  Pallas kernels  143 us (28%)
  waiting for transfers between devices  46.6 us (9%)
  starting transfers between devices  34.9 us (7%)
  local copies, waits for them, and re-layouts  28.3 us (6%)
  matrix products  28.3 us (6%)
  other arithmetic  13.8 us (3%)
    pallas_call x2, Pallas kernels, chol_inv(): pl.pallas_call(chol_kernel, out_shape=jax.ShapeDtypeStruct((n, n), jnp.fl...  143 us
    all_to_all x3, blocking collectives, scatter_sum(): lax.all_to_all(x.astype(BF).reshape(n, x.shape[0] // n, x.shape[1]), axis...  62.3 us
    all_to_all x2, blocking collectives, gather(): lax.all_to_all(jnp.broadcast_to(x[None], (n,) + x.shape), axis, 0, 0, til...  57.6 us
    all_gather x2, blocking collectives, per_device(): gram = lax.all_gather(gram.astype(BF), 'fsdp', axis=0, tiled=True)  45.5 us
    dot_general x23, matrix products, mm(): lax.dot_general(a, b, (((ca,), (cb,)), ((), ())), preferred_element_type=...  28.3 us
    all_gather x2, blocking collectives, per_device(): image = lax.all_gather(image, 'tp', axis=0, tiled=True)  26.4 us
    all_to_all x5, starting transfers between devices, scatter_sum(): lax.all_to_all(x.astype(BF).reshape(n, x.shape[0] // n, x.shape[1]), axis...  22.7 us
    all_to_all x5, waiting for transfers between devices, scatter_sum(): lax.all_to_all(x.astype(BF).reshape(n, x.shape[0] // n, x.shape[1]), axis...  20.8 us
  transfers between devices with their start and end apart: 8, of which 6 were waited for; matrix products, arithmetic and copies ran while one was open for 6% of the time, Pallas kernels for 28%

profile of v2, /device:TPU:0, one launch (start us, length us, event | category | flops | bytes accessed | tf_op | source)
XLA Modules:
  0.0 504.4 jit_solution(15453552386705823614)
XLA Ops:
  4.4 33.9 %all_to_all.70 = bf16[16,120,512]{2,1,0:T(8,128)(2,1)S(1)} all-to-all(bf16[16,120,512]{2,1,0:T(8,128)(2,1)S(1)} %bitcast.73), channel_id=1, replica_groups=mesh['fsdp'=16,'tp'=8] {'fsdp'}, dimensions={0} | all-to-all | bytes 3932160 | tf_op jit(solution)/shard_map/all_to_all | solution.py:97
  38.8 29.4 %all_to_all.71 = bf16[16,120,512]{2,1,0:T(8,128)(2,1)S(1)} all-to-all(bf16[16,120,512]{2,1,0:T(8,128)(2,1)S(1)} %broadcast_in_dim.8), channel_id=1, replica_groups=mesh['fsdp'=16,'tp'=8] {'fsdp'}, dimensions={0} | all-to-all | bytes 3932160 | tf_op jit(solution)/shard_map/all_to_all | solution.py:102
  69.5 15.5 %all_to_all.72 = bf16[8,64,512]{2,1,0:T(8,128)(2,1)S(1)} all-to-all(bf16[8,64,512]{2,1,0:T(8,128)(2,1)S(1)} %bitcast.77), channel_id=1, replica_groups=mesh['fsdp'=16,'tp'=8] {'tp'}, dimensions={0} | all-to-all | bytes 1048576 | tf_op jit(solution)/shard_map/all_to_all | solution.py:97
  85.1 13.1 %all_gather.12 = bf16[512,512]{1,0:T(8,128)(2,1)S(1)} all-gather(bf16[64,512]{1,0:T(8,128)(2,1)S(1)} %reduce_sum.88), channel_id=1, replica_groups=mesh['fsdp'=16,'tp'=8] {'tp'}, dimensions={0}, use_global_device_ids=true | all-gather | bytes 589824 | tf_op jit(solution)/shard_map/all_gather | solution.py:121
  99.5 3.6 all-to-all-start.3
  103.1 2.6 fusion
  105.6 9.7 %all-to-all-done.3 = bf16[16,32,512]{2,1,0:T(8,128)(2,1)S(1)} async-done(((bf16[16,32,512]{2,1,0:T(8,128)(2,1)}), bf16[16,32,512]{2,1,0:T(8,128)(2,1)S(1)}, u32[]{:S(2)}, u32[]{:S(2)}) %all-to-all-start.3) | async-done | bytes 524320 | tf_op jit(solution)/shard_map/all_to_all | solution.py:97
  115.4 21.8 %all_gather.13 = bf16[512,512]{1,0:T(8,128)(2,1)S(1)} all-gather(bf16[32,512]{1,0:T(8,128)(2,1)S(1)} %reduce_sum.89), channel_id=1, replica_groups=mesh['fsdp'=16,'tp'=8] {'fsdp'}, dimensions={0}, use_global_device_ids=true | all-gather | bytes 557056 | tf_op jit(solution)/shard_map/all_gather | solution.py:123
  138.3 4.0 copy.16
  142.3 5.1 %all-to-all-start.4 = ((bf16[16,120,512]{2,1,0:T(8,128)(2,1)}), bf16[16,120,512]{2,1,0:T(8,128)(2,1)}, u32[]{:S(2)}, u32[]{:S(2)}) async-start(bf16[16,120,512]{2,1,0:T(8,128)(2,1)} %bitcast.68), calls=%async_computation.4 | async-start | bytes 3932160 | tf_op jit(solution)/shard_map/all_to_all | solution.py:97
  148.7 71.7 %shard_map.92 = f32[512,512]{1,0:T(8,128)S(1)} custom-call(f32[512,512]{1,0:T(8,128)S(1)} %copy-done.2), custom_call_target="tpu_custom_call" | custom-call | flops 60000002048 | bytes 2097152 | tf_op jit(solution)/shard_map/pallas_call | solution.py:69
  223.3 28.2 %all_to_all.73 = bf16[16,120,512]{2,1,0:T(8,128)(2,1)S(1)} all-to-all(bf16[16,120,512]{2,1,0:T(8,128)(2,1)S(1)} %broadcast_in_dim.9), channel_id=1, replica_groups=mesh['fsdp'=16,'tp'=8] {'fsdp'}, dimensions={0} | all-to-all | bytes 3932160 | tf_op jit(solution)/shard_map/all_to_all | solution.py:102
  252.8 12.9 %all_to_all.74 = bf16[8,64,512]{2,1,0:T(8,128)(2,1)S(1)} all-to-all(bf16[8,64,512]{2,1,0:T(8,128)(2,1)S(1)} %bitcast.78), channel_id=1, replica_groups=mesh['fsdp'=16,'tp'=8] {'tp'}, dimensions={0} | all-to-all | bytes 1048576 | tf_op jit(solution)/shard_map/all_to_all | solution.py:97
  266.4 13.3 %all_gather.14 = bf16[512,512]{1,0:T(8,128)(2,1)S(1)} all-gather(bf16[64,512]{1,0:T(8,128)(2,1)} %reduce_sum.91), channel_id=1, replica_groups=mesh['fsdp'=16,'tp'=8] {'tp'}, dimensions={0}, use_global_device_ids=true | all-gather | bytes 589824 | tf_op jit(solution)/shard_map/all_gather | solution.py:132
  281.0 4.2 all-to-all-start.7
  285.2 2.3 convolution_convert_fusion.6
  287.5 2.5 fusion.1
  290.1 7.5 %all-to-all-done.7 = bf16[16,32,512]{2,1,0:T(8,128)(2,1)} async-done(((bf16[16,32,512]{2,1,0:T(8,128)(2,1)}), bf16[16,32,512]{2,1,0:T(8,128)(2,1)}, u32[]{:S(2)}, u32[]{:S(2)}) %all-to-all-start.7) | async-done | bytes 524320 | tf_op jit(solution)/shard_map/all_to_all | solution.py:97
  298.7 23.7 %all_gather.15 = bf16[512,512]{1,0:T(8,128)(2,1)} all-gather(bf16[32,512]{1,0:T(8,128)(2,1)S(1)} %reduce_sum.92), channel_id=1, replica_groups=mesh['fsdp'=16,'tp'=8] {'fsdp'}, dimensions={0}, use_global_device_ids=true | all-gather | bytes 557056 | tf_op jit(solution)/shard_map/all_gather | solution.py:134
  322.4 4.6 all-to-all-start.9
  333.6 3.6 all-to-all-done.9
  337.1 4.2 all-to-all-start.8
  342.0 8.0 %all-to-all-done.8 = bf16[16,120,64]{1,2,0:T(8,128)(2,1)} async-done(((bf16[16,120,64]{1,2,0:T(8,128)(2,1)}), bf16[16,120,64]{1,2,0:T(8,128)(2,1)}, u32[]{:S(2)}, u32[]{:S(2)}) %all-to-all-start.8) | async-done | bytes 245792 | tf_op jit(solution)/shard_map/all_to_all | solution.py:114
  351.6 3.6 all-to-all-start.10
  356.9 4.0 copy.18
  366.1 5.1 %all-to-all-start.11 = ((bf16[16,120,512]{2,1,0:T(8,128)(2,1)}), bf16[16,120,512]{2,1,0:T(8,128)(2,1)}, u32[]{:S(2)}, u32[]{:S(2)}) async-start(bf16[16,120,512]{2,1,0:T(8,128)(2,1)} %bitcast.67), calls=%async_computation.11 | async-start | bytes 3932160 | tf_op jit(solution)/shard_map/all_to_all | solution.py:97
  372.5 71.7 %shard_map.93 = f32[512,512]{1,0:T(8,128)S(1)} custom-call(f32[512,512]{1,0:T(8,128)S(1)} %copy-done.1), custom_call_target="tpu_custom_call" | custom-call | flops 60000002048 | bytes 2097152 | tf_op jit(solution)/shard_map/pallas_call | solution.py:69
  456.0 15.8 %all_to_all.75 = bf16[16,120,64]{1,2,0:T(8,128)(2,1)} all-to-all(bf16[16,120,64]{1,2,0:T(8,128)(2,1)S(1)} %maximum_bitcast_fusion), channel_id=1, replica_groups=mesh['fsdp'=16,'tp'=8] {'fsdp'}, dimensions={0} | all-to-all | bytes 491520 | tf_op jit(solution)/shard_map/all_to_all | solution.py:156
  471.8 2.3 broadcast_in_dim.11
  474.1 4.4 all-to-all-start.13
  483.6 15.6 %all-to-all-done.13 = bf16[16,120,512]{2,1,0:T(8,128)(2,1)} async-done(((bf16[16,120,512]{2,1,0:T(8,128)(2,1)}), bf16[16,120,512]{2,1,0:T(8,128)(2,1)}, u32[]{:S(2)}, u32[]{:S(2)}) %all-to-all-start.13) | async-done | bytes 1966112 | tf_op jit(solution)/shard_map/all_to_all | solution.py:102
  499.2 4.7 subtract_convert_fusion
  (83 shorter events, 50.3 us)
Async XLA Ops:
  0.6 1.6 copy-start
  98.2 7.4 %copy-start.7 = (bf16[512,512]{1,0:T(8,128)(2,1)}, bf16[512,512]{1,0:T(8,128)(2,1)S(1)}, u32[]{:S(2)}) copy-start(bf16[512,512]{1,0:T(8,128)(2,1)S(1)} %all_gather.12) | copy-start | bytes 1572868
  99.5 15.9 %all-to-all-start.3 = ((bf16[16,32,512]{2,1,0:T(8,128)(2,1)}), bf16[16,32,512]{2,1,0:T(8,128)(2,1)S(1)}, u32[]{:S(2)}, u32[]{:S(2)}) async-start(bf16[16,32,512]{2,1,0:T(8,128)(2,1)} %bitcast.5), calls=%async_computation.3 | async-start | bytes 1048576 | tf_op jit(solution)/shard_map/all_to_all | solution.py:97
  142.3 78.0 %all-to-all-start.4 = ((bf16[16,120,512]{2,1,0:T(8,128)(2,1)}), bf16[16,120,512]{2,1,0:T(8,128)(2,1)}, u32[]{:S(2)}, u32[]{:S(2)}) async-start(bf16[16,120,512]{2,1,0:T(8,128)(2,1)} %bitcast.68), calls=%async_computation.4 | async-start | bytes 3932160 | tf_op jit(solution)/shard_map/all_to_all | solution.py:97
  147.5 1.2 copy-start.2
  279.7 7.8 %copy-start.9 = (bf16[512,512]{1,0:T(8,128)(2,1)}, bf16[512,512]{1,0:T(8,128)(2,1)S(1)}, u32[]{:S(2)}) copy-start(bf16[512,512]{1,0:T(8,128)(2,1)S(1)} %all_gather.14) | copy-start | bytes 1572868
  281.0 16.6 %all-to-all-start.7 = ((bf16[16,32,512]{2,1,0:T(8,128)(2,1)}), bf16[16,32,512]{2,1,0:T(8,128)(2,1)}, u32[]{:S(2)}, u32[]{:S(2)}) async-start(bf16[16,32,512]{2,1,0:T(8,128)(2,1)} %bitcast.76), calls=%async_computation.7 | async-start | bytes 1048576 | tf_op jit(solution)/shard_map/all_to_all | solution.py:97
  322.4 14.8 %all-to-all-start.9 = ((bf16[16,32,512]{2,1,0:T(8,128)(2,1)}), bf16[16,32,512]{2,1,0:T(8,128)(2,1)S(1)}, u32[]{:S(2)}, u32[]{:S(2)}) async-start(bf16[16,32,512]{2,1,0:T(8,128)(2,1)} %bitcast.75), calls=%async_computation.9 | async-start | bytes 1048576 | tf_op jit(solution)/shard_map/all_to_all | solution.py:97
  337.1 12.9 %all-to-all-start.8 = ((bf16[16,120,64]{1,2,0:T(8,128)(2,1)}), bf16[16,120,64]{1,2,0:T(8,128)(2,1)}, u32[]{:S(2)}, u32[]{:S(2)}) async-start(bf16[16,120,64]{1,2,0:T(8,128)(2,1)} %copy.17), calls=%async_computation.8 | async-start | bytes 524288 | tf_op jit(solution)/shard_map/all_to_all | solution.py:114
  351.6 13.7 %all-to-all-start.10 = ((bf16[16,32,512]{2,1,0:T(8,128)(2,1)}), bf16[16,32,512]{2,1,0:T(8,128)(2,1)S(1)}, u32[]{:S(2)}, u32[]{:S(2)}) async-start(bf16[16,32,512]{2,1,0:T(8,128)(2,1)} %broadcast_in_dim.10), calls=%async_computation.10 | async-start | bytes 1048576 | tf_op jit(solution)/shard_map/all_to_all | solution.py:102
  365.3 0.8 copy-start.11
  366.1 81.1 %all-to-all-start.11 = ((bf16[16,120,512]{2,1,0:T(8,128)(2,1)}), bf16[16,120,512]{2,1,0:T(8,128)(2,1)}, u32[]{:S(2)}, u32[]{:S(2)}) async-start(bf16[16,120,512]{2,1,0:T(8,128)(2,1)} %bitcast.67), calls=%async_computation.11 | async-start | bytes 3932160 | tf_op jit(solution)/shard_map/all_to_all | solution.py:97
  371.3 1.2 copy-start.1
  444.2 1.0 copy-start.12
  444.4 1.4 copy-start.4
  447.2 2.3 copy-start.5
  449.1 1.2 copy-start.3
  449.2 1.2 copy-start.16
  449.5 1.1 copy-start.15
  474.1 25.2 %all-to-all-start.13 = ((bf16[16,120,512]{2,1,0:T(8,128)(2,1)}), bf16[16,120,512]{2,1,0:T(8,128)(2,1)}, u32[]{:S(2)}, u32[]{:S(2)}) async-start(bf16[16,120,512]{2,1,0:T(8,128)(2,1)} %broadcast_in_dim.11), calls=%async_computation.13 | async-start | bytes 3932160 | tf_op jit(solution)/shard_map/all_to_all | solution.py:102
  478.5 1.6 copy-start.8
  480.1 1.3 copy-start.10
  480.1 1.8 copy-start.6
  481.4 1.0 copy-start.13
  482.4 21.6 %copy-start.14 = (bf16[512,512]{1,0:T(8,128)(2,1)}, bf16[512,512]{1,0:T(8,128)(2,1)S(1)}, u32[]{:S(2)}) copy-start(bf16[512,512]{1,0:T(8,128)(2,1)S(1)} %fusion.4) | copy-start | bytes 1572868

commit v3 on v2

--- a/solution.py
+++ b/solution.py
@@ -39,40 +39,130 @@
         out.append(acc)
     return out
 
-def dot(a, b, dims):
-    return lax.dot_general(a, b, (dims, ((), ())), precision=lax.Precision.HIGHEST, preferred_element_type=jnp.float32)
 
 NB = 128
-def chol_kernel(a_ref, x_ref, w_ref, s_ref, b_ref):
+
+
+def exact_dot(a, b, dims):
+    return lax.dot_general(a, b, (dims, ((), ())), precision=lax.Precision.HIGHEST, preferred_element_type=F32)
+
+
+def fast_dot(a, b, dims):
+    return lax.dot_general(a, b, (dims, ((), ())), preferred_element_type=F32)
+
+
+def halves(x):
+    hi = x.astype(BF)
+    return hi, (x - hi.astype(F32)).astype(BF)
+
+
+def eliminate(a_ref, x_ref, w_ref, s_ref, b_ref):
     n = a_ref.shape[0]
+    nb = n // NB
     s_ref[...] = a_ref[...]
     b_ref[...] = jnp.zeros_like(b_ref)
-    nb = n // NB
-    for k in range(nb):
-        lo = k * NB
-        for g, v in enumerate(elim(lambda g: s_ref[pl.ds(lo + 8 * g, 8), pl.ds(lo, NB)])):
+    x_ref[...] = jnp.zeros_like(x_ref)
+
+    @pl.loop(0, nb)
+    def _(k):
+        rows = pl.ds(pl.multiple_of(k * NB, NB), NB)
+        for g, v in enumerate(elim(lambda g: s_ref[pl.ds(pl.multiple_of(k * NB + 8 * g, 8), 8), rows])):
             w_ref[pl.ds(8 * g, 8), :] = v
         w = w_ref[...]
-        if k:
-            xk = dot(w, b_ref[lo:lo + NB, :lo], ((1,), (0,)))
-            x_ref[lo:lo + NB, :lo] = xk
-        x_ref[lo:lo + NB, lo:lo + NB] = w
-        if lo + NB < n:
-            x_ref[lo:lo + NB, lo + NB:] = jnp.zeros((NB, n - lo - NB), jnp.float32)
-            hi = lo + NB
-            u = dot(w, s_ref[lo:hi, hi:], ((1,), (0,)))
-            s_ref[hi:, hi:] -= dot(u, u, ((0,), (0,)))
-            b_ref[hi:, :hi] -= dot(u, x_ref[lo:hi, :hi], ((0,), (0,)))
+        u = exact_dot(w, s_ref[rows, :], ((1,), (0,)))
+        x_ref[rows, :] = exact_dot(w, b_ref[rows, :], ((1,), (0,)))
+        x_ref[rows, rows] = w
+
+        @pl.loop(k + 1, nb)
+        def _(i):
+            below = pl.ds(pl.multiple_of(i * NB, NB), NB)
+            ui = exact_dot(w, s_ref[rows, below], ((1,), (0,)))
+            s_ref[below, :] -= exact_dot(ui, u, ((0,), (0,)))
+            b_ref[below, :] -= exact_dot(ui, x_ref[rows, :], ((0,), (0,)))
+
+
+def chol_kernel(a_ref, x_ref, w_ref, s_ref, b_ref, ah_ref, al_ref, yh_ref, yl_ref, e_ref, d_ref):
+    n = a_ref.shape[0]
+    nb = n // NB
+    eye = (lax.broadcasted_iota(jnp.int32, (NB, NB), 0) == lax.broadcasted_iota(jnp.int32, (NB, NB), 1)).astype(F32)
+    lower = (lax.broadcasted_iota(jnp.int32, (NB, NB), 0) > lax.broadcasted_iota(jnp.int32, (NB, NB), 1)).astype(F32) + 0.5 * eye
+
+    for r in range(nb):
+        at = pl.ds(r * NB, NB)
+        d_ref[:, at] = lax.rsqrt(jnp.sum(a_ref[at, at] * eye, axis=0, keepdims=True))
+    for r in range(nb):
+        at = pl.ds(r * NB, NB)
+        here = jnp.sum(eye * d_ref[:, at], axis=1, keepdims=True)
+        hi, lo = halves(a_ref[at, :] * here * d_ref[...])
+        ah_ref[at, :] = hi
+        al_ref[at, :] = lo
+    x_ref[...] = jnp.zeros_like(x_ref)
+    for r in range(nb):
+        at = pl.ds(r * NB, NB)
+        end = (r + 1) * NB
+        a = ah_ref[at, :end].astype(F32)
+        if r:
+            x_ref[at, : r * NB] = -a[:, : r * NB]
+        x_ref[at, at] = eye - (a[:, r * NB :] - eye) * lower
+
+    def step(fine):
+        for r in range(nb):
+            at, end = pl.ds(r * NB, NB), (r + 1) * NB
+            hi, lo = halves(x_ref[at, :end])
+            yh_ref[at, :end] = hi
+            if fine:
+                yl_ref[at, :end] = lo
+        total = jnp.zeros((1, 1), F32)
+        for r in range(nb):
+            at, start, end = pl.ds(r * NB, NB), r * NB, (r + 1) * NB
+            yh = yh_ref[at, :end]
+            t = fast_dot(yh, ah_ref[:end, :end], ((1,), (0,)))
+            if fine:
+                t += fast_dot(yh, al_ref[:end, :end], ((1,), (0,))) + fast_dot(yl_ref[at, :end], ah_ref[:end, :end], ((1,), (0,)))
+            hi, lo = halves(t)
+            e = fast_dot(hi, yh_ref[:end, :end], ((1,), (1,)))
+            if fine:
+                e += fast_dot(lo, yh_ref[:end, :end], ((1,), (1,))) + fast_dot(hi, yl_ref[:end, :end], ((1,), (1,)))
+            corner = (e[:, start:] - eye) * lower
+            total += jnp.sum(corner * corner, keepdims=True)
+            e_ref[at, start:end] = corner.astype(BF)
+            if r:
+                left = e[:, :start]
+                total += jnp.sum(left * left, keepdims=True)
+                e_ref[at, :start] = left.astype(BF)
+        for r in reversed(range(nb)):
+            at, end = pl.ds(r * NB, NB), (r + 1) * NB
+            x_ref[at, :end] -= fast_dot(e_ref[at, :end], yh_ref[:end, :end], ((1,), (0,)))
+        return total[0, 0]
+
+    def more(tol, most):
+        return lambda state: jnp.logical_and(state[0] < most, state[1] > tol)
+
+    _, size = lax.while_loop(more(0.05, 10), lambda s: (s[0] + 1, step(False)), (0, jnp.float32(1e9)))
+    _, size = lax.while_loop(more(1e-5, 6), lambda s: (s[0] + 1, step(True)), (0, jnp.float32(1e9)))
+    good = size <= 1e-5
+
+    @pl.when(good)
+    def _():
+        for r in range(nb):
+            at, end = pl.ds(r * NB, NB), (r + 1) * NB
+            x_ref[at, :end] *= d_ref[:, :end]
+
+    @pl.when(jnp.logical_not(good))
+    def _():
+        eliminate(a_ref, x_ref, w_ref, s_ref, b_ref)
+
 
 def chol_inv(a):
     n = a.shape[0]
+    square = lambda kind: pltpu.VMEM((n, n), kind)
     return pl.pallas_call(
         chol_kernel,
-        out_shape=jax.ShapeDtypeStruct((n, n), jnp.float32),
+        out_shape=jax.ShapeDtypeStruct((n, n), F32),
         in_specs=[pl.BlockSpec(memory_space=pltpu.VMEM)],
         out_specs=pl.BlockSpec(memory_space=pltpu.VMEM),
-        scratch_shapes=[pltpu.VMEM((NB, NB), jnp.float32), pltpu.VMEM((n, n), jnp.float32), pltpu.VMEM((n, n), jnp.float32)],
-        cost_estimate=pl.CostEstimate(flops=60 * 10**9, bytes_accessed=2 * 2**20, transcendentals=0),
+        scratch_shapes=[pltpu.VMEM((NB, NB), F32), square(F32), square(F32), square(BF), square(BF), square(BF), square(BF), square(BF), pltpu.VMEM((1, n), F32)],
+        cost_estimate=pl.CostEstimate(flops=20 * 10**9, bytes_accessed=2 * 2**20, transcendentals=0),
         compiler_params=pltpu.CompilerParams(vmem_limit_bytes=32 * 2**20),
     )(a)
 
@@ -101,6 +191,18 @@
 def gather(x, axis, n):
     parts = lax.all_to_all(jnp.broadcast_to(x[None], (n,) + x.shape), axis, 0, 0, tiled=True)
     return parts.reshape(n * x.shape[0], x.shape[1])
+
+
+def inner_sums(x, nf, nt):
+    rank = x.shape[0]
+    k = x.shape[1] // rank
+    rows = rank // nt
+    mine = lax.dynamic_slice_in_dim(x, lax.axis_index("tp") * rows, rows, 0).astype(BF)
+    groups = rows // 8
+    wide = nf // groups
+    mine = mine.reshape(groups, 8, wide, x.shape[1] // wide).transpose(0, 2, 1, 3).reshape(nf * 8, x.shape[1] // wide)
+    whole = gather(scatter_sum(mine, "fsdp", nf).astype(BF), "fsdp", nf)
+    return whole.reshape(groups, wide, 8, x.shape[1] // wide).transpose(0, 2, 1, 3).reshape(rows, k * rank)
 
 
 def per_device(nf, nt, grad, start_basis, weight, first_moment, second_moment):
@@ -119,9 +221,9 @@
     panel = gather(panel, "fsdp", nf)
     image = scatter_sum(mm(grad, panel, 1, 0), "tp", nt).astype(BF)
     image = lax.all_gather(image, "tp", axis=0, tiled=True)
-    gram = scatter_sum(mm(image, image, 0, 0), "fsdp", nf)
-    gram = lax.all_gather(gram.astype(BF), "fsdp", axis=0, tiled=True)
+    gram = inner_sums(mm(image, image, 0, 0), nf, nt)
     raw, gram = lax.optimization_barrier((mm(grad, image, 0, 0).astype(BF), gram))
+    gram = lax.all_gather(gram, "tp", axis=0, tiled=True)
     inverse = chol_inv(gram.astype(F32) / M)
     first_basis = mm_split(image, inverse, 1, 1).astype(BF)
     raw = scatter_sum(raw, "fsdp", nf)
@@ -130,14 +232,11 @@
     panel = gather(panel, "fsdp", nf)
     image = scatter_sum(mm(grad, panel, 1, 0), "tp", nt).astype(BF)
     image = lax.all_gather(image, "tp", axis=0, tiled=True)
-    gram = scatter_sum(mm(image, image, 0, 0), "fsdp", nf)
-    gram = lax.all_gather(gram.astype(BF), "fsdp", axis=0, tiled=True)
-    raw, cross, gram = lax.optimization_barrier(
-        (mm(grad, image, 0, 0).astype(BF), mm(image, start_basis, 0, 0).astype(BF), gram)
-    )
+    both = inner_sums(mm(image, jnp.concatenate([image, start_basis], axis=1), 0, 0), nf, nt)
+    raw, both = lax.optimization_barrier((mm(grad, image, 0, 0).astype(BF), both))
+    gram = lax.all_gather(both[:, :rank], "tp", axis=0, tiled=True)
+    cross = lax.all_gather(both[:, rank:], "tp", axis=0, tiled=True)
     inverse = chol_inv(gram.astype(F32) / M)
-    cross = scatter_sum(cross, "fsdp", nf)
-    cross = gather(cross.astype(BF), "fsdp", nf)
     margin = mm_split(cross, inverse, 0, 1) / M
     new_basis = mm_split(image, inverse, 1, 1).astype(BF)
     raw = scatter_sum(raw, "fsdp", nf)

time: 511 us -> 516 us (level)
  blocking collectives: 208 us -> 190 us
  Pallas kernels: 143 us -> 160 us
  waiting for transfers between devices: 46.6 us -> 54.5 us
  starting transfers between devices: 34.9 us -> 41.6 us
    all_to_all x3 -> x2, blocking collectives: 62.3 us -> 44.3 us  [scatter_sum(): lax.all_to_all(x.astype(BF).reshape(n, x.shape[0] // n, x.shape[1]), axis...]
    pallas_call x2, Pallas kernels: 143 us -> 160 us  [chol_inv(): pl.pallas_call(chol_kernel, out_shape=jax.ShapeDtypeStruct((n, n), F32),...]
    all_to_all x2 -> x3, waiting for transfers between devices: 17.9 us -> 34.1 us  [gather(): lax.all_to_all(jnp.broadcast_to(x[None], (n,) + x.shape), axis, 0, 0, til...]
    all_to_all x1, waiting for transfers between devices: 8 us -> 0.01 us  [per_device(): lax.all_to_all(moments, 'fsdp', 0, 0, tiled=True).transpose(1, 0, 2)]
    all_gather x2 -> x3, blocking collectives: 45.5 us -> 39.3 us  [the longest x1 13.1 us: per_device(): gram = lax.all_gather(both[:, :rank], 'tp', axis=0, tiled=True)]
    all_to_all x2, blocking collectives: 57.6 us -> 63.5 us  [gather(): lax.all_to_all(jnp.broadcast_to(x[None], (n,) + x.shape), axis, 0, 0, til...]
    all_to_all x2 -> x3, starting transfers between devices: 8 us -> 12.4 us  [gather(): lax.all_to_all(jnp.broadcast_to(x[None], (n,) + x.shape), axis, 0, 0, til...]
    dot_general x23 -> x22, matrix products: 28.3 us -> 27.5 us  [mm(): lax.dot_general(a, b, (((ca,), (cb,)), ((), ())), preferred_element_type=...]
  transfers between devices with their start and end apart: 8 -> 9, of which waited for: 6 -> 6; matrix products, arithmetic and copies ran while one was open for 6% -> 5% of each run, Pallas kernels for 28% -> 31%
where the time goes in v3:
time: 516 us; the launch traced here: 514 us
  blocking collectives  190 us (37%)
  Pallas kernels  160 us (31%)
  waiting for transfers between devices  54.5 us (11%)
  starting transfers between devices  41.6 us (8%)
  local copies, waits for them, and re-layouts  28.1 us (5%)
  matrix products  27.5 us (5%)
  other arithmetic  11.8 us (2%)
    pallas_call x2, Pallas kernels, chol_inv(): pl.pallas_call(chol_kernel, out_shape=jax.ShapeDtypeStruct((n, n), F32),...  160 us
    all_to_all x2, blocking collectives, gather(): lax.all_to_all(jnp.broadcast_to(x[None], (n,) + x.shape), axis, 0, 0, til...  63.5 us
    all_to_all x2, blocking collectives, scatter_sum(): lax.all_to_all(x.astype(BF).reshape(n, x.shape[0] // n, x.shape[1]), axis...  44.3 us
    all_to_all x3, waiting for transfers between devices, gather(): lax.all_to_all(jnp.broadcast_to(x[None], (n,) + x.shape), axis, 0, 0, til...  34.1 us
    dot_general x22, matrix products, mm(): lax.dot_general(a, b, (((ca,), (cb,)), ((), ())), preferred_element_type=...  27.5 us
    all_gather x2, blocking collectives, per_device(): image = lax.all_gather(image, 'tp', axis=0, tiled=True)  26.4 us
    all_to_all x5, starting transfers between devices, scatter_sum(): lax.all_to_all(x.astype(BF).reshape(n, x.shape[0] // n, x.shape[1]), axis...  25 us
    all_to_all x5, waiting for transfers between devices, scatter_sum(): lax.all_to_all(x.astype(BF).reshape(n, x.shape[0] // n, x.shape[1]), axis...  20.4 us
  transfers between devices with their start and end apart: 9, of which 6 were waited for; matrix products, arithmetic and copies ran while one was open for 5% of the time, Pallas kernels for 31%

profile of v3, /device:TPU:0, one launch (start us, length us, event | category | flops | bytes accessed | tf_op | source)
XLA Modules:
  0.0 513.9 jit_solution(3167138974774199738)
XLA Ops:
  4.4 33.9 %all_to_all.70 = bf16[16,120,512]{2,1,0:T(8,128)(2,1)S(1)} all-to-all(bf16[16,120,512]{2,1,0:T(8,128)(2,1)S(1)} %bitcast.84), channel_id=1, replica_groups=mesh['fsdp'=16,'tp'=8] {'fsdp'}, dimensions={0} | all-to-all | bytes 3932160 | tf_op jit(solution)/shard_map/all_to_all | solution.py:187
  38.8 29.4 %all_to_all.71 = bf16[16,120,512]{2,1,0:T(8,128)(2,1)S(1)} all-to-all(bf16[16,120,512]{2,1,0:T(8,128)(2,1)S(1)} %broadcast_in_dim.10), channel_id=1, replica_groups=mesh['fsdp'=16,'tp'=8] {'fsdp'}, dimensions={0} | all-to-all | bytes 3932160 | tf_op jit(solution)/shard_map/all_to_all | solution.py:192
  70.3 5.3 %all-to-all-start.2 = ((bf16[8,64,512]{2,1,0:T(8,128)(2,1)}), bf16[8,64,512]{2,1,0:T(8,128)(2,1)S(1)}, u32[]{:S(2)}, u32[]{:S(2)}) async-start(bf16[8,64,512]{2,1,0:T(8,128)(2,1)} %bitcast.3), calls=%async_computation.2 | async-start | bytes 1048576 | tf_op jit(solution)/shard_map/all_to_all | solution.py:187
  75.6 10.3 %all-to-all-done.2 = bf16[8,64,512]{2,1,0:T(8,128)(2,1)S(1)} async-done(((bf16[8,64,512]{2,1,0:T(8,128)(2,1)}), bf16[8,64,512]{2,1,0:T(8,128)(2,1)S(1)}, u32[]{:S(2)}, u32[]{:S(2)}) %all-to-all-start.2) | async-done | bytes 524320 | tf_op jit(solution)/shard_map/all_to_all | solution.py:187
  86.0 13.1 %all_gather.15 = bf16[512,512]{1,0:T(8,128)(2,1)S(1)} all-gather(bf16[64,512]{1,0:T(8,128)(2,1)S(1)} %reduce_sum.76), channel_id=1, replica_groups=mesh['fsdp'=16,'tp'=8] {'tp'}, dimensions={0}, use_global_device_ids=true | all-gather | bytes 589824 | tf_op jit(solution)/shard_map/all_gather | solution.py:223
  99.7 10.4 %all_to_all.72 = bf16[16,8,256]{2,1,0:T(8,128)(2,1)S(1)} all-to-all(bf16[16,8,256]{2,1,0:T(8,128)(2,1)S(1)} %bitcast.93), channel_id=1, replica_groups=mesh['fsdp'=16,'tp'=8] {'fsdp'}, dimensions={0} | all-to-all | bytes 131072 | tf_op jit(solution)/shard_map/all_to_all | solution.py:187
  110.7 3.5 all-to-all-start.4
  114.2 2.6 fusion
  116.7 5.0 all-to-all-done.4
  121.8 13.1 %all_gather.16 = bf16[512,512]{1,0:T(8,128)(2,1)S(1)} all-gather(bf16[64,512]{1,0:T(8,128)(2,1)S(1)} %bitcast.92), channel_id=1, replica_groups=mesh['fsdp'=16,'tp'=8] {'tp'}, dimensions={0}, use_global_device_ids=true | all-gather | bytes 589824 | tf_op jit(solution)/shard_map/all_gather | solution.py:226
  136.0 4.0 copy.16
  140.0 4.4 all-to-all-start.5
  145.6 80.0 %shard_map.92 = f32[512,512]{1,0:T(8,128)S(1)} custom-call(f32[512,512]{1,0:T(8,128)S(1)} %copy-done.1), custom_call_target="tpu_custom_call" | custom-call | flops 20000000000 | bytes 2097152 | tf_op jit(solution)/shard_map/pallas_call | solution.py:159
  228.6 34.1 %all_to_all.73 = bf16[16,120,512]{2,1,0:T(8,128)(2,1)S(1)} all-to-all(bf16[16,120,512]{2,1,0:T(8,128)(2,1)S(1)} %broadcast_in_dim.12), channel_id=1, replica_groups=mesh['fsdp'=16,'tp'=8] {'fsdp'}, dimensions={0} | all-to-all | bytes 3932160 | tf_op jit(solution)/shard_map/all_to_all | solution.py:192
  264.8 3.5 all-to-all-start.7
  274.9 3.7 all-to-all-done.7
  278.6 4.2 all-to-all-start.10
  283.5 13.3 %all_gather.17 = bf16[512,512]{1,0:T(8,128)(2,1)S(1)} all-gather(bf16[64,512]{1,0:T(8,128)(2,1)} %reduce_sum.79), channel_id=1, replica_groups=mesh['fsdp'=16,'tp'=8] {'tp'}, dimensions={0}, use_global_device_ids=true | all-gather | bytes 589824 | tf_op jit(solution)/shard_map/all_gather | solution.py:234
  299.4 7.1 %all-to-all-start.8 = ((bf16[16,8,512]{2,1,0:T(8,128)(2,1)}), bf16[16,8,512]{2,1,0:T(8,128)(2,1)}, u32[]{:S(2)}, u32[]{:S(2)}) async-start(bf16[16,8,512]{2,1,0:T(8,128)(2,1)} %bitcast.89), calls=%async_computation.8 | async-start | bytes 262144 | tf_op jit(solution)/shard_map/all_to_all | solution.py:187
  308.3 6.4 %all-to-all-done.8 = bf16[16,8,512]{2,1,0:T(8,128)(2,1)} async-done(((bf16[16,8,512]{2,1,0:T(8,128)(2,1)}), bf16[16,8,512]{2,1,0:T(8,128)(2,1)}, u32[]{:S(2)}, u32[]{:S(2)}) %all-to-all-start.8) | async-done | bytes 131104 | tf_op jit(solution)/shard_map/all_to_all | solution.py:187
  316.2 4.2 all-to-all-start.9
  320.4 2.6 fusion.1
  323.0 5.4 %all-to-all-done.9 = bf16[16,8,512]{2,1,0:T(8,128)(2,1)} async-done(((bf16[16,8,512]{2,1,0:T(8,128)(2,1)}), bf16[16,8,512]{2,1,0:T(8,128)(2,1)}, u32[]{:S(2)}, u32[]{:S(2)}) %all-to-all-start.9) | async-done | bytes 131104 | tf_op jit(solution)/shard_map/all_to_all | solution.py:192
  329.3 13.1 %all_gather.18 = bf16[512,512]{1,0:T(8,128)(2,1)S(1)} all-gather(bf16[64,512]{1,0:T(8,128)(2,1)S(1)} %get-tuple-element.23), channel_id=1, replica_groups=mesh['fsdp'=16,'tp'=8] {'tp'}, dimensions={0}, use_global_device_ids=true | all-gather | bytes 589824 | tf_op jit(solution)/shard_map/all_gather | solution.py:237
  343.5 4.0 copy.18
  347.5 4.6 all-to-all-start.11
  353.4 79.8 %shard_map.93 = f32[512,512]{1,0:T(8,128)S(1)} custom-call(f32[512,512]{1,0:T(8,128)S(1)} %copy-done.2), custom_call_target="tpu_custom_call" | custom-call | flops 20000000000 | bytes 2097152 | tf_op jit(solution)/shard_map/pallas_call | solution.py:159
  433.2 13.1 %all_gather.19 = bf16[512,512]{1,0:T(8,128)(2,1)S(1)} all-gather(bf16[64,512]{1,0:T(8,128)(2,1)S(1)} %get-tuple-element.22), channel_id=1, replica_groups=mesh['fsdp'=16,'tp'=8] {'tp'}, dimensions={0}, use_global_device_ids=true | all-gather | bytes 589824 | tf_op jit(solution)/shard_map/all_gather | solution.py:238
  457.5 16.0 %all_to_all.74 = bf16[16,120,64]{1,2,0:T(8,128)(2,1)} all-to-all(bf16[16,120,64]{1,2,0:T(8,128)(2,1)S(1)} %maximum_bitcast_fusion), channel_id=1, replica_groups=mesh['fsdp'=16,'tp'=8] {'fsdp'}, dimensions={0} | all-to-all | bytes 491520 | tf_op jit(solution)/shard_map/all_to_all | solution.py:255
  475.8 4.7 all-to-all-start.13
  485.6 23.6 %all-to-all-done.13 = bf16[16,120,512]{2,1,0:T(8,128)(2,1)} async-done(((bf16[16,120,512]{2,1,0:T(8,128)(2,1)}), bf16[16,120,512]{2,1,0:T(8,128)(2,1)}, u32[]{:S(2)}, u32[]{:S(2)}) %all-to-all-start.13) | async-done | bytes 1966112 | tf_op jit(solution)/shard_map/all_to_all | solution.py:192
  509.2 4.7 subtract_convert_fusion
  (83 shorter events, 49.7 us)
Async XLA Ops:
  0.6 1.6 copy-start
  70.3 15.7 %all-to-all-start.2 = ((bf16[8,64,512]{2,1,0:T(8,128)(2,1)}), bf16[8,64,512]{2,1,0:T(8,128)(2,1)S(1)}, u32[]{:S(2)}, u32[]{:S(2)}) async-start(bf16[8,64,512]{2,1,0:T(8,128)(2,1)} %bitcast.3), calls=%async_computation.2 | async-start | bytes 1048576 | tf_op jit(solution)/shard_map/all_to_all | solution.py:187
  99.2 17.6 %copy-start.7 = (bf16[512,512]{1,0:T(8,128)(2,1)}, bf16[512,512]{1,0:T(8,128)(2,1)S(1)}, u32[]{:S(2)}) copy-start(bf16[512,512]{1,0:T(8,128)(2,1)S(1)} %all_gather.15) | copy-start | bytes 1572868
  110.7 11.1 %all-to-all-start.4 = ((bf16[16,8,256]{2,1,0:T(8,128)(2,1)}), bf16[16,8,256]{2,1,0:T(8,128)(2,1)S(1)}, u32[]{:S(2)}, u32[]{:S(2)}) async-start(bf16[16,8,256]{2,1,0:T(8,128)(2,1)} %broadcast_in_dim.11), calls=%async_computation.4 | async-start | bytes 131072 | tf_op jit(solution)/shard_map/all_to_all | solution.py:192
  140.0 85.7 %all-to-all-start.5 = ((bf16[16,120,512]{2,1,0:T(8,128)(2,1)}), bf16[16,120,512]{2,1,0:T(8,128)(2,1)}, u32[]{:S(2)}, u32[]{:S(2)}) async-start(bf16[16,120,512]{2,1,0:T(8,128)(2,1)} %bitcast.81), calls=%async_computation.5 | async-start | bytes 3932160 | tf_op jit(solution)/shard_map/all_to_all | solution.py:187
  144.4 1.2 copy-start.1
  264.8 13.8 %all-to-all-start.7 = ((bf16[8,64,512]{2,1,0:T(8,128)(2,1)}), bf16[8,64,512]{2,1,0:T(8,128)(2,1)S(1)}, u32[]{:S(2)}, u32[]{:S(2)}) async-start(bf16[8,64,512]{2,1,0:T(8,128)(2,1)} %bitcast.86), calls=%async_computation.7 | async-start | bytes 1048576 | tf_op jit(solution)/shard_map/all_to_all | solution.py:187
  278.6 20.9 %all-to-all-start.10 = ((bf16[16,120,64]{1,2,0:T(8,128)(2,1)}), bf16[16,120,64]{1,2,0:T(8,128)(2,1)}, u32[]{:S(2)}, u32[]{:S(2)}) async-start(bf16[16,120,64]{1,2,0:T(8,128)(2,1)} %copy.17), calls=%async_computation.10 | async-start | bytes 524288 | tf_op jit(solution)/shard_map/all_to_all | solution.py:216
  296.8 23.6 %copy-start.9 = (bf16[512,512]{1,0:T(8,128)(2,1)}, bf16[512,512]{1,0:T(8,128)(2,1)S(1)}, u32[]{:S(2)}) copy-start(bf16[512,512]{1,0:T(8,128)(2,1)S(1)} %all_gather.17) | copy-start | bytes 1572868
  299.4 15.2 %all-to-all-start.8 = ((bf16[16,8,512]{2,1,0:T(8,128)(2,1)}), bf16[16,8,512]{2,1,0:T(8,128)(2,1)}, u32[]{:S(2)}, u32[]{:S(2)}) async-start(bf16[16,8,512]{2,1,0:T(8,128)(2,1)} %bitcast.89), calls=%async_computation.8 | async-start | bytes 262144 | tf_op jit(solution)/shard_map/all_to_all | solution.py:187
  316.2 12.2 %all-to-all-start.9 = ((bf16[16,8,512]{2,1,0:T(8,128)(2,1)}), bf16[16,8,512]{2,1,0:T(8,128)(2,1)}, u32[]{:S(2)}, u32[]{:S(2)}) async-start(bf16[16,8,512]{2,1,0:T(8,128)(2,1)} %broadcast_in_dim.13), calls=%async_computation.9 | async-start | bytes 262144 | tf_op jit(solution)/shard_map/all_to_all | solution.py:192
  347.5 101.2 %all-to-all-start.11 = ((bf16[16,120,512]{2,1,0:T(8,128)(2,1)}), bf16[16,120,512]{2,1,0:T(8,128)(2,1)}, u32[]{:S(2)}, u32[]{:S(2)}) async-start(bf16[16,120,512]{2,1,0:T(8,128)(2,1)} %bitcast.80), calls=%async_computation.11 | async-start | bytes 3932160 | tf_op jit(solution)/shard_map/all_to_all | solution.py:187
  352.1 1.2 copy-start.2
  446.5 0.8 copy-start.4
  448.7 2.3 copy-start.5
  450.6 1.2 copy-start.3
  450.6 1.2 copy-start.14
  451.0 1.1 copy-start.13
  475.8 33.4 %all-to-all-start.13 = ((bf16[16,120,512]{2,1,0:T(8,128)(2,1)}), bf16[16,120,512]{2,1,0:T(8,128)(2,1)}, u32[]{:S(2)}, u32[]{:S(2)}) async-start(bf16[16,120,512]{2,1,0:T(8,128)(2,1)} %broadcast_in_dim.14), calls=%async_computation.13 | async-start | bytes 3932160 | tf_op jit(solution)/shard_map/all_to_all | solution.py:192
  480.5 1.6 copy-start.8
  482.1 1.3 copy-start.10
  482.1 1.8 copy-start.6
  483.4 1.0 copy-start.11
  484.3 29.5 %copy-start.12 = (bf16[512,512]{1,0:T(8,128)(2,1)}, bf16[512,512]{1,0:T(8,128)(2,1)S(1)}, u32[]{:S(2)}) copy-start(bf16[512,512]{1,0:T(8,128)(2,1)S(1)} %fusion.4) | copy-start | bytes 1572868

commit v4 on v3

--- a/solution.py
+++ b/solution.py
@@ -97,6 +97,8 @@
         ah_ref[at, :] = hi
         al_ref[at, :] = lo
     x_ref[...] = jnp.zeros_like(x_ref)
+    yh_ref[...] = jnp.zeros_like(yh_ref)
+    yl_ref[...] = jnp.zeros_like(yl_ref)
     for r in range(nb):
         at = pl.ds(r * NB, NB)
         end = (r + 1) * NB
@@ -162,7 +164,7 @@
         in_specs=[pl.BlockSpec(memory_space=pltpu.VMEM)],
         out_specs=pl.BlockSpec(memory_space=pltpu.VMEM),
         scratch_shapes=[pltpu.VMEM((NB, NB), F32), square(F32), square(F32), square(BF), square(BF), square(BF), square(BF), square(BF), pltpu.VMEM((1, n), F32)],
-        cost_estimate=pl.CostEstimate(flops=20 * 10**9, bytes_accessed=2 * 2**20, transcendentals=0),
+        cost_estimate=pl.CostEstimate(flops=10**9, bytes_accessed=2 * 2**20, transcendentals=0),
         compiler_params=pltpu.CompilerParams(vmem_limit_bytes=32 * 2**20),
     )(a)
 
@@ -193,7 +195,7 @@
     return parts.reshape(n * x.shape[0], x.shape[1])
 
 
-def inner_sums(x, nf, nt):
+def inner_sums(x, raw, nf, nt):
     rank = x.shape[0]
     k = x.shape[1] // rank
     rows = rank // nt
@@ -201,8 +203,9 @@
     groups = rows // 8
     wide = nf // groups
     mine = mine.reshape(groups, 8, wide, x.shape[1] // wide).transpose(0, 2, 1, 3).reshape(nf * 8, x.shape[1] // wide)
-    whole = gather(scatter_sum(mine, "fsdp", nf).astype(BF), "fsdp", nf)
-    return whole.reshape(groups, wide, 8, x.shape[1] // wide).transpose(0, 2, 1, 3).reshape(rows, k * rank)
+    sums, raw = lax.optimization_barrier((scatter_sum(mine, "fsdp", nf).astype(BF), raw))
+    whole = lax.all_gather(sums, "fsdp", axis=0, tiled=True)
+    return whole.reshape(groups, wide, 8, x.shape[1] // wide).transpose(0, 2, 1, 3).reshape(rows, k * rank), raw
 
 
 def per_device(nf, nt, grad, start_basis, weight, first_moment, second_moment):
@@ -221,8 +224,7 @@
     panel = gather(panel, "fsdp", nf)
     image = scatter_sum(mm(grad, panel, 1, 0), "tp", nt).astype(BF)
     image = lax.all_gather(image, "tp", axis=0, tiled=True)
-    gram = inner_sums(mm(image, image, 0, 0), nf, nt)
-    raw, gram = lax.optimization_barrier((mm(grad, image, 0, 0).astype(BF), gram))
+    gram, raw = inner_sums(mm(image, image, 0, 0), mm(grad, image, 0, 0).astype(BF), nf, nt)
     gram = lax.all_gather(gram, "tp", axis=0, tiled=True)
     inverse = chol_inv(gram.astype(F32) / M)
     first_basis = mm_split(image, inverse, 1, 1).astype(BF)
@@ -232,8 +234,8 @@
     panel = gather(panel, "fsdp", nf)
     image = scatter_sum(mm(grad, panel, 1, 0), "tp", nt).astype(BF)
     image = lax.all_gather(image, "tp", axis=0, tiled=True)
-    both = inner_sums(mm(image, jnp.concatenate([image, start_basis], axis=1), 0, 0), nf, nt)
-    raw, both = lax.optimization_barrier((mm(grad, image, 0, 0).astype(BF), both))
+    both = mm(image, jnp.concatenate([image, start_basis], axis=1), 0, 0)
+    both, raw = inner_sums(both, mm(grad, image, 0, 0).astype(BF), nf, nt)
     gram = lax.all_gather(both[:, :rank], "tp", axis=0, tiled=True)
     cross = lax.all_gather(both[:, rank:], "tp", axis=0, tiled=True)
     inverse = chol_inv(gram.astype(F32) / M)
@@ -248,14 +250,14 @@
     moment_two = BETA_TWO * rotated_two + (1.0 - BETA_TWO) * reduced * reduced
     direction = (moment_one / (jnp.sqrt(moment_two) + ADAM_EPS)).astype(BF)
 
-    back = jnp.concatenate(
-        [moment_one.astype(BF).reshape(share_cols, nf, share_rows), moment_two.astype(BF).reshape(share_cols, nf, share_rows)], axis=2
-    ).transpose(1, 0, 2)
-    direction = gather(direction, "fsdp", nf)
-    back = lax.all_to_all(back, "fsdp", 0, 0, tiled=True).reshape(cols, 2 * share_rows)
-    expanded = mm(new_basis, direction, 1, 1)
+    back = jnp.stack([moment_one.astype(BF), moment_two.astype(BF)], axis=1)
+    back = back.reshape(share_cols, 2, nf, share_rows).transpose(2, 0, 1, 3).reshape(nf, share_cols, 2 * share_rows)
+    back = jnp.pad(back, ((0, 0), (0, 0), (0, -2 * share_rows % 128)))
+    sent = jnp.concatenate([jnp.broadcast_to(direction[None], (nf, share_cols, rank)), back], axis=2)
+    got = lax.all_to_all(sent, "fsdp", 0, 0, tiled=True).reshape(cols, sent.shape[2])
+    expanded = mm(new_basis, got[:, :rank], 1, 1)
     new_weight = (weight.astype(F32) - STEP_SIZE * inv_sqrt * expanded).astype(BF)
-    moments = back.astype(F32).T
+    moments = got[:, rank : rank + 2 * share_rows].astype(F32).T
     moment_one, moment_two = moments[:share_rows], moments[share_rows:]
     return (first_basis, new_basis, moment_one, moment_two, new_weight)
 

time: 516 us -> 574 us (1.11)
  waiting for transfers between devices: 54.5 us -> 101 us
  Pallas kernels: 160 us -> 169 us
    all_gather x0 -> x2, blocking collectives: none -> 62.9 us  [inner_sums(): whole = lax.all_gather(sums, 'fsdp', axis=0, tiled=True)]
    all_to_all x0 -> x1, waiting for transfers between devices: none -> 35 us  [per_device(): lax.all_to_all(sent, 'fsdp', 0, 0, tiled=True).reshape(cols, sent.shape[2])]
    all_to_all x2 -> x1, blocking collectives: 63.5 us -> 29.4 us  [gather(): lax.all_to_all(jnp.broadcast_to(x[None], (n,) + x.shape), axis, 0, 0, til...]
    all_to_all x1 -> x0, blocking collectives: 16 us -> none  [per_device(): lax.all_to_all(back, 'fsdp', 0, 0, tiled=True).reshape(cols, 2 * share_rows)]
    all_to_all x2 -> x1, blocking collectives: 44.3 us -> 33.9 us  [scatter_sum(): lax.all_to_all(x.astype(BF).reshape(n, x.shape[0] // n, x.shape[1]), axis...]
    all_to_all x5 -> x6, waiting for transfers between devices: 20.4 us -> 29.5 us  [scatter_sum(): lax.all_to_all(x.astype(BF).reshape(n, x.shape[0] // n, x.shape[1]), axis...]
    pallas_call x2, Pallas kernels: 160 us -> 169 us  [chol_inv(): pl.pallas_call(chol_kernel, out_shape=jax.ShapeDtypeStruct((n, n), F32),...]
    all_to_all x3 -> x1, starting transfers between devices: 12.4 us -> 4.58 us  [gather(): lax.all_to_all(jnp.broadcast_to(x[None], (n,) + x.shape), axis, 0, 0, til...]
  transfers between devices with their start and end apart: 9 -> 9, of which waited for: 6 -> 7; matrix products, arithmetic and copies ran while one was open for 5% -> 3% of each run, Pallas kernels for 31% -> 29%
where the time goes in v4:
time: 574 us; the launch traced here: 573 us
  blocking collectives  192 us (33%)
  Pallas kernels  169 us (29%)
  waiting for transfers between devices  101 us (18%)
  starting transfers between devices  40.9 us (7%)
  local copies, waits for them, and re-layouts  29.7 us (5%)
  matrix products  29 us (5%)
  other arithmetic  10.1 us (2%)
    pallas_call x2, Pallas kernels, chol_inv(): pl.pallas_call(chol_kernel, out_shape=jax.ShapeDtypeStruct((n, n), F32),...  169 us
    all_gather x2, blocking collectives, inner_sums(): whole = lax.all_gather(sums, 'fsdp', axis=0, tiled=True)  62.9 us
    all_to_all x1, waiting for transfers between devices, per_device(): lax.all_to_all(sent, 'fsdp', 0, 0, tiled=True).reshape(cols, sent.shape[2])  35 us
    all_to_all x1, blocking collectives, scatter_sum(): lax.all_to_all(x.astype(BF).reshape(n, x.shape[0] // n, x.shape[1]), axis...  33.9 us
    all_to_all x1, waiting for transfers between devices, gather(): lax.all_to_all(jnp.broadcast_to(x[None], (n,) + x.shape), axis, 0, 0, til...  31.2 us
    all_to_all x6, waiting for transfers between devices, scatter_sum(): lax.all_to_all(x.astype(BF).reshape(n, x.shape[0] // n, x.shape[1]), axis...  29.5 us
    all_to_all x1, blocking collectives, gather(): lax.all_to_all(jnp.broadcast_to(x[None], (n,) + x.shape), axis, 0, 0, til...  29.4 us
    dot_general x22, matrix products, mm(): lax.dot_general(a, b, (((ca,), (cb,)), ((), ())), preferred_element_type=...  29 us
  transfers between devices with their start and end apart: 9, of which 7 were waited for; matrix products, arithmetic and copies ran while one was open for 3% of the time, Pallas kernels for 29%

profile of v4, /device:TPU:0, one launch (start us, length us, event | category | flops | bytes accessed | tf_op | source)
XLA Modules:
  0.0 572.5 jit_solution(4351693360903451301)
XLA Ops:
  4.4 33.9 %all_to_all.55 = bf16[16,120,512]{2,1,0:T(8,128)(2,1)S(1)} all-to-all(bf16[16,120,512]{2,1,0:T(8,128)(2,1)S(1)} %bitcast.82), channel_id=1, replica_groups=mesh['fsdp'=16,'tp'=8] {'fsdp'}, dimensions={0} | all-to-all | bytes 3932160 | tf_op jit(solution)/shard_map/all_to_all | solution.py:189
  38.8 29.4 %all_to_all.56 = bf16[16,120,512]{2,1,0:T(8,128)(2,1)S(1)} all-to-all(bf16[16,120,512]{2,1,0:T(8,128)(2,1)S(1)} %broadcast_in_dim.6), channel_id=1, replica_groups=mesh['fsdp'=16,'tp'=8] {'fsdp'}, dimensions={0} | all-to-all | bytes 3932160 | tf_op jit(solution)/shard_map/all_to_all | solution.py:194
  70.3 5.3 all-to-all-start.2
  75.6 10.3 %all-to-all-done.2 = bf16[8,64,512]{2,1,0:T(8,128)(2,1)S(1)} async-done(((bf16[8,64,512]{2,1,0:T(8,128)(2,1)}), bf16[8,64,512]{2,1,0:T(8,128)(2,1)S(1)}, u32[]{:S(2)}, u32[]{:S(2)}) %all-to-all-start.2) | async-done | bytes 524320 | tf_op jit(solution)/shard_map/all_to_all | solution.py:189
  86.0 13.1 %all_gather.21 = bf16[512,512]{1,0:T(8,128)(2,1)S(1)} all-gather(bf16[64,512]{1,0:T(8,128)(2,1)S(1)} %reduce_sum.76), channel_id=1, replica_groups=mesh['fsdp'=16,'tp'=8] {'tp'}, dimensions={0}, use_global_device_ids=true | all-gather | bytes 589824 | tf_op jit(solution)/shard_map/all_gather | solution.py:226
  100.3 3.5 all-to-all-start.3
  103.8 2.6 fusion.1
  106.3 5.0 all-to-all-done.3
  111.4 4.0 copy.11
  115.4 4.4 all-to-all-start.4
  119.9 41.5 %all_gather.22 = bf16[128,256]{1,0:T(8,128)(2,1)S(1)} all-gather(bf16[8,256]{1,0:T(8,128)(2,1)S(1)} %reduce_sum.77), channel_id=1, replica_groups=mesh['fsdp'=16,'tp'=8] {'fsdp'}, dimensions={0}, use_global_device_ids=true | all-gather | bytes 69632 | tf_op jit(solution)/shard_map/all_gather | solution.py:207
  161.3 13.1 %all_gather.23 = bf16[512,512]{1,0:T(8,128)(2,1)S(1)} all-gather(bf16[64,512]{1,0:T(8,128)(2,1)S(1)} %bitcast.92), channel_id=1, replica_groups=mesh['fsdp'=16,'tp'=8] {'tp'}, dimensions={0}, use_global_device_ids=true | all-gather | bytes 589824 | tf_op jit(solution)/shard_map/all_gather | solution.py:228
  174.6 85.5 %shard_map.92 = f32[512,512]{1,0:T(8,128)S(1)} custom-call(f32[512,512]{1,0:T(8,128)S(1)} %convert_multiply_fusion.1.a_ref), custom_call_target="tpu_custom_call" | custom-call | flops 1000000000 | bytes 2097152 | tf_op jit(solution)/shard_map/pallas_call | solution.py:161
  264.3 4.6 all-to-all-start.5
  270.4 31.2 %all-to-all-done.5 = bf16[16,120,512]{2,1,0:T(8,128)(2,1)} async-done(((bf16[16,120,512]{2,1,0:T(8,128)(2,1)}), bf16[16,120,512]{2,1,0:T(8,128)(2,1)}, u32[]{:S(2)}, u32[]{:S(2)}) %all-to-all-start.5) | async-done | bytes 1966112 | tf_op jit(solution)/shard_map/all_to_all | solution.py:194
  301.6 3.5 all-to-all-start.8
  305.1 3.6 convolution_convert_fusion.3
  308.7 5.1 all-to-all-done.8
  314.5 3.5 all-to-all-start.6
  319.7 8.6 %all-to-all-done.6 = bf16[8,64,512]{2,1,0:T(8,128)(2,1)S(1)} async-done(((bf16[8,64,512]{2,1,0:T(8,128)(2,1)}), bf16[8,64,512]{2,1,0:T(8,128)(2,1)S(1)}, u32[]{:S(2)}, u32[]{:S(2)}) %all-to-all-start.6) | async-done | bytes 524320 | tf_op jit(solution)/shard_map/all_to_all | solution.py:189
  329.0 13.3 %all_gather.24 = bf16[512,512]{1,0:T(8,128)(2,1)S(1)} all-gather(bf16[64,512]{1,0:T(8,128)(2,1)} %reduce_sum.79), channel_id=1, replica_groups=mesh['fsdp'=16,'tp'=8] {'tp'}, dimensions={0}, use_global_device_ids=true | all-gather | bytes 589824 | tf_op jit(solution)/shard_map/all_gather | solution.py:236
  344.9 4.2 all-to-all-start.7
  351.6 5.5 all-to-all-done.7
  358.1 21.5 %all_gather.25 = bf16[128,512]{1,0:T(8,128)(2,1)S(1)} all-gather(bf16[8,512]{1,0:T(8,128)(2,1)S(1)} %reduce_sum.80), channel_id=1, replica_groups=mesh['fsdp'=16,'tp'=8] {'fsdp'}, dimensions={0}, use_global_device_ids=true | all-gather | bytes 139264 | tf_op jit(solution)/shard_map/all_gather | solution.py:207
  379.6 4.0 copy.13
  383.5 4.7 all-to-all-start.9
  388.2 13.3 %all_gather.26 = bf16[512,512]{1,0:T(8,128)(2,1)S(1)} all-gather(bf16[64,512]{1,0:T(8,128)(2,1)S(1)} %get-tuple-element.28), channel_id=1, replica_groups=mesh['fsdp'=16,'tp'=8] {'tp'}, dimensions={0}, use_global_device_ids=true | all-gather | bytes 589824 | tf_op jit(solution)/shard_map/all_gather | solution.py:239
  401.7 83.2 %shard_map.93 = f32[512,512]{1,0:T(8,128)S(1)} custom-call(f32[512,512]{1,0:T(8,128)S(1)} %convert_multiply_fusion.a_ref), custom_call_target="tpu_custom_call" | custom-call | flops 1000000000 | bytes 2097152 | tf_op jit(solution)/shard_map/pallas_call | solution.py:161
  484.9 13.1 %all_gather.27 = bf16[512,512]{1,0:T(8,128)(2,1)S(1)} all-gather(bf16[64,512]{1,0:T(8,128)(2,1)S(1)} %get-tuple-element.27), channel_id=1, replica_groups=mesh['fsdp'=16,'tp'=8] {'tp'}, dimensions={0}, use_global_device_ids=true | all-gather | bytes 589824 | tf_op jit(solution)/shard_map/all_gather | solution.py:240
  514.6 7.2 %all-to-all-start.10 = ((bf16[16,120,640]{2,1,0:T(8,128)(2,1)}), bf16[16,120,640]{2,1,0:T(8,128)(2,1)}, u32[]{:S(2)}, u32[]{:S(2)}) async-start(bf16[16,120,640]{2,1,0:T(8,128)(2,1)} %fusion.3), calls=%async_computation.10 | async-start | bytes 4915200 | tf_op jit(solution)/shard_map/all_to_all | solution.py:257
  525.7 35.0 %all-to-all-done.10 = bf16[16,120,640]{2,1,0:T(8,128)(2,1)} async-done(((bf16[16,120,640]{2,1,0:T(8,128)(2,1)}), bf16[16,120,640]{2,1,0:T(8,128)(2,1)}, u32[]{:S(2)}, u32[]{:S(2)}) %all-to-all-start.10) | async-done | bytes 2457632 | tf_op jit(solution)/shard_map/all_to_all | solution.py:257
  567.8 4.7 subtract_convert_fusion
  (86 shorter events, 50.0 us)
Async XLA Ops:
  0.6 1.6 copy-start
  70.3 15.7 %all-to-all-start.2 = ((bf16[8,64,512]{2,1,0:T(8,128)(2,1)}), bf16[8,64,512]{2,1,0:T(8,128)(2,1)S(1)}, u32[]{:S(2)}, u32[]{:S(2)}) async-start(bf16[8,64,512]{2,1,0:T(8,128)(2,1)} %bitcast.3), calls=%async_computation.2 | async-start | bytes 1048576 | tf_op jit(solution)/shard_map/all_to_all | solution.py:189
  99.2 7.2 %copy-start.5 = (bf16[512,512]{1,0:T(8,128)(2,1)}, bf16[512,512]{1,0:T(8,128)(2,1)S(1)}, u32[]{:S(2)}) copy-start(bf16[512,512]{1,0:T(8,128)(2,1)S(1)} %all_gather.21) | copy-start | bytes 1572868
  100.3 11.1 %all-to-all-start.3 = ((bf16[16,8,256]{2,1,0:T(8,128)(2,1)}), bf16[16,8,256]{2,1,0:T(8,128)(2,1)S(1)}, u32[]{:S(2)}, u32[]{:S(2)}) async-start(bf16[16,8,256]{2,1,0:T(8,128)(2,1)} %bitcast.6), calls=%async_computation.3 | async-start | bytes 131072 | tf_op jit(solution)/shard_map/all_to_all | solution.py:189
  115.4 144.7 %all-to-all-start.4 = ((bf16[16,120,512]{2,1,0:T(8,128)(2,1)}), bf16[16,120,512]{2,1,0:T(8,128)(2,1)}, u32[]{:S(2)}, u32[]{:S(2)}) async-start(bf16[16,120,512]{2,1,0:T(8,128)(2,1)} %bitcast.80), calls=%async_computation.4 | async-start | bytes 3932160 | tf_op jit(solution)/shard_map/all_to_all | solution.py:189
  264.3 4.6 copy-start.14
  264.3 4.6 copy-start.15
  264.3 37.2 %all-to-all-start.5 = ((bf16[16,120,512]{2,1,0:T(8,128)(2,1)}), bf16[16,120,512]{2,1,0:T(8,128)(2,1)}, u32[]{:S(2)}, u32[]{:S(2)}) async-start(bf16[16,120,512]{2,1,0:T(8,128)(2,1)} %broadcast_in_dim.7), calls=%async_computation.5 | async-start | bytes 3932160 | tf_op jit(solution)/shard_map/all_to_all | solution.py:194
  301.6 12.2 %all-to-all-start.8 = ((bf16[16,120,64]{1,2,0:T(8,128)(2,1)}), bf16[16,120,64]{1,2,0:T(8,128)(2,1)S(1)}, u32[]{:S(2)}, u32[]{:S(2)}) async-start(bf16[16,120,64]{1,2,0:T(8,128)(2,1)} %copy.12), calls=%async_computation.8 | async-start | bytes 524288 | tf_op jit(solution)/shard_map/all_to_all | solution.py:219
  313.8 0.7 copy-start.10
  314.5 13.8 %all-to-all-start.6 = ((bf16[8,64,512]{2,1,0:T(8,128)(2,1)}), bf16[8,64,512]{2,1,0:T(8,128)(2,1)S(1)}, u32[]{:S(2)}, u32[]{:S(2)}) async-start(bf16[8,64,512]{2,1,0:T(8,128)(2,1)} %bitcast.85), calls=%async_computation.6 | async-start | bytes 1048576 | tf_op jit(solution)/shard_map/all_to_all | solution.py:189
  342.3 6.8 %copy-start.7 = (bf16[512,512]{1,0:T(8,128)(2,1)}, bf16[512,512]{1,0:T(8,128)(2,1)S(1)}, u32[]{:S(2)}) copy-start(bf16[512,512]{1,0:T(8,128)(2,1)S(1)} %all_gather.24) | copy-start | bytes 1572868
  344.9 12.2 %all-to-all-start.7 = ((bf16[16,8,512]{2,1,0:T(8,128)(2,1)}), bf16[16,8,512]{2,1,0:T(8,128)(2,1)}, u32[]{:S(2)}, u32[]{:S(2)}) async-start(bf16[16,8,512]{2,1,0:T(8,128)(2,1)} %bitcast.89), calls=%async_computation.7 | async-start | bytes 262144 | tf_op jit(solution)/shard_map/all_to_all | solution.py:189
  383.5 116.9 %all-to-all-start.9 = ((bf16[16,120,512]{2,1,0:T(8,128)(2,1)}), bf16[16,120,512]{2,1,0:T(8,128)(2,1)}, u32[]{:S(2)}, u32[]{:S(2)}) async-start(bf16[16,120,512]{2,1,0:T(8,128)(2,1)} %bitcast.79), calls=%async_computation.9 | async-start | bytes 3932160 | tf_op jit(solution)/shard_map/all_to_all | solution.py:189
  498.1 0.8 copy-start.2
  500.4 2.3 copy-start.3
  502.3 1.2 copy-start.1
  502.3 1.2 copy-start.13
  502.7 1.1 copy-start.12
  511.8 1.1 copy-start.9
  514.6 46.1 %all-to-all-start.10 = ((bf16[16,120,640]{2,1,0:T(8,128)(2,1)}), bf16[16,120,640]{2,1,0:T(8,128)(2,1)}, u32[]{:S(2)}, u32[]{:S(2)}) async-start(bf16[16,120,640]{2,1,0:T(8,128)(2,1)} %fusion.3), calls=%async_computation.10 | async-start | bytes 4915200 | tf_op jit(solution)/shard_map/all_to_all | solution.py:257
  521.9 1.6 copy-start.6
  523.5 1.3 copy-start.8
  523.5 1.8 copy-start.4
  525.7 42.1 %copy-start.11 = (bf16[512,512]{1,0:T(8,128)(2,1)}, bf16[512,512]{1,0:T(8,128)(2,1)S(1)}, u32[]{:S(2)}) copy-start(bf16[512,512]{1,0:T(8,128)(2,1)S(1)} %fusion.7) | copy-start | bytes 1572868

commit v5 on v4

--- a/solution.py
+++ b/solution.py
@@ -1,3 +1,4 @@
+import functools
 import math
 
 import jax
@@ -5,6 +6,7 @@
 from jax import lax
 from jax.experimental import pallas as pl
 from jax.experimental.pallas import tpu as pltpu
+from jax.experimental.layout import Layout, with_layout_constraint
 from jax.sharding import PartitionSpec as P
 
 M = 8192
@@ -195,17 +197,52 @@
     return parts.reshape(n * x.shape[0], x.shape[1])
 
 
-def inner_sums(x, raw, nf, nt):
-    rank = x.shape[0]
-    k = x.shape[1] // rank
-    rows = rank // nt
+def row_major(x):
+    return with_layout_constraint(x, Layout(tuple(range(x.ndim))))
+
+
+def chunks(x, nf, nt):
+    rows = x.shape[0] // nt
     mine = lax.dynamic_slice_in_dim(x, lax.axis_index("tp") * rows, rows, 0).astype(BF)
-    groups = rows // 8
-    wide = nf // groups
-    mine = mine.reshape(groups, 8, wide, x.shape[1] // wide).transpose(0, 2, 1, 3).reshape(nf * 8, x.shape[1] // wide)
-    sums, raw = lax.optimization_barrier((scatter_sum(mine, "fsdp", nf).astype(BF), raw))
-    whole = lax.all_gather(sums, "fsdp", axis=0, tiled=True)
-    return whole.reshape(groups, wide, 8, x.shape[1] // wide).transpose(0, 2, 1, 3).reshape(rows, k * rank), raw
+    return mine.reshape(rows // 8, 8, x.shape[1] // 128, 128).transpose(0, 2, 1, 3).reshape(nf, -1, 128)
+
+
+def unchunk(parts, nf, rows):
+    whole = gather(jnp.sum(parts.astype(F32), axis=0).astype(BF), "fsdp", nf)
+    return whole.reshape(rows // 8, -1, 8, 128).transpose(0, 2, 1, 3).reshape(rows, -1)
+
+
+def finish_kernel(scale, parts_ref, high_ref, low_ref, one_ref, two_ref, out_ref):
+    nf, rows, rank = parts_ref.shape
+    share = rank // nf
+    raw = parts_ref[0].astype(F32)
+    for g in range(1, nf):
+        raw += parts_ref[g].astype(F32)
+    hi, lo = halves(raw)
+    dims = ((1,), (1,))
+    reduced = (fast_dot(hi, high_ref[...], dims) + fast_dot(lo, high_ref[...], dims) + fast_dot(hi, low_ref[...], dims)) * scale
+    one = BETA_ONE * one_ref[...] + (1.0 - BETA_ONE) * reduced
+    two = BETA_TWO * two_ref[...] + (1.0 - BETA_TWO) * reduced * reduced
+    direction = (one / (jnp.sqrt(two) + ADAM_EPS)).astype(BF)
+    fill = jnp.zeros((rows, out_ref.shape[2] - rank - 2 * share), F32)
+    for g in range(nf):
+        out_ref[g, :, :rank] = direction
+        at = slice(g * share, (g + 1) * share)
+        out_ref[g, :, rank:] = jnp.concatenate([one[:, at], two[:, at], fill], axis=1).astype(BF)
+
+
+def finish(scale, parts, high, low, one, two):
+    nf, rows, rank = parts.shape
+    width = rank + 2 * rank // nf
+    width += -width % 128
+    return pl.pallas_call(
+        functools.partial(finish_kernel, scale),
+        out_shape=jax.ShapeDtypeStruct((nf, rows, width), BF),
+        in_specs=[pl.BlockSpec(memory_space=pltpu.VMEM)] * 5,
+        out_specs=pl.BlockSpec(memory_space=pltpu.VMEM),
+        cost_estimate=pl.CostEstimate(flops=10**9, bytes_accessed=6 * 2**20, transcendentals=0),
+        compiler_params=pltpu.CompilerParams(vmem_limit_bytes=32 * 2**20),
+    )(parts, high, low, one, two)
 
 
 def per_device(nf, nt, grad, start_basis, weight, first_moment, second_moment):
@@ -214,17 +251,21 @@
     share_cols = cols // nf
     rank = start_basis.shape[1]
 
-    moments = jnp.concatenate([first_moment.astype(BF), second_moment.astype(BF)], axis=0)
-    moments = moments.T.reshape(nf, share_cols, 2 * share_rows)
-    moments = lax.all_to_all(moments, "fsdp", 0, 0, tiled=True).transpose(1, 0, 2)
-    first_t = moments[:, :, :share_rows].reshape(share_cols, rank)
-    second_t = moments[:, :, share_rows:].reshape(share_cols, rank)
+    sent = jnp.concatenate([first_moment.astype(BF), second_moment.astype(BF)], axis=0)
+    sent = sent.reshape(2 * share_rows, nf, share_cols).transpose(1, 0, 2)
+    sent = row_major(jnp.pad(sent, ((0, 0), (0, 0), (0, -share_cols % 128))))
 
     panel = (scatter_sum(mm(grad, start_basis, 0, 0), "fsdp", nf) * inv_sqrt).astype(BF)
     panel = gather(panel, "fsdp", nf)
     image = scatter_sum(mm(grad, panel, 1, 0), "tp", nt).astype(BF)
     image = lax.all_gather(image, "tp", axis=0, tiled=True)
-    gram, raw = inner_sums(mm(image, image, 0, 0), mm(grad, image, 0, 0).astype(BF), nf, nt)
+    raw = row_major(mm(grad, image, 0, 0).astype(BF))
+    rows = rank // nt
+    got = jnp.concatenate([sent, chunks(mm(image, image, 0, 0), nf, nt)], axis=1)
+    got = lax.all_to_all(got, "fsdp", 0, 0, tiled=True)
+    first_old = got[:, :share_rows].reshape(rank, -1)
+    second_old = got[:, share_rows : 2 * share_rows].reshape(rank, -1)
+    gram, raw = lax.optimization_barrier((unchunk(got[:, 2 * share_rows :], nf, rows), raw))
     gram = lax.all_gather(gram, "tp", axis=0, tiled=True)
     inverse = chol_inv(gram.astype(F32) / M)
     first_basis = mm_split(image, inverse, 1, 1).astype(BF)
@@ -234,31 +275,25 @@
     panel = gather(panel, "fsdp", nf)
     image = scatter_sum(mm(grad, panel, 1, 0), "tp", nt).astype(BF)
     image = lax.all_gather(image, "tp", axis=0, tiled=True)
-    both = mm(image, jnp.concatenate([image, start_basis], axis=1), 0, 0)
-    both, raw = inner_sums(both, mm(grad, image, 0, 0).astype(BF), nf, nt)
+    raw = row_major(mm(grad, image, 0, 0).astype(BF))
+    both = chunks(mm(image, jnp.concatenate([image, start_basis], axis=1), 0, 0), nf, nt)
+    both = unchunk(lax.all_to_all(both, "fsdp", 0, 0, tiled=True), nf, rows)
+    both, raw = lax.optimization_barrier((both, raw))
     gram = lax.all_gather(both[:, :rank], "tp", axis=0, tiled=True)
     cross = lax.all_gather(both[:, rank:], "tp", axis=0, tiled=True)
     inverse = chol_inv(gram.astype(F32) / M)
     margin = mm_split(cross, inverse, 0, 1) / M
     new_basis = mm_split(image, inverse, 1, 1).astype(BF)
-    raw = scatter_sum(raw, "fsdp", nf)
-    reduced = mm_split2(raw, inverse, 1, 1) * inv_sqrt
-
-    rotated_one = mm(first_t, margin.astype(BF), 1, 0)
-    rotated_two = mm(second_t, (margin * margin).astype(BF), 1, 0)
-    moment_one = BETA_ONE * rotated_one + (1.0 - BETA_ONE) * reduced
-    moment_two = BETA_TWO * rotated_two + (1.0 - BETA_TWO) * reduced * reduced
-    direction = (moment_one / (jnp.sqrt(moment_two) + ADAM_EPS)).astype(BF)
-
-    back = jnp.stack([moment_one.astype(BF), moment_two.astype(BF)], axis=1)
-    back = back.reshape(share_cols, 2, nf, share_rows).transpose(2, 0, 1, 3).reshape(nf, share_cols, 2 * share_rows)
-    back = jnp.pad(back, ((0, 0), (0, 0), (0, -2 * share_rows % 128)))
-    sent = jnp.concatenate([jnp.broadcast_to(direction[None], (nf, share_cols, rank)), back], axis=2)
+    rotated_one = mm(first_old, margin.astype(BF), 0, 0)[:share_cols]
+    rotated_two = mm(second_old, (margin * margin).astype(BF), 0, 0)[:share_cols]
+    parts = lax.all_to_all(raw.reshape(nf, share_cols, rank), "fsdp", 0, 0, tiled=True)
+    sent = finish(inv_sqrt, parts, *halves(inverse), rotated_one, rotated_two)
     got = lax.all_to_all(sent, "fsdp", 0, 0, tiled=True).reshape(cols, sent.shape[2])
     expanded = mm(new_basis, got[:, :rank], 1, 1)
     new_weight = (weight.astype(F32) - STEP_SIZE * inv_sqrt * expanded).astype(BF)
-    moments = got[:, rank : rank + 2 * share_rows].astype(F32).T
-    moment_one, moment_two = moments[:share_rows], moments[share_rows:]
+    eye = jnp.eye(share_rows, dtype=BF)
+    moment_one = mm(eye, got[:, rank : rank + share_rows], 1, 1)
+    moment_two = mm(eye, got[:, rank + share_rows : rank + 2 * share_rows], 1, 1)
     return (first_basis, new_basis, moment_one, moment_two, new_weight)
 
 

time: 574 us -> 505 us (0.88)
  waiting for transfers between devices: 101 us -> 61.6 us
  local copies, waits for them, and re-layouts: 29.7 us -> 13.2 us
  starting transfers between devices: 40.9 us -> 33.2 us
    all_gather x2 -> x0, blocking collectives: 62.9 us -> none  [inner_sums(): whole = lax.all_gather(sums, 'fsdp', axis=0, tiled=True)]
    all_to_all x1 -> x2, blocking collectives: 29.4 us -> 63.8 us  [gather(): lax.all_to_all(jnp.broadcast_to(x[None], (n,) + x.shape), axis, 0, 0, til...]
    all_to_all x1 -> x2, waiting for transfers between devices: 31.2 us -> 10.6 us  [gather(): lax.all_to_all(jnp.broadcast_to(x[None], (n,) + x.shape), axis, 0, 0, til...]
    all_to_all x6 -> x2, waiting for transfers between devices: 29.5 us -> 9.61 us  [scatter_sum(): lax.all_to_all(x.astype(BF).reshape(n, x.shape[0] // n, x.shape[1]), axis...]
    all_to_all x6 -> x2, starting transfers between devices: 25.6 us -> 9.74 us  [scatter_sum(): lax.all_to_all(x.astype(BF).reshape(n, x.shape[0] // n, x.shape[1]), axis...]
    all_to_all x1 -> x2, blocking collectives: 33.9 us -> 46.8 us  [scatter_sum(): lax.all_to_all(x.astype(BF).reshape(n, x.shape[0] // n, x.shape[1]), axis...]
    all_to_all x0 -> x1, blocking collectives: none -> 12.8 us  [per_device(): got = lax.all_to_all(got, 'fsdp', 0, 0, tiled=True)]
    optimization_barrier x2 -> x0, local copies, waits for them, and re-layouts: 7.97 us -> none  [inner_sums(): lax.optimization_barrier((scatter_sum(mine, 'fsdp', nf).astype(BF), raw))]
  transfers between devices with their start and end apart: 9 -> 7, of which waited for: 7 -> 5; matrix products, arithmetic and copies ran while one was open for 3% -> 3% of each run, Pallas kernels for 29% -> 34%
where the time goes in v5:
time: 505 us; the launch traced here: 503 us
  blocking collectives  189 us (37%)
  Pallas kernels  171 us (34%)
  waiting for transfers between devices  61.6 us (12%)
  starting transfers between devices  33.2 us (7%)
  matrix products  29.4 us (6%)
  local copies, waits for them, and re-layouts  13.2 us (3%)
    pallas_call x2, Pallas kernels, chol_inv(): pl.pallas_call(chol_kernel, out_shape=jax.ShapeDtypeStruct((n, n), F32),...  169 us
    all_to_all x2, blocking collectives, gather(): lax.all_to_all(jnp.broadcast_to(x[None], (n,) + x.shape), axis, 0, 0, til...  63.8 us
    all_to_all x2, blocking collectives, scatter_sum(): lax.all_to_all(x.astype(BF).reshape(n, x.shape[0] // n, x.shape[1]), axis...  46.8 us
    all_to_all x1, waiting for transfers between devices, per_device(): lax.all_to_all(sent, 'fsdp', 0, 0, tiled=True).reshape(cols, sent.shape[2])  35 us
    dot_general x21, matrix products, mm(): lax.dot_general(a, b, (((ca,), (cb,)), ((), ())), preferred_element_type=...  29.4 us
    all_gather x2, blocking collectives, per_device(): image = lax.all_gather(image, 'tp', axis=0, tiled=True)  26.4 us
    all_gather x1, blocking collectives, per_device(): gram = lax.all_gather(gram, 'tp', axis=0, tiled=True)  13.1 us
    all_gather x1, blocking collectives, per_device(): cross = lax.all_gather(both[:, rank:], 'tp', axis=0, tiled=True)  13.1 us
  transfers between devices with their start and end apart: 7, of which 5 were waited for; matrix products, arithmetic and copies ran while one was open for 3% of the time, Pallas kernels for 34%

profile of v5, /device:TPU:0, one launch (start us, length us, event | category | flops | bytes accessed | tf_op | source)
XLA Modules:
  0.0 503.3 jit_solution(9163937217038539086)
XLA Ops:
  2.2 2.3 convolution_convert_fusion.2
  4.4 33.9 %all_to_all.60 = bf16[16,120,512]{2,1,0:T(8,128)(2,1)S(1)} all-to-all(bf16[16,120,512]{2,1,0:T(8,128)(2,1)S(1)} %bitcast.69), channel_id=1, replica_groups=mesh['fsdp'=16,'tp'=8] {'fsdp'}, dimensions={0} | all-to-all | bytes 3932160 | tf_op jit(solution)/shard_map/all_to_all | solution.py:191
  38.8 29.4 %all_to_all.61 = bf16[16,120,512]{2,1,0:T(8,128)(2,1)S(1)} all-to-all(bf16[16,120,512]{2,1,0:T(8,128)(2,1)S(1)} %broadcast_in_dim.8), channel_id=1, replica_groups=mesh['fsdp'=16,'tp'=8] {'fsdp'}, dimensions={0} | all-to-all | bytes 3932160 | tf_op jit(solution)/shard_map/all_to_all | solution.py:196
  68.2 2.1 convolution_convert_fusion.4
  70.3 5.3 %all-to-all-start.2 = ((bf16[8,64,512]{2,1,0:T(8,128)(2,1)}), bf16[8,64,512]{2,1,0:T(8,128)(2,1)S(1)}, u32[]{:S(2)}, u32[]{:S(2)}) async-start(bf16[8,64,512]{2,1,0:T(8,128)(2,1)} %bitcast.3), calls=%async_computation.2 | async-start | bytes 1048576 | tf_op jit(solution)/shard_map/all_to_all | solution.py:191
  76.4 9.6 %all-to-all-done.2 = bf16[8,64,512]{2,1,0:T(8,128)(2,1)S(1)} async-done(((bf16[8,64,512]{2,1,0:T(8,128)(2,1)}), bf16[8,64,512]{2,1,0:T(8,128)(2,1)S(1)}, u32[]{:S(2)}, u32[]{:S(2)}) %all-to-all-start.2) | async-done | bytes 524320 | tf_op jit(solution)/shard_map/all_to_all | solution.py:191
  86.1 13.1 %all_gather.15 = bf16[512,512]{1,0:T(8,128)(2,1)S(1)} all-gather(bf16[64,512]{1,0:T(8,128)(2,1)S(1)} %reduce_sum.67), channel_id=1, replica_groups=mesh['fsdp'=16,'tp'=8] {'tp'}, dimensions={0}, use_global_device_ids=true | all-gather | bytes 589824 | tf_op jit(solution)/shard_map/all_gather | solution.py:261
  99.7 12.8 %all_to_all.62 = bf16[16,80,128]{2,1,0:T(8,128)(2,1)S(1)} all-to-all(bf16[16,80,128]{2,1,0:T(8,128)(2,1)S(1)} %fusion.20), channel_id=1, replica_groups=mesh['fsdp'=16,'tp'=8] {'fsdp'}, dimensions={0} | all-to-all | bytes 655360 | tf_op jit(solution)/shard_map/all_to_all | solution.py:265
  113.9 3.5 all-to-all-start.4
  117.4 2.5 fusion
  119.9 5.1 %all-to-all-done.4 = bf16[16,16,128]{2,1,0:T(8,128)(2,1)S(1)} async-done(((bf16[16,16,128]{2,1,0:T(8,128)(2,1)}), bf16[16,16,128]{2,1,0:T(8,128)(2,1)S(1)}, u32[]{:S(2)}, u32[]{:S(2)}) %all-to-all-start.4) | async-done | bytes 65568 | tf_op jit(solution)/shard_map/all_to_all | solution.py:196
  125.0 4.4 all-to-all-start.5
  129.4 13.1 %all_gather.16 = bf16[512,512]{1,0:T(8,128)(2,1)S(1)} all-gather(bf16[64,512]{1,0:T(8,128)(2,1)S(1)} %bitcast.75), channel_id=1, replica_groups=mesh['fsdp'=16,'tp'=8] {'tp'}, dimensions={0}, use_global_device_ids=true | all-gather | bytes 589824 | tf_op jit(solution)/shard_map/all_gather | solution.py:269
  142.7 85.5 %shard_map.92 = f32[512,512]{1,0:T(8,128)S(1)} custom-call(f32[512,512]{1,0:T(8,128)S(1)} %convert_multiply_fusion.1.a_ref), custom_call_target="tpu_custom_call" | custom-call | flops 1000000000 | bytes 2097152 | tf_op jit(solution)/shard_map/pallas_call | solution.py:163
  231.2 34.4 %all_to_all.63 = bf16[16,120,512]{2,1,0:T(8,128)(2,1)S(1)} all-to-all(bf16[16,120,512]{2,1,0:T(8,128)(2,1)S(1)} %broadcast_in_dim.10), channel_id=1, replica_groups=mesh['fsdp'=16,'tp'=8] {'fsdp'}, dimensions={0} | all-to-all | bytes 3932160 | tf_op jit(solution)/shard_map/all_to_all | solution.py:196
  266.8 12.9 %all_to_all.64 = bf16[8,64,512]{2,1,0:T(8,128)(2,1)S(1)} all-to-all(bf16[8,64,512]{2,1,0:T(8,128)(2,1)S(1)} %bitcast.71), channel_id=1, replica_groups=mesh['fsdp'=16,'tp'=8] {'tp'}, dimensions={0} | all-to-all | bytes 1048576 | tf_op jit(solution)/shard_map/all_to_all | solution.py:191
  280.5 13.3 %all_gather.17 = bf16[512,512]{1,0:T(8,128)(2,1)S(1)} all-gather(bf16[64,512]{1,0:T(8,128)(2,1)} %reduce_sum.70), channel_id=1, replica_groups=mesh['fsdp'=16,'tp'=8] {'tp'}, dimensions={0}, use_global_device_ids=true | all-gather | bytes 589824 | tf_op jit(solution)/shard_map/all_gather | solution.py:277
  296.4 4.2 all-to-all-start.8
  302.3 6.4 %all-to-all-done.8 = bf16[16,32,128]{2,1,0:T(8,128)(2,1)} async-done(((bf16[16,32,128]{2,1,0:T(8,128)(2,1)}), bf16[16,32,128]{2,1,0:T(8,128)(2,1)}, u32[]{:S(2)}, u32[]{:S(2)}) %all-to-all-start.8) | async-done | bytes 131104 | tf_op jit(solution)/shard_map/all_to_all | solution.py:280
  310.3 4.2 all-to-all-start.9
  314.5 2.5 fusion.1
  317.0 5.5 %all-to-all-done.9 = bf16[16,32,128]{2,1,0:T(8,128)(2,1)} async-done(((bf16[16,32,128]{2,1,0:T(8,128)(2,1)}), bf16[16,32,128]{2,1,0:T(8,128)(2,1)}, u32[]{:S(2)}, u32[]{:S(2)}) %all-to-all-start.9) | async-done | bytes 131104 | tf_op jit(solution)/shard_map/all_to_all | solution.py:196
  324.0 13.1 %all_gather.18 = bf16[512,512]{1,0:T(8,128)(2,1)S(1)} all-gather(bf16[64,512]{1,0:T(8,128)(2,1)S(1)} %get-tuple-element.18), channel_id=1, replica_groups=mesh['fsdp'=16,'tp'=8] {'tp'}, dimensions={0}, use_global_device_ids=true | all-gather | bytes 589824 | tf_op jit(solution)/shard_map/all_gather | solution.py:282
  337.1 4.6 all-to-all-start.10
  341.9 83.2 %shard_map.93 = f32[512,512]{1,0:T(8,128)S(1)} custom-call(f32[512,512]{1,0:T(8,128)S(1)} %convert_multiply_fusion.a_ref), custom_call_target="tpu_custom_call" | custom-call | flops 1000000000 | bytes 2097152 | tf_op jit(solution)/shard_map/pallas_call | solution.py:163
  425.1 13.1 %all_gather.19 = bf16[512,512]{1,0:T(8,128)(2,1)S(1)} all-gather(bf16[64,512]{1,0:T(8,128)(2,1)S(1)} %copy-done.15), channel_id=1, replica_groups=mesh['fsdp'=16,'tp'=8] {'tp'}, dimensions={0}, use_global_device_ids=true | all-gather | bytes 589824 | tf_op jit(solution)/shard_map/all_gather | solution.py:283
  444.6 2.6 shard_map.94
  448.7 6.9 %all-to-all-start.11 = ((bf16[16,120,640]{2,1,0:T(8,128)(2,1)}), bf16[16,120,640]{2,1,0:T(8,128)(2,1)}, u32[]{:S(2)}, u32[]{:S(2)}) async-start(bf16[16,120,640]{2,1,0:T(8,128)(2,1)} %copy-done.1), calls=%async_computation.11 | async-start | bytes 4915200 | tf_op jit(solution)/shard_map/all_to_all | solution.py:291
  459.5 35.0 %all-to-all-done.11 = bf16[16,120,640]{2,1,0:T(8,128)(2,1)} async-done(((bf16[16,120,640]{2,1,0:T(8,128)(2,1)}), bf16[16,120,640]{2,1,0:T(8,128)(2,1)}, u32[]{:S(2)}, u32[]{:S(2)}) %all-to-all-start.11) | async-done | bytes 2457632 | tf_op jit(solution)/shard_map/all_to_all | solution.py:291
  494.5 2.0 fusion.18
  496.5 2.1 fusion.16
  498.6 4.7 subtract_convert_fusion
  (76 shorter events, 28.9 us)
Async XLA Ops:
  0.6 1.6 copy-start
  68.2 7.4 %copy-start.16 = (f32[32,1920]{1,0:T(8,128)S(1)}, f32[32,1920]{1,0:T(8,128)}, u32[]{:S(2)}) copy-start(f32[32,1920]{1,0:T(8,128)} %param.9) | copy-start | bytes 737284
  68.2 7.4 %copy-start.17 = (f32[32,1920]{1,0:T(8,128)S(1)}, f32[32,1920]{1,0:T(8,128)}, u32[]{:S(2)}) copy-start(f32[32,1920]{1,0:T(8,128)} %param.8) | copy-start | bytes 737284
  70.3 15.7 %all-to-all-start.2 = ((bf16[8,64,512]{2,1,0:T(8,128)(2,1)}), bf16[8,64,512]{2,1,0:T(8,128)(2,1)S(1)}, u32[]{:S(2)}, u32[]{:S(2)}) async-start(bf16[8,64,512]{2,1,0:T(8,128)(2,1)} %bitcast.3), calls=%async_computation.2 | async-start | bytes 1048576 | tf_op jit(solution)/shard_map/all_to_all | solution.py:191
  99.2 20.7 %copy-start.7 = (bf16[512,512]{1,0:T(8,128)(2,1)}, bf16[512,512]{1,0:T(8,128)(2,1)S(1)}, u32[]{:S(2)}) copy-start(bf16[512,512]{1,0:T(8,128)(2,1)S(1)} %all_gather.15) | copy-start | bytes 1572868
  112.5 0.7 copy-start.11
  113.9 11.1 %all-to-all-start.4 = ((bf16[16,16,128]{2,1,0:T(8,128)(2,1)}), bf16[16,16,128]{2,1,0:T(8,128)(2,1)S(1)}, u32[]{:S(2)}, u32[]{:S(2)}) async-start(bf16[16,16,128]{2,1,0:T(8,128)(2,1)} %broadcast_in_dim.9), calls=%async_computation.4 | async-start | bytes 131072 | tf_op jit(solution)/shard_map/all_to_all | solution.py:196
  125.0 103.2 %all-to-all-start.5 = ((bf16[16,120,512]{2,1,0:T(8,128)(2,1)}), bf16[16,120,512]{2,1,0:T(8,128)(2,1)}, u32[]{:S(2)}, u32[]{:S(2)}) async-start(bf16[16,120,512]{2,1,0:T(8,128)(2,1)} %bitcast.66), calls=%async_computation.5 | async-start | bytes 3932160 | tf_op jit(solution)/shard_map/all_to_all | solution.py:191
  293.8 20.7 %copy-start.9 = (bf16[512,512]{1,0:T(8,128)(2,1)}, bf16[512,512]{1,0:T(8,128)(2,1)S(1)}, u32[]{:S(2)}) copy-start(bf16[512,512]{1,0:T(8,128)(2,1)S(1)} %all_gather.17) | copy-start | bytes 1572868
  296.4 12.3 %all-to-all-start.8 = ((bf16[16,32,128]{2,1,0:T(8,128)(2,1)}), bf16[16,32,128]{2,1,0:T(8,128)(2,1)}, u32[]{:S(2)}, u32[]{:S(2)}) async-start(bf16[16,32,128]{2,1,0:T(8,128)(2,1)} %bitcast.72), calls=%async_computation.8 | async-start | bytes 262144 | tf_op jit(solution)/shard_map/all_to_all | solution.py:280
  310.3 12.2 %all-to-all-start.9 = ((bf16[16,32,128]{2,1,0:T(8,128)(2,1)}), bf16[16,32,128]{2,1,0:T(8,128)(2,1)}, u32[]{:S(2)}, u32[]{:S(2)}) async-start(bf16[16,32,128]{2,1,0:T(8,128)(2,1)} %broadcast_in_dim.11), calls=%async_computation.9 | async-start | bytes 262144 | tf_op jit(solution)/shard_map/all_to_all | solution.py:196
  337.1 104.5 %all-to-all-start.10 = ((bf16[16,120,512]{2,1,0:T(8,128)(2,1)}), bf16[16,120,512]{2,1,0:T(8,128)(2,1)}, u32[]{:S(2)}, u32[]{:S(2)}) async-start(bf16[16,120,512]{2,1,0:T(8,128)(2,1)} %bitcast.65), calls=%async_computation.10 | async-start | bytes 3932160 | tf_op jit(solution)/shard_map/all_to_all | solution.py:289
  341.9 83.2 %copy-start.15 = (bf16[64,512]{1,0:T(8,128)(2,1)S(1)}, bf16[64,512]{1,0:T(8,128)(2,1)}, u32[]{:S(2)}) copy-start(bf16[64,512]{1,0:T(8,128)(2,1)} %get-tuple-element.17) | copy-start | bytes 196612
  438.3 1.0 copy-start.2
  438.8 0.9 copy-start.14
  438.8 1.8 copy-start.13
  441.6 1.0 copy-start.3
  442.7 0.9 copy-start.5
  443.6 0.9 copy-start.6
  447.2 1.5 copy-start.1
  448.7 45.8 %all-to-all-start.11 = ((bf16[16,120,640]{2,1,0:T(8,128)(2,1)}), bf16[16,120,640]{2,1,0:T(8,128)(2,1)}, u32[]{:S(2)}, u32[]{:S(2)}) async-start(bf16[16,120,640]{2,1,0:T(8,128)(2,1)} %copy-done.1), calls=%async_computation.11 | async-start | bytes 4915200 | tf_op jit(solution)/shard_map/all_to_all | solution.py:291
  455.6 1.6 copy-start.8
  457.2 1.3 copy-start.4
  457.2 1.3 copy-start.10
  459.5 43.8 %copy-start.12 = (bf16[512,512]{1,0:T(8,128)(2,1)}, bf16[512,512]{1,0:T(8,128)(2,1)S(1)}, u32[]{:S(2)}) copy-start(bf16[512,512]{1,0:T(8,128)(2,1)S(1)} %fusion.5) | copy-start | bytes 1572868

commit v6 on v5

--- a/solution.py
+++ b/solution.py
@@ -181,10 +181,8 @@
     return mm(a, hi, ca, cb) + mm(a, lo, ca, cb)
 
 
-def mm_split2(a, b, ca, cb):
-    hi = a.astype(BF)
-    lo = (a - hi.astype(F32)).astype(BF)
-    return mm_split(hi, b, ca, cb) + mm(lo, b.astype(BF), ca, cb)
+def mm_high(a, b, ca, cb):
+    return lax.dot_general(a, b, (((ca,), (cb,)), ((), ())), precision=lax.Precision.HIGH, preferred_element_type=F32)
 
 
 def scatter_sum(x, axis, n):
@@ -201,18 +199,12 @@
     return with_layout_constraint(x, Layout(tuple(range(x.ndim))))
 
 
-def chunks(x, nf, nt):
-    rows = x.shape[0] // nt
-    mine = lax.dynamic_slice_in_dim(x, lax.axis_index("tp") * rows, rows, 0).astype(BF)
-    return mine.reshape(rows // 8, 8, x.shape[1] // 128, 128).transpose(0, 2, 1, 3).reshape(nf, -1, 128)
-
-
-def unchunk(parts, nf, rows):
-    whole = gather(jnp.sum(parts.astype(F32), axis=0).astype(BF), "fsdp", nf)
-    return whole.reshape(rows // 8, -1, 8, 128).transpose(0, 2, 1, 3).reshape(rows, -1)
-
-
-def finish_kernel(scale, parts_ref, high_ref, low_ref, one_ref, two_ref, out_ref):
+def tiles(x):
+    n, rows, cols = x.shape
+    return x.reshape(n, rows // 8, 8, cols // 128, 128).transpose(0, 1, 3, 2, 4).reshape(n, -1, 128)
+
+
+def finish_kernel(scale, parts_ref, high_ref, low_ref, one_ref, two_ref, out_ref, back_ref):
     nf, rows, rank = parts_ref.shape
     share = rank // nf
     raw = parts_ref[0].astype(F32)
@@ -224,25 +216,46 @@
     one = BETA_ONE * one_ref[...] + (1.0 - BETA_ONE) * reduced
     two = BETA_TWO * two_ref[...] + (1.0 - BETA_TWO) * reduced * reduced
     direction = (one / (jnp.sqrt(two) + ADAM_EPS)).astype(BF)
-    fill = jnp.zeros((rows, out_ref.shape[2] - rank - 2 * share), F32)
+    pad = jnp.zeros((back_ref.shape[2] - rows, rank), F32)
+    one = jnp.concatenate([one, pad], axis=0).T
+    two = jnp.concatenate([two, pad], axis=0).T
     for g in range(nf):
-        out_ref[g, :, :rank] = direction
+        out_ref[g] = direction
         at = slice(g * share, (g + 1) * share)
-        out_ref[g, :, rank:] = jnp.concatenate([one[:, at], two[:, at], fill], axis=1).astype(BF)
+        back_ref[g, :share, :] = one[at].astype(BF)
+        back_ref[g, share:, :] = two[at].astype(BF)
 
 
 def finish(scale, parts, high, low, one, two):
     nf, rows, rank = parts.shape
-    width = rank + 2 * rank // nf
-    width += -width % 128
+    back = (nf, 2 * rank // nf, rows + -rows % 128)
     return pl.pallas_call(
         functools.partial(finish_kernel, scale),
-        out_shape=jax.ShapeDtypeStruct((nf, rows, width), BF),
+        out_shape=[jax.ShapeDtypeStruct(parts.shape, BF), jax.ShapeDtypeStruct(back, BF)],
         in_specs=[pl.BlockSpec(memory_space=pltpu.VMEM)] * 5,
-        out_specs=pl.BlockSpec(memory_space=pltpu.VMEM),
+        out_specs=[pl.BlockSpec(memory_space=pltpu.VMEM)] * 2,
         cost_estimate=pl.CostEstimate(flops=10**9, bytes_accessed=6 * 2**20, transcendentals=0),
         compiler_params=pltpu.CompilerParams(vmem_limit_bytes=32 * 2**20),
     )(parts, high, low, one, two)
+
+
+def unpack_kernel(width, got_ref, one_ref, two_ref):
+    share = one_ref.shape[0]
+    for ref, first in ((one_ref, 0), (two_ref, share)):
+        rows = [got_ref[g, first : first + share, :].astype(F32)[:, :width] for g in range(got_ref.shape[0])]
+        ref[...] = jnp.concatenate(rows, axis=1)
+
+
+def unpack(got, width):
+    nf, share, _ = got.shape
+    shape = jax.ShapeDtypeStruct((share // 2, nf * width), F32)
+    return pl.pallas_call(
+        functools.partial(unpack_kernel, width),
+        out_shape=[shape, shape],
+        in_specs=[pl.BlockSpec(memory_space=pltpu.VMEM)],
+        out_specs=[pl.BlockSpec(memory_space=pltpu.VMEM)] * 2,
+        cost_estimate=pl.CostEstimate(flops=10**6, bytes_accessed=2**20, transcendentals=0),
+    )(got)
 
 
 def per_device(nf, nt, grad, start_basis, weight, first_moment, second_moment):
@@ -259,41 +272,47 @@
     panel = gather(panel, "fsdp", nf)
     image = scatter_sum(mm(grad, panel, 1, 0), "tp", nt).astype(BF)
     image = lax.all_gather(image, "tp", axis=0, tiled=True)
-    raw = row_major(mm(grad, image, 0, 0).astype(BF))
+    raw = scatter_sum(row_major(mm(grad, image, 0, 0).astype(BF)), "fsdp", nf).astype(BF)
+
+    raw = gather(raw, "fsdp", nf)
     rows = rank // nt
-    got = jnp.concatenate([sent, chunks(mm(image, image, 0, 0), nf, nt)], axis=1)
+    few = rank // nf // nt
+    mine = lax.dynamic_slice_in_dim(mm(panel, raw, 0, 0), lax.axis_index("fsdp") * (rank // nf), rank // nf, 0)
+    mine = jnp.pad(mine.astype(BF).reshape(nt, few, rank), ((0, 0), (0, -few % 8), (0, 0)))
+    both = jnp.concatenate([mm(grad, raw, 1, 0).astype(BF).reshape(nt, rows, rank), mine], axis=1)
+    both = jnp.sum(lax.all_to_all(both, "tp", 0, 0, tiled=True).astype(F32), axis=0).astype(BF)
+    both = lax.all_gather(both, "tp", axis=0, tiled=False)
+    wide = both[:, :rows].reshape(-1, rank)
+    gram = both[:, rows : rows + few].reshape(1, rank // nf, rank)
+    outer = (mm(wide, wide, 0, 0) / M).astype(BF).reshape(nf, -1, rank)
+    raw = row_major(mm(grad, wide, 0, 0).astype(BF))
+    got = jnp.concatenate([sent, tiles(outer)], axis=1)
     got = lax.all_to_all(got, "fsdp", 0, 0, tiled=True)
     first_old = got[:, :share_rows].reshape(rank, -1)
     second_old = got[:, share_rows : 2 * share_rows].reshape(rank, -1)
-    gram, raw = lax.optimization_barrier((unchunk(got[:, 2 * share_rows :], nf, rows), raw))
-    gram = lax.all_gather(gram, "tp", axis=0, tiled=True)
-    inverse = chol_inv(gram.astype(F32) / M)
+    sums = jnp.sum(got[:, 2 * share_rows :].astype(F32), axis=0).astype(BF)
+    grams = gather(jnp.concatenate([sums, tiles(gram)[0]], axis=0), "fsdp", nf)
+    grams, raw = lax.optimization_barrier((grams, raw))
+    grams = grams.reshape(nf, 2, -1, rank // 128, 8, 128).transpose(1, 0, 2, 4, 3, 5).reshape(2, rank, rank)
+    outer, gram = grams[0].astype(F32), grams[1].astype(F32) / M
+    inverse = chol_inv(gram)
+    second = chol_inv(mm_high(mm_high(inverse, outer, 1, 0), inverse, 1, 1) / M)
+    both = mm_high(second, inverse, 1, 0)
+    margin = mm_high(gram, both, 0, 1)
     first_basis = mm_split(image, inverse, 1, 1).astype(BF)
-    raw = scatter_sum(raw, "fsdp", nf)
-    panel = (mm_split2(raw, inverse, 1, 1) * inv_sqrt).astype(BF)
-
-    panel = gather(panel, "fsdp", nf)
-    image = scatter_sum(mm(grad, panel, 1, 0), "tp", nt).astype(BF)
-    image = lax.all_gather(image, "tp", axis=0, tiled=True)
-    raw = row_major(mm(grad, image, 0, 0).astype(BF))
-    both = chunks(mm(image, jnp.concatenate([image, start_basis], axis=1), 0, 0), nf, nt)
-    both = unchunk(lax.all_to_all(both, "fsdp", 0, 0, tiled=True), nf, rows)
-    both, raw = lax.optimization_barrier((both, raw))
-    gram = lax.all_gather(both[:, :rank], "tp", axis=0, tiled=True)
-    cross = lax.all_gather(both[:, rank:], "tp", axis=0, tiled=True)
-    inverse = chol_inv(gram.astype(F32) / M)
-    margin = mm_split(cross, inverse, 0, 1) / M
-    new_basis = mm_split(image, inverse, 1, 1).astype(BF)
+    new_basis = (mm_split(wide, both, 1, 1) * inv_sqrt).astype(BF)
     rotated_one = mm(first_old, margin.astype(BF), 0, 0)[:share_cols]
     rotated_two = mm(second_old, (margin * margin).astype(BF), 0, 0)[:share_cols]
     parts = lax.all_to_all(raw.reshape(nf, share_cols, rank), "fsdp", 0, 0, tiled=True)
-    sent = finish(inv_sqrt, parts, *halves(inverse), rotated_one, rotated_two)
-    got = lax.all_to_all(sent, "fsdp", 0, 0, tiled=True).reshape(cols, sent.shape[2])
-    expanded = mm(new_basis, got[:, :rank], 1, 1)
+    rotated_one, rotated_two, first_basis, new_basis = lax.optimization_barrier(
+        (rotated_one, rotated_two, first_basis, new_basis)
+    )
+    direction, back = finish(1.0 / M, parts, *halves(both), rotated_one, rotated_two)
+    direction = lax.all_to_all(direction, "fsdp", 0, 0, tiled=True).reshape(cols, rank)
+    direction, back = lax.optimization_barrier((direction, back))
+    moment_one, moment_two = unpack(lax.all_to_all(back, "fsdp", 0, 0, tiled=True), share_cols)
+    expanded = mm(new_basis, direction, 1, 1)
     new_weight = (weight.astype(F32) - STEP_SIZE * inv_sqrt * expanded).astype(BF)
-    eye = jnp.eye(share_rows, dtype=BF)
-    moment_one = mm(eye, got[:, rank : rank + share_rows], 1, 1)
-    moment_two = mm(eye, got[:, rank + share_rows : rank + 2 * share_rows], 1, 1)
     return (first_basis, new_basis, moment_one, moment_two, new_weight)
 
 

time: 505 us -> 481 us (0.952)
  blocking collectives: 189 us -> 168 us
  starting transfers between devices: 33.2 us -> 23.4 us
  waiting for transfers between devices: 61.6 us -> 69.6 us
    all_to_all x2 -> x1, blocking collectives: 63.8 us -> 29.4 us  [gather(): lax.all_to_all(jnp.broadcast_to(x[None], (n,) + x.shape), axis, 0, 0, til...]
    all_to_all x2 -> x3, blocking collectives: 46.8 us -> 80.6 us  [scatter_sum(): lax.all_to_all(x.astype(BF).reshape(n, x.shape[0] // n, x.shape[1]), axis...]
    all_to_all x2, waiting for transfers between devices: 10.6 us -> 40.9 us  [gather(): lax.all_to_all(jnp.broadcast_to(x[None], (n,) + x.shape), axis, 0, 0, til...]
    all_gather x3 -> x1, blocking collectives: 39.3 us -> 13.3 us  [per_device(): both = lax.all_gather(both, 'tp', axis=0, tiled=False)]
    all_to_all x4 -> x3, waiting for transfers between devices: 51 us -> 28.7 us  [the longest x1 15.2 us: per_device(): got = lax.all_to_all(got, 'fsdp', 0, 0, tiled=True)]
    all_to_all x1, blocking collectives: 12.8 us -> 31.5 us  [per_device(): lax.all_to_all(direction, 'fsdp', 0, 0, tiled=True).reshape(cols, rank)]
    all_gather x2 -> x1, blocking collectives: 26.4 us -> 13.1 us  [per_device(): image = lax.all_gather(image, 'tp', axis=0, tiled=True)]
    all_to_all x4 -> x3, starting transfers between devices: 20.9 us -> 10.7 us  [the longest x1 3.61 us: per_device(): got = lax.all_to_all(got, 'fsdp', 0, 0, tiled=True)]
  transfers between devices with their start and end apart: 7 -> 6, of which waited for: 5 -> 5; matrix products, arithmetic and copies ran while one was open for 3% -> 4% of each run, Pallas kernels for 34% -> 35%
where the time goes in v6:
time: 481 us; the launch traced here: 480 us
  Pallas kernels  174 us (36%)
  blocking collectives  168 us (35%)
  waiting for transfers between devices  69.6 us (14%)
  matrix products  27.2 us (6%)
  starting transfers between devices  23.4 us (5%)
  local copies, waits for them, and re-layouts  11.5 us (2%)
  other arithmetic  5.47 us (1%)
    pallas_call x2, Pallas kernels, chol_inv(): pl.pallas_call(chol_kernel, out_shape=jax.ShapeDtypeStruct((n, n), F32),...  169 us
    all_to_all x3, blocking collectives, scatter_sum(): lax.all_to_all(x.astype(BF).reshape(n, x.shape[0] // n, x.shape[1]), axis...  80.6 us
    all_to_all x2, waiting for transfers between devices, gather(): lax.all_to_all(jnp.broadcast_to(x[None], (n,) + x.shape), axis, 0, 0, til...  40.9 us
    all_to_all x1, blocking collectives, per_device(): lax.all_to_all(direction, 'fsdp', 0, 0, tiled=True).reshape(cols, rank)  31.5 us
    all_to_all x1, blocking collectives, gather(): lax.all_to_all(jnp.broadcast_to(x[None], (n,) + x.shape), axis, 0, 0, til...  29.4 us
    dot_general x14, matrix products, mm(): lax.dot_general(a, b, (((ca,), (cb,)), ((), ())), preferred_element_type=...  22.6 us
    all_to_all x1, waiting for transfers between devices, per_device(): got = lax.all_to_all(got, 'fsdp', 0, 0, tiled=True)  15.2 us
    all_gather x1, blocking collectives, per_device(): both = lax.all_gather(both, 'tp', axis=0, tiled=False)  13.3 us
  transfers between devices with their start and end apart: 6, of which 5 were waited for; matrix products, arithmetic and copies ran while one was open for 4% of the time, Pallas kernels for 35%

profile of v6, /device:TPU:0, one launch (start us, length us, event | category | flops | bytes accessed | tf_op | source)
XLA Modules:
  0.0 480.0 jit_solution(6561381972099076400)
XLA Ops:
  0.6 1.5 copy-done
  2.2 2.3 convolution_convert_fusion.2
  4.4 33.9 %all_to_all.55 = bf16[16,120,512]{2,1,0:T(8,128)(2,1)S(1)} all-to-all(bf16[16,120,512]{2,1,0:T(8,128)(2,1)S(1)} %bitcast.87), channel_id=1, replica_groups=mesh['fsdp'=16,'tp'=8] {'fsdp'}, dimensions={0} | all-to-all | bytes 3932160 | tf_op jit(solution)/shard_map/all_to_all | solution.py:189
  38.8 29.4 %all_to_all.56 = bf16[16,120,512]{2,1,0:T(8,128)(2,1)S(1)} all-to-all(bf16[16,120,512]{2,1,0:T(8,128)(2,1)S(1)} %broadcast_in_dim.6), channel_id=1, replica_groups=mesh['fsdp'=16,'tp'=8] {'fsdp'}, dimensions={0} | all-to-all | bytes 3932160 | tf_op jit(solution)/shard_map/all_to_all | solution.py:194
  69.5 15.5 %all_to_all.57 = bf16[8,64,512]{2,1,0:T(8,128)(2,1)S(1)} all-to-all(bf16[8,64,512]{2,1,0:T(8,128)(2,1)S(1)} %bitcast.92), channel_id=1, replica_groups=mesh['fsdp'=16,'tp'=8] {'tp'}, dimensions={0} | all-to-all | bytes 1048576 | tf_op jit(solution)/shard_map/all_to_all | solution.py:189
  85.1 13.1 %all_gather.9 = bf16[512,512]{1,0:T(8,128)(2,1)S(1)} all-gather(bf16[64,512]{1,0:T(8,128)(2,1)S(1)} %reduce_sum.58), channel_id=1, replica_groups=mesh['fsdp'=16,'tp'=8] {'tp'}, dimensions={0}, use_global_device_ids=true | all-gather | bytes 589824 | tf_op jit(solution)/shard_map/all_gather | solution.py:274
  99.5 31.2 %all_to_all.58 = bf16[16,120,512]{2,1,0:T(8,128)(2,1)} all-to-all(bf16[16,120,512]{2,1,0:T(8,128)(2,1)S(1)} %bitcast.88), channel_id=1, replica_groups=mesh['fsdp'=16,'tp'=8] {'fsdp'}, dimensions={0} | all-to-all | bytes 3932160 | tf_op jit(solution)/shard_map/all_to_all | solution.py:189
  130.7 1.8 reduce_sum.59
  132.5 1.4 broadcast_in_dim.7
  133.9 4.4 all-to-all-start.4
  138.3 29.0 %all-to-all-done.4 = bf16[16,120,512]{2,1,0:T(8,128)(2,1)} async-done(((bf16[16,120,512]{2,1,0:T(8,128)(2,1)}), bf16[16,120,512]{2,1,0:T(8,128)(2,1)}, u32[]{:S(2)}, u32[]{:S(2)}) %all-to-all-start.4) | async-done | bytes 1966112 | tf_op jit(solution)/shard_map/all_to_all | solution.py:194
  167.3 3.4 convolution_bitcast_fusion.1
  170.8 2.8 convolution_convert_fusion.3
  174.5 3.5 all-to-all-start.5
  179.5 9.5 %all-to-all-done.5 = bf16[8,72,512]{2,1,0:T(8,128)(2,1)S(1)} async-done(((bf16[8,72,512]{2,1,0:T(8,128)(2,1)}), bf16[8,72,512]{2,1,0:T(8,128)(2,1)S(1)}, u32[]{:S(2)}, u32[]{:S(2)}) %all-to-all-start.5) | async-done | bytes 589856 | tf_op jit(solution)/shard_map/all_to_all | solution.py:283
  189.1 13.3 %all-gather = bf16[576,512]{1,0:T(8,128)(2,1)S(1)} all-gather(bf16[72,512]{1,0:T(8,128)(2,1)S(1)} %reduce_sum.60), channel_id=2, replica_groups=mesh['fsdp'=16,'tp'=8] {'tp'}, dimensions={0}, use_global_device_ids=true | all-gather | bytes 663552 | tf_op jit(solution)/shard_map/all_gather | solution.py:284
  203.9 3.6 all-to-all-start.6
  207.6 15.2 %all-to-all-done.6 = bf16[16,192,128]{2,1,0:T(8,128)(2,1)S(1)} async-done(((bf16[16,192,128]{2,1,0:T(8,128)(2,1)}), bf16[16,192,128]{2,1,0:T(8,128)(2,1)S(1)}, u32[]{:S(2)}, u32[]{:S(2)}) %all-to-all-start.6) | async-done | bytes 786464 | tf_op jit(solution)/shard_map/all_to_all | solution.py:290
  224.1 3.7 all-to-all-start.7
  228.8 2.5 fusion
  231.4 1.7 fusion.19
  233.0 11.9 %all-to-all-done.7 = bf16[16,256,128]{2,1,0:T(8,128)(2,1)S(1)} async-done(((bf16[16,256,128]{2,1,0:T(8,128)(2,1)}), bf16[16,256,128]{2,1,0:T(8,128)(2,1)S(1)}, u32[]{:S(2)}, u32[]{:S(2)}) %all-to-all-start.7) | async-done | bytes 1048608 | tf_op jit(solution)/shard_map/all_to_all | solution.py:194
  248.0 4.6 all-to-all-start.8
  252.6 85.3 %shard_map.92 = f32[512,512]{1,0:T(8,128)S(1)} custom-call(f32[512,512]{1,0:T(8,128)S(1)} %bitcast.73), custom_call_target="tpu_custom_call" | custom-call | flops 1000000000 | bytes 2097152 | tf_op jit(solution)/shard_map/pallas_call | solution.py:163
  339.7 83.4 %shard_map.93 = f32[512,512]{1,0:T(8,128)S(1)} custom-call(f32[512,512]{1,0:T(8,128)S(1)} %convolution_multiply_fusion.a_ref), custom_call_target="tpu_custom_call" | custom-call | flops 1000000000 | bytes 2097152 | tf_op jit(solution)/shard_map/pallas_call | solution.py:163
  424.2 1.9 fusion.21
  430.6 3.2 shard_map.94
  433.8 31.5 %all_to_all.59 = bf16[16,120,512]{2,1,0:T(8,128)(2,1)} all-to-all(bf16[16,120,512]{2,1,0:T(8,128)(2,1)S(1)} %get-tuple-element.23), channel_id=1, replica_groups=mesh['fsdp'=16,'tp'=8] {'fsdp'}, dimensions={0} | all-to-all | bytes 3932160 | tf_op jit(solution)/shard_map/all_to_all | solution.py:311
  465.3 3.5 all-to-all-start.10
  468.8 4.7 subtract_convert_fusion
  473.5 3.9 all-to-all-done.10.got_ref
  478.2 1.8 shard_map.95
  (73 shorter events, 20.3 us)
Async XLA Ops:
  0.6 1.6 copy-start
  68.2 1.3 copy-start.3
  98.2 1.2 copy-start.4
  133.9 33.4 %all-to-all-start.4 = ((bf16[16,120,512]{2,1,0:T(8,128)(2,1)}), bf16[16,120,512]{2,1,0:T(8,128)(2,1)}, u32[]{:S(2)}, u32[]{:S(2)}) async-start(bf16[16,120,512]{2,1,0:T(8,128)(2,1)} %broadcast_in_dim.7), calls=%async_computation.4 | async-start | bytes 3932160 | tf_op jit(solution)/shard_map/all_to_all | solution.py:194
  173.6 4.4 copy-start.17
  173.6 4.5 copy-start.18
  174.5 14.5 %all-to-all-start.5 = ((bf16[8,72,512]{2,1,0:T(8,128)(2,1)}), bf16[8,72,512]{2,1,0:T(8,128)(2,1)S(1)}, u32[]{:S(2)}, u32[]{:S(2)}) async-start(bf16[8,72,512]{2,1,0:T(8,128)(2,1)} %fusion.9), calls=%async_computation.5 | async-start | bytes 1179648 | tf_op jit(solution)/shard_map/all_to_all | solution.py:283
  189.1 13.8 %copy-start.13 = (bf16[64,16,120]{2,0,1:T(8,128)(2,1)S(1)}, bf16[64,16,120]{2,0,1:T(8,128)(2,1)}, u32[]{:S(2)}) copy-start(bf16[64,16,120]{2,0,1:T(8,128)(2,1)} %copy.13) | copy-start | bytes 737284
  202.4 5.1 %copy-start.10 = (bf16[576,512]{1,0:T(8,128)(2,1)}, bf16[576,512]{1,0:T(8,128)(2,1)S(1)}, u32[]{:S(2)}) copy-start(bf16[576,512]{1,0:T(8,128)(2,1)S(1)} %all-gather) | copy-start | bytes 1769476
  203.9 18.9 %all-to-all-start.6 = ((bf16[16,192,128]{2,1,0:T(8,128)(2,1)}), bf16[16,192,128]{2,1,0:T(8,128)(2,1)S(1)}, u32[]{:S(2)}, u32[]{:S(2)}) async-start(bf16[16,192,128]{2,1,0:T(8,128)(2,1)} %fusion.8), calls=%async_computation.6 | async-start | bytes 1572864 | tf_op jit(solution)/shard_map/all_to_all | solution.py:290
  222.8 1.3 copy-start.9
  224.1 20.9 %all-to-all-start.7 = ((bf16[16,256,128]{2,1,0:T(8,128)(2,1)}), bf16[16,256,128]{2,1,0:T(8,128)(2,1)S(1)}, u32[]{:S(2)}, u32[]{:S(2)}) async-start(bf16[16,256,128]{2,1,0:T(8,128)(2,1)} %broadcast_in_dim.8), calls=%async_computation.7 | async-start | bytes 2097152 | tf_op jit(solution)/shard_map/all_to_all | solution.py:194
  228.8 2.5 copy-start.6
  244.9 1.0 copy-start.8
  248.0 182.6 %all-to-all-start.8 = ((bf16[16,120,512]{2,1,0:T(8,128)(2,1)}), bf16[16,120,512]{2,1,0:T(8,128)(2,1)}, u32[]{:S(2)}, u32[]{:S(2)}) async-start(bf16[16,120,512]{2,1,0:T(8,128)(2,1)} %bitcast.85), calls=%async_computation.8 | async-start | bytes 3932160 | tf_op jit(solution)/shard_map/all_to_all | solution.py:306
  252.6 85.4 %copy-start.11 = (bf16[1,16,4,8,4,128]{5,3,4,2,0,1:T(8,128)(2,1)S(1)}, bf16[1,16,4,8,4,128]{5,3,4,2,0,1:T(8,128)(2,1)}, u32[]{:S(2)}) copy-start(bf16[1,16,4,8,4,128]{5,3,4,2,0,1:T(8,128)(2,1)} %slice.46) | copy-start | bytes 1572868
  424.1 2.5 copy-start.1
  424.1 1.9 copy-start.16
  424.1 2.2 copy-start.15
  426.0 1.0 copy-start.7
  426.3 1.2 copy-start.5
  429.3 1.3 copy-start.2
  433.8 35.1 %copy-start.14 = (bf16[512,512]{1,0:T(8,128)(2,1)S(1)}, bf16[512,512]{1,0:T(8,128)(2,1)}, u32[]{:S(2)}) copy-start(bf16[512,512]{1,0:T(8,128)(2,1)} %fusion.4) | copy-start | bytes 1572868
  465.3 12.2 %all-to-all-start.10 = ((bf16[16,64,128]{2,1,0:T(8,128)(2,1)}), bf16[16,64,128]{2,1,0:T(8,128)(2,1)S(1)}, u32[]{:S(2)}, u32[]{:S(2)}) async-start(bf16[16,64,128]{2,1,0:T(8,128)(2,1)} %get-tuple-element.25), calls=%async_computation.10 | async-start | bytes 524288 | tf_op jit(solution)/shard_map/all_to_all | solution.py:313
  477.5 0.7 copy-start.12

commit v7 on v6

--- a/solution.py
+++ b/solution.py
@@ -271,7 +271,12 @@
     panel = (scatter_sum(mm(grad, start_basis, 0, 0), "fsdp", nf) * inv_sqrt).astype(BF)
     panel = gather(panel, "fsdp", nf)
     image = scatter_sum(mm(grad, panel, 1, 0), "tp", nt).astype(BF)
+    image, sent = lax.optimization_barrier((image, sent))
     image = lax.all_gather(image, "tp", axis=0, tiled=True)
+    got = lax.all_to_all(sent, "fsdp", 0, 0, tiled=True)
+    image, got = lax.optimization_barrier((image, got))
+    first_old = got[:, :share_rows].reshape(rank, -1)
+    second_old = got[:, share_rows:].reshape(rank, -1)
     raw = scatter_sum(row_major(mm(grad, image, 0, 0).astype(BF)), "fsdp", nf).astype(BF)
 
     raw = gather(raw, "fsdp", nf)
@@ -281,16 +286,14 @@
     mine = jnp.pad(mine.astype(BF).reshape(nt, few, rank), ((0, 0), (0, -few % 8), (0, 0)))
     both = jnp.concatenate([mm(grad, raw, 1, 0).astype(BF).reshape(nt, rows, rank), mine], axis=1)
     both = jnp.sum(lax.all_to_all(both, "tp", 0, 0, tiled=True).astype(F32), axis=0).astype(BF)
+    outer = (mm(both[:rows], both[:rows], 0, 0) / M).astype(BF).reshape(nf, -1, rank)
+    outer = lax.all_to_all(tiles(outer), "fsdp", 0, 0, tiled=True)
     both = lax.all_gather(both, "tp", axis=0, tiled=False)
     wide = both[:, :rows].reshape(-1, rank)
     gram = both[:, rows : rows + few].reshape(1, rank // nf, rank)
-    outer = (mm(wide, wide, 0, 0) / M).astype(BF).reshape(nf, -1, rank)
     raw = row_major(mm(grad, wide, 0, 0).astype(BF))
-    got = jnp.concatenate([sent, tiles(outer)], axis=1)
-    got = lax.all_to_all(got, "fsdp", 0, 0, tiled=True)
-    first_old = got[:, :share_rows].reshape(rank, -1)
-    second_old = got[:, share_rows : 2 * share_rows].reshape(rank, -1)
-    sums = jnp.sum(got[:, 2 * share_rows :].astype(F32), axis=0).astype(BF)
+    sums = jnp.sum(outer.astype(F32), axis=0).astype(BF)
+    sums = jnp.sum(lax.all_gather(sums, "tp", axis=0, tiled=False).astype(F32), axis=0).astype(BF)
     grams = gather(jnp.concatenate([sums, tiles(gram)[0]], axis=0), "fsdp", nf)
     grams, raw = lax.optimization_barrier((grams, raw))
     grams = grams.reshape(nf, 2, -1, rank // 128, 8, 128).transpose(1, 0, 2, 4, 3, 5).reshape(2, rank, rank)

time: 481 us -> 491 us (1.021)
  blocking collectives: 168 us -> 184 us
  waiting for transfers between devices: 69.6 us -> 54.4 us
  starting transfers between devices: 23.4 us -> 32.1 us
    all_to_all x2 -> x3, waiting for transfers between devices: 24.7 us -> 8.84 us  [the longest x1 8.84 us: scatter_sum(): lax.all_to_all(x.astype(BF).reshape(n, x.shape[0] // n, x.shape[1]), axis...]
    all_to_all x0 -> x1, blocking collectives: none -> 13.6 us  [per_device(): lax.all_to_all(both, 'tp', 0, 0, tiled=True).astype(F32)]
    all_gather x0 -> x1, blocking collectives: none -> 12.8 us  [per_device(): lax.all_gather(sums, 'tp', axis=0, tiled=False).astype(F32)]
    all_to_all x3 -> x2, blocking collectives: 80.6 us -> 68.4 us  [scatter_sum(): lax.all_to_all(x.astype(BF).reshape(n, x.shape[0] // n, x.shape[1]), axis...]
    all_to_all x2 -> x3, starting transfers between devices: 7.15 us -> 12.4 us  [the longest x1 5.31 us: scatter_sum(): lax.all_to_all(x.astype(BF).reshape(n, x.shape[0] // n, x.shape[1]), axis...]
  transfers between devices with their start and end apart: 6 -> 7, of which waited for: 5 -> 4; matrix products, arithmetic and copies ran while one was open for 4% -> 4% of each run, Pallas kernels for 35% -> 34%
where the time goes in v7:
time: 491 us; the launch traced here: 490 us
  blocking collectives  184 us (37%)
  Pallas kernels  174 us (35%)
  waiting for transfers between devices  54.4 us (11%)
  starting transfers between devices  32.1 us (7%)
  matrix products  28.6 us (6%)
  local copies, waits for them, and re-layouts  12.2 us (2%)
    pallas_call x2, Pallas kernels, chol_inv(): pl.pallas_call(chol_kernel, out_shape=jax.ShapeDtypeStruct((n, n), F32),...  169 us
    all_to_all x2, blocking collectives, scatter_sum(): lax.all_to_all(x.astype(BF).reshape(n, x.shape[0] // n, x.shape[1]), axis...  68.4 us
    all_to_all x2, waiting for transfers between devices, gather(): lax.all_to_all(jnp.broadcast_to(x[None], (n,) + x.shape), axis, 0, 0, til...  41.6 us
    all_to_all x1, blocking collectives, per_device(): lax.all_to_all(direction, 'fsdp', 0, 0, tiled=True).reshape(cols, rank)  33.2 us
    all_to_all x1, blocking collectives, gather(): lax.all_to_all(jnp.broadcast_to(x[None], (n,) + x.shape), axis, 0, 0, til...  29.4 us
    dot_general x14, matrix products, mm(): lax.dot_general(a, b, (((ca,), (cb,)), ((), ())), preferred_element_type=...  24 us
    all_to_all x1, blocking collectives, per_device(): lax.all_to_all(both, 'tp', 0, 0, tiled=True).astype(F32)  13.6 us
    all_gather x1, blocking collectives, per_device(): both = lax.all_gather(both, 'tp', axis=0, tiled=False)  13.2 us
  transfers between devices with their start and end apart: 7, of which 4 were waited for; matrix products, arithmetic and copies ran while one was open for 4% of the time, Pallas kernels for 34%

profile of v7, /device:TPU:0, one launch (start us, length us, event | category | flops | bytes accessed | tf_op | source)
XLA Modules:
  0.0 489.7 jit_solution(8727319076964208189)
XLA Ops:
  0.6 1.5 copy-done
  2.2 2.3 convolution_convert_fusion.2
  4.4 33.9 %all_to_all.60 = bf16[16,120,512]{2,1,0:T(8,128)(2,1)S(1)} all-to-all(bf16[16,120,512]{2,1,0:T(8,128)(2,1)S(1)} %bitcast.80), channel_id=1, replica_groups=mesh['fsdp'=16,'tp'=8] {'fsdp'}, dimensions={0} | all-to-all | bytes 3932160 | tf_op jit(solution)/shard_map/all_to_all | solution.py:189
  38.8 29.4 %all_to_all.61 = bf16[16,120,512]{2,1,0:T(8,128)(2,1)S(1)} all-to-all(bf16[16,120,512]{2,1,0:T(8,128)(2,1)S(1)} %broadcast_in_dim.6), channel_id=1, replica_groups=mesh['fsdp'=16,'tp'=8] {'fsdp'}, dimensions={0} | all-to-all | bytes 3932160 | tf_op jit(solution)/shard_map/all_to_all | solution.py:194
  68.2 2.1 convolution_convert_fusion.4
  70.3 5.3 %all-to-all-start.2 = ((bf16[8,64,512]{2,1,0:T(8,128)(2,1)}), bf16[8,64,512]{2,1,0:T(8,128)(2,1)S(1)}, u32[]{:S(2)}, u32[]{:S(2)}) async-start(bf16[8,64,512]{2,1,0:T(8,128)(2,1)} %bitcast.3), calls=%async_computation.2 | async-start | bytes 1048576 | tf_op jit(solution)/shard_map/all_to_all | solution.py:189
  77.1 8.8 %all-to-all-done.2 = bf16[8,64,512]{2,1,0:T(8,128)(2,1)S(1)} async-done(((bf16[8,64,512]{2,1,0:T(8,128)(2,1)}), bf16[8,64,512]{2,1,0:T(8,128)(2,1)S(1)}, u32[]{:S(2)}, u32[]{:S(2)}) %all-to-all-start.2) | async-done | bytes 524320 | tf_op jit(solution)/shard_map/all_to_all | solution.py:189
  86.1 3.5 all-to-all-start.3
  89.6 13.1 %all_gather.15 = bf16[512,512]{1,0:T(8,128)(2,1)S(1)} all-gather(bf16[64,512]{1,0:T(8,128)(2,1)S(1)} %reduce_sum.70), channel_id=1, replica_groups=mesh['fsdp'=16,'tp'=8] {'tp'}, dimensions={0}, use_global_device_ids=true | all-gather | bytes 589824 | tf_op jit(solution)/shard_map/all_gather | solution.py:275
  104.0 34.5 %all_to_all.62 = bf16[16,120,512]{2,1,0:T(8,128)(2,1)} all-to-all(bf16[16,120,512]{2,1,0:T(8,128)(2,1)S(1)} %bitcast.81), channel_id=1, replica_groups=mesh['fsdp'=16,'tp'=8] {'fsdp'}, dimensions={0} | all-to-all | bytes 3932160 | tf_op jit(solution)/shard_map/all_to_all | solution.py:189
  138.5 1.8 reduce_sum.71
  141.7 4.4 all-to-all-start.5
  146.2 28.5 %all-to-all-done.5 = bf16[16,120,512]{2,1,0:T(8,128)(2,1)} async-done(((bf16[16,120,512]{2,1,0:T(8,128)(2,1)}), bf16[16,120,512]{2,1,0:T(8,128)(2,1)}, u32[]{:S(2)}, u32[]{:S(2)}) %all-to-all-start.5) | async-done | bytes 1966112 | tf_op jit(solution)/shard_map/all_to_all | solution.py:194
  174.7 3.4 convolution_bitcast_fusion
  178.2 2.8 convolution_convert_fusion.3
  181.0 13.6 %all_to_all.63 = bf16[8,72,512]{2,1,0:T(8,128)(2,1)S(1)} all-to-all(bf16[8,72,512]{2,1,0:T(8,128)(2,1)S(1)} %fusion.6), channel_id=1, replica_groups=mesh['fsdp'=16,'tp'=8] {'tp'}, dimensions={0} | all-to-all | bytes 1179648 | tf_op jit(solution)/shard_map/all_to_all | solution.py:288
  195.8 3.6 all-to-all-start.7
  199.4 13.2 %all-gather.1 = bf16[576,512]{1,0:T(8,128)(2,1)S(1)} all-gather(bf16[72,512]{1,0:T(8,128)(2,1)S(1)} %reduce_sum.72), channel_id=3, replica_groups=mesh['fsdp'=16,'tp'=8] {'tp'}, dimensions={0}, use_global_device_ids=true | all-gather | bytes 663552 | tf_op jit(solution)/shard_map/all_gather | solution.py:291
  213.6 12.8 %all-gather = bf16[1024,128]{1,0:T(8,128)(2,1)S(1)} all-gather(bf16[128,128]{1,0:T(8,128)(2,1)S(1)} %reduce_sum.73), channel_id=2, replica_groups=mesh['fsdp'=16,'tp'=8] {'tp'}, dimensions={0}, use_global_device_ids=true | all-gather | bytes 294912 | tf_op jit(solution)/shard_map/all_gather | solution.py:296
  227.7 7.1 %all-to-all-start.8 = ((bf16[16,256,128]{2,1,0:T(8,128)(2,1)}), bf16[16,256,128]{2,1,0:T(8,128)(2,1)S(1)}, u32[]{:S(2)}, u32[]{:S(2)}) async-start(bf16[16,256,128]{2,1,0:T(8,128)(2,1)} %broadcast_in_dim.8), calls=%async_computation.8 | async-start | bytes 2097152 | tf_op jit(solution)/shard_map/all_to_all | solution.py:194
  237.4 2.5 fusion
  239.9 13.0 %all-to-all-done.8 = bf16[16,256,128]{2,1,0:T(8,128)(2,1)S(1)} async-done(((bf16[16,256,128]{2,1,0:T(8,128)(2,1)}), bf16[16,256,128]{2,1,0:T(8,128)(2,1)S(1)}, u32[]{:S(2)}, u32[]{:S(2)}) %all-to-all-start.8) | async-done | bytes 1048608 | tf_op jit(solution)/shard_map/all_to_all | solution.py:194
  256.0 4.6 all-to-all-start.9
  260.6 85.3 %shard_map.92 = f32[512,512]{1,0:T(8,128)S(1)} custom-call(f32[512,512]{1,0:T(8,128)S(1)} %bitcast.67), custom_call_target="tpu_custom_call" | custom-call | flops 1000000000 | bytes 2097152 | tf_op jit(solution)/shard_map/pallas_call | solution.py:163
  347.7 83.4 %shard_map.93 = f32[512,512]{1,0:T(8,128)S(1)} custom-call(f32[512,512]{1,0:T(8,128)S(1)} %convolution_multiply_fusion.a_ref), custom_call_target="tpu_custom_call" | custom-call | flops 1000000000 | bytes 2097152 | tf_op jit(solution)/shard_map/pallas_call | solution.py:163
  432.2 1.9 fusion.18
  438.6 3.2 shard_map.94
  441.8 33.2 %all_to_all.64 = bf16[16,120,512]{2,1,0:T(8,128)(2,1)} all-to-all(bf16[16,120,512]{2,1,0:T(8,128)(2,1)S(1)} %get-tuple-element.31), channel_id=1, replica_groups=mesh['fsdp'=16,'tp'=8] {'fsdp'}, dimensions={0} | all-to-all | bytes 3932160 | tf_op jit(solution)/shard_map/all_to_all | solution.py:314
  474.9 3.5 all-to-all-start.11
  478.5 4.7 subtract_convert_fusion
  483.2 3.9 all-to-all-done.11.got_ref
  487.8 1.8 shard_map.95
  (73 shorter events, 21.6 us)
Async XLA Ops:
  0.6 1.6 copy-start
  68.2 2.1 copy-start.3
  68.2 7.4 %copy-start.15 = (f32[32,1920]{1,0:T(8,128)S(1)}, f32[32,1920]{1,0:T(8,128)}, u32[]{:S(2)}) copy-start(f32[32,1920]{1,0:T(8,128)} %param.8) | copy-start | bytes 737284
  68.2 7.4 %copy-start.16 = (f32[32,1920]{1,0:T(8,128)S(1)}, f32[32,1920]{1,0:T(8,128)}, u32[]{:S(2)}) copy-start(f32[32,1920]{1,0:T(8,128)} %param.9) | copy-start | bytes 737284
  70.3 15.7 %all-to-all-start.2 = ((bf16[8,64,512]{2,1,0:T(8,128)(2,1)}), bf16[8,64,512]{2,1,0:T(8,128)(2,1)S(1)}, u32[]{:S(2)}, u32[]{:S(2)}) async-start(bf16[8,64,512]{2,1,0:T(8,128)(2,1)} %bitcast.3), calls=%async_computation.2 | async-start | bytes 1048576 | tf_op jit(solution)/shard_map/all_to_all | solution.py:189
  86.1 16.7 %all-to-all-start.3 = ((bf16[16,64,128]{2,1,0:T(8,128)(2,1)}), bf16[16,64,128]{2,1,0:T(8,128)(2,1)S(1)}, u32[]{:S(2)}, u32[]{:S(2)}) async-start(bf16[16,64,128]{2,1,0:T(8,128)(2,1)} %pad.8), calls=%async_computation.3 | async-start | bytes 524288 | tf_op jit(solution)/shard_map/all_to_all | solution.py:276
  102.7 1.2 copy-start.4
  141.7 33.0 %all-to-all-start.5 = ((bf16[16,120,512]{2,1,0:T(8,128)(2,1)}), bf16[16,120,512]{2,1,0:T(8,128)(2,1)}, u32[]{:S(2)}, u32[]{:S(2)}) async-start(bf16[16,120,512]{2,1,0:T(8,128)(2,1)} %broadcast_in_dim.7), calls=%async_computation.5 | async-start | bytes 3932160 | tf_op jit(solution)/shard_map/all_to_all | solution.py:194
  195.8 17.6 %all-to-all-start.7 = ((bf16[16,128,128]{2,1,0:T(8,128)(2,1)}), bf16[16,128,128]{2,1,0:T(8,128)(2,1)S(1)}, u32[]{:S(2)}, u32[]{:S(2)}) async-start(bf16[16,128,128]{2,1,0:T(8,128)(2,1)} %bitcast.14), calls=%async_computation.7 | async-start | bytes 1048576 | tf_op jit(solution)/shard_map/all_to_all | solution.py:290
  212.6 0.8 copy-start.9
  227.7 25.3 %all-to-all-start.8 = ((bf16[16,256,128]{2,1,0:T(8,128)(2,1)}), bf16[16,256,128]{2,1,0:T(8,128)(2,1)S(1)}, u32[]{:S(2)}, u32[]{:S(2)}) async-start(bf16[16,256,128]{2,1,0:T(8,128)(2,1)} %broadcast_in_dim.8), calls=%async_computation.8 | async-start | bytes 2097152 | tf_op jit(solution)/shard_map/all_to_all | solution.py:194
  236.6 0.8 copy-start.6
  253.0 1.0 copy-start.8
  256.0 182.6 %all-to-all-start.9 = ((bf16[16,120,512]{2,1,0:T(8,128)(2,1)}), bf16[16,120,512]{2,1,0:T(8,128)(2,1)}, u32[]{:S(2)}, u32[]{:S(2)}) async-start(bf16[16,120,512]{2,1,0:T(8,128)(2,1)} %bitcast.78), calls=%async_computation.9 | async-start | bytes 3932160 | tf_op jit(solution)/shard_map/all_to_all | solution.py:309
  260.6 85.4 %copy-start.10 = (bf16[1,16,4,8,4,128]{5,3,4,2,0,1:T(8,128)(2,1)S(1)}, bf16[1,16,4,8,4,128]{5,3,4,2,0,1:T(8,128)(2,1)}, u32[]{:S(2)}) copy-start(bf16[1,16,4,8,4,128]{5,3,4,2,0,1:T(8,128)(2,1)} %slice.46) | copy-start | bytes 1572868
  432.1 2.5 copy-start.1
  432.1 1.9 copy-start.14
  432.2 2.2 copy-start.13
  434.0 1.0 copy-start.7
  434.3 1.2 copy-start.5
  437.3 1.3 copy-start.2
  441.8 36.7 %copy-start.12 = (bf16[512,512]{1,0:T(8,128)(2,1)S(1)}, bf16[512,512]{1,0:T(8,128)(2,1)}, u32[]{:S(2)}) copy-start(bf16[512,512]{1,0:T(8,128)(2,1)} %fusion.3) | copy-start | bytes 1572868
  474.9 12.2 %all-to-all-start.11 = ((bf16[16,64,128]{2,1,0:T(8,128)(2,1)}), bf16[16,64,128]{2,1,0:T(8,128)(2,1)S(1)}, u32[]{:S(2)}, u32[]{:S(2)}) async-start(bf16[16,64,128]{2,1,0:T(8,128)(2,1)} %get-tuple-element.33), calls=%async_computation.11 | async-start | bytes 524288 | tf_op jit(solution)/shard_map/all_to_all | solution.py:316
  487.1 0.7 copy-start.11

commit v8 on v6

--- a/solution.py
+++ b/solution.py
@@ -166,7 +166,7 @@
         in_specs=[pl.BlockSpec(memory_space=pltpu.VMEM)],
         out_specs=pl.BlockSpec(memory_space=pltpu.VMEM),
         scratch_shapes=[pltpu.VMEM((NB, NB), F32), square(F32), square(F32), square(BF), square(BF), square(BF), square(BF), square(BF), pltpu.VMEM((1, n), F32)],
-        cost_estimate=pl.CostEstimate(flops=10**9, bytes_accessed=2 * 2**20, transcendentals=0),
+        cost_estimate=pl.CostEstimate(flops=10**6, bytes_accessed=2**10, transcendentals=0),
         compiler_params=pltpu.CompilerParams(vmem_limit_bytes=32 * 2**20),
     )(a)
 
@@ -268,7 +268,9 @@
     sent = sent.reshape(2 * share_rows, nf, share_cols).transpose(1, 0, 2)
     sent = row_major(jnp.pad(sent, ((0, 0), (0, 0), (0, -share_cols % 128))))
 
-    panel = (scatter_sum(mm(grad, start_basis, 0, 0), "fsdp", nf) * inv_sqrt).astype(BF)
+    first_row = (lax.axis_index("fsdp") * (rank // nf)).astype(jnp.uint32)
+    panel, first_row = lax.optimization_barrier((mm(grad, start_basis, 0, 0).astype(BF), first_row))
+    panel = (scatter_sum(panel, "fsdp", nf) * inv_sqrt).astype(BF)
     panel = gather(panel, "fsdp", nf)
     image = scatter_sum(mm(grad, panel, 1, 0), "tp", nt).astype(BF)
     image = lax.all_gather(image, "tp", axis=0, tiled=True)
@@ -277,7 +279,7 @@
     raw = gather(raw, "fsdp", nf)
     rows = rank // nt
     few = rank // nf // nt
-    mine = lax.dynamic_slice_in_dim(mm(panel, raw, 0, 0), lax.axis_index("fsdp") * (rank // nf), rank // nf, 0)
+    mine = lax.dynamic_slice(mm(panel, raw, 0, 0), (first_row, jnp.uint32(0)), (rank // nf, rank))
     mine = jnp.pad(mine.astype(BF).reshape(nt, few, rank), ((0, 0), (0, -few % 8), (0, 0)))
     both = jnp.concatenate([mm(grad, raw, 1, 0).astype(BF).reshape(nt, rows, rank), mine], axis=1)
     both = jnp.sum(lax.all_to_all(both, "tp", 0, 0, tiled=True).astype(F32), axis=0).astype(BF)

time: 481 us -> 474 us (0.985)
  blocking collectives: 168 us -> 198 us
  waiting for transfers between devices: 69.6 us -> 40.5 us
    all_to_all x1 -> x2, blocking collectives: 29.4 us -> 59 us  [gather(): lax.all_to_all(jnp.broadcast_to(x[None], (n,) + x.shape), axis, 0, 0, til...]
    all_to_all x2 -> x1, waiting for transfers between devices: 40.9 us -> 11.9 us  [gather(): lax.all_to_all(jnp.broadcast_to(x[None], (n,) + x.shape), axis, 0, 0, til...]
  transfers between devices with their start and end apart: 6 -> 5, of which waited for: 5 -> 4; matrix products, arithmetic and copies ran while one was open for 4% -> 4% of each run, Pallas kernels for 35% -> 36%
where the time goes in v8:
time: 474 us; the launch traced here: 473 us
  blocking collectives  198 us (42%)
  Pallas kernels  174 us (37%)
  waiting for transfers between devices  40.5 us (9%)
  matrix products  25.1 us (5%)
  starting transfers between devices  19 us (4%)
  local copies, waits for them, and re-layouts  10.3 us (2%)
  other arithmetic  5.47 us (1%)
    pallas_call x2, Pallas kernels, chol_inv(): pl.pallas_call(chol_kernel, out_shape=jax.ShapeDtypeStruct((n, n), F32),...  169 us
    all_to_all x3, blocking collectives, scatter_sum(): lax.all_to_all(x.astype(BF).reshape(n, x.shape[0] // n, x.shape[1]), axis...  80.6 us
    all_to_all x2, blocking collectives, gather(): lax.all_to_all(jnp.broadcast_to(x[None], (n,) + x.shape), axis, 0, 0, til...  59 us
    all_to_all x1, blocking collectives, per_device(): lax.all_to_all(direction, 'fsdp', 0, 0, tiled=True).reshape(cols, rank)  31.5 us
    dot_general x14, matrix products, mm(): lax.dot_general(a, b, (((ca,), (cb,)), ((), ())), preferred_element_type=...  20.4 us
    all_to_all x1, waiting for transfers between devices, per_device(): got = lax.all_to_all(got, 'fsdp', 0, 0, tiled=True)  15.2 us
    all_gather x1, blocking collectives, per_device(): both = lax.all_gather(both, 'tp', axis=0, tiled=False)  13.3 us
    all_gather x1, blocking collectives, per_device(): image = lax.all_gather(image, 'tp', axis=0, tiled=True)  13.1 us
  transfers between devices with their start and end apart: 5, of which 4 were waited for; matrix products, arithmetic and copies ran while one was open for 4% of the time, Pallas kernels for 36%

profile of v8, /device:TPU:0, one launch (start us, length us, event | category | flops | bytes accessed | tf_op | source)
XLA Modules:
  0.0 472.7 jit_solution(665268781118823414)
XLA Ops:
  0.7 1.5 copy-done
  2.2 2.3 convolution_convert_fusion.2
  4.4 33.9 %all_to_all.55 = bf16[16,120,512]{2,1,0:T(8,128)(2,1)S(1)} all-to-all(bf16[16,120,512]{2,1,0:T(8,128)(2,1)S(1)} %bitcast.88), channel_id=1, replica_groups=mesh['fsdp'=16,'tp'=8] {'fsdp'}, dimensions={0} | all-to-all | bytes 3932160 | tf_op jit(solution)/shard_map/all_to_all | solution.py:189
  38.8 29.4 %all_to_all.56 = bf16[16,120,512]{2,1,0:T(8,128)(2,1)S(1)} all-to-all(bf16[16,120,512]{2,1,0:T(8,128)(2,1)S(1)} %broadcast_in_dim.6), channel_id=1, replica_groups=mesh['fsdp'=16,'tp'=8] {'fsdp'}, dimensions={0} | all-to-all | bytes 3932160 | tf_op jit(solution)/shard_map/all_to_all | solution.py:194
  69.5 15.5 %all_to_all.57 = bf16[8,64,512]{2,1,0:T(8,128)(2,1)S(1)} all-to-all(bf16[8,64,512]{2,1,0:T(8,128)(2,1)S(1)} %bitcast.93), channel_id=1, replica_groups=mesh['fsdp'=16,'tp'=8] {'tp'}, dimensions={0} | all-to-all | bytes 1048576 | tf_op jit(solution)/shard_map/all_to_all | solution.py:189
  85.1 13.1 %all_gather.9 = bf16[512,512]{1,0:T(8,128)(2,1)S(1)} all-gather(bf16[64,512]{1,0:T(8,128)(2,1)S(1)} %reduce_sum.58), channel_id=1, replica_groups=mesh['fsdp'=16,'tp'=8] {'tp'}, dimensions={0}, use_global_device_ids=true | all-gather | bytes 589824 | tf_op jit(solution)/shard_map/all_gather | solution.py:276
  99.5 31.2 %all_to_all.58 = bf16[16,120,512]{2,1,0:T(8,128)(2,1)} all-to-all(bf16[16,120,512]{2,1,0:T(8,128)(2,1)S(1)} %bitcast.89), channel_id=1, replica_groups=mesh['fsdp'=16,'tp'=8] {'fsdp'}, dimensions={0} | all-to-all | bytes 3932160 | tf_op jit(solution)/shard_map/all_to_all | solution.py:189
  130.7 1.8 reduce_sum.59
  132.7 29.6 %all_to_all.59 = bf16[16,120,512]{2,1,0:T(8,128)(2,1)S(1)} all-to-all(bf16[16,120,512]{2,1,0:T(8,128)(2,1)S(1)} %broadcast_in_dim.7), channel_id=1, replica_groups=mesh['fsdp'=16,'tp'=8] {'fsdp'}, dimensions={0} | all-to-all | bytes 3932160 | tf_op jit(solution)/shard_map/all_to_all | solution.py:194
  162.2 1.3 convolution_bitcast_fusion.1
  163.6 2.8 convolution_convert_fusion.3
  167.3 3.5 all-to-all-start.5
  172.2 9.5 %all-to-all-done.5 = bf16[8,72,512]{2,1,0:T(8,128)(2,1)S(1)} async-done(((bf16[8,72,512]{2,1,0:T(8,128)(2,1)}), bf16[8,72,512]{2,1,0:T(8,128)(2,1)S(1)}, u32[]{:S(2)}, u32[]{:S(2)}) %all-to-all-start.5) | async-done | bytes 589856 | tf_op jit(solution)/shard_map/all_to_all | solution.py:285
  181.9 13.3 %all-gather = bf16[576,512]{1,0:T(8,128)(2,1)S(1)} all-gather(bf16[72,512]{1,0:T(8,128)(2,1)S(1)} %reduce_sum.60), channel_id=2, replica_groups=mesh['fsdp'=16,'tp'=8] {'tp'}, dimensions={0}, use_global_device_ids=true | all-gather | bytes 663552 | tf_op jit(solution)/shard_map/all_gather | solution.py:286
  196.7 3.6 all-to-all-start.6
  200.4 15.2 %all-to-all-done.6 = bf16[16,192,128]{2,1,0:T(8,128)(2,1)S(1)} async-done(((bf16[16,192,128]{2,1,0:T(8,128)(2,1)}), bf16[16,192,128]{2,1,0:T(8,128)(2,1)S(1)}, u32[]{:S(2)}, u32[]{:S(2)}) %all-to-all-start.6) | async-done | bytes 786464 | tf_op jit(solution)/shard_map/all_to_all | solution.py:292
  216.8 3.7 all-to-all-start.7
  221.6 2.5 fusion
  224.1 1.7 fusion.19
  225.8 11.9 %all-to-all-done.7 = bf16[16,256,128]{2,1,0:T(8,128)(2,1)S(1)} async-done(((bf16[16,256,128]{2,1,0:T(8,128)(2,1)}), bf16[16,256,128]{2,1,0:T(8,128)(2,1)S(1)}, u32[]{:S(2)}, u32[]{:S(2)}) %all-to-all-start.7) | async-done | bytes 1048608 | tf_op jit(solution)/shard_map/all_to_all | solution.py:194
  240.7 4.6 all-to-all-start.8
  245.3 85.3 %shard_map.92 = f32[512,512]{1,0:T(8,128)S(1)} custom-call(f32[512,512]{1,0:T(8,128)S(1)} %bitcast.73), custom_call_target="tpu_custom_call" | custom-call | flops 1000000 | bytes 1024 | tf_op jit(solution)/shard_map/pallas_call | solution.py:163
  332.5 83.4 %shard_map.93 = f32[512,512]{1,0:T(8,128)S(1)} custom-call(f32[512,512]{1,0:T(8,128)S(1)} %convolution_multiply_fusion.a_ref), custom_call_target="tpu_custom_call" | custom-call | flops 1000000 | bytes 1024 | tf_op jit(solution)/shard_map/pallas_call | solution.py:163
  416.9 1.9 fusion.21
  420.8 1.3 fusion.4
  422.0 1.3 fusion.6
  423.3 3.2 shard_map.94
  426.5 31.5 %all_to_all.60 = bf16[16,120,512]{2,1,0:T(8,128)(2,1)} all-to-all(bf16[16,120,512]{2,1,0:T(8,128)(2,1)S(1)} %get-tuple-element.27), channel_id=1, replica_groups=mesh['fsdp'=16,'tp'=8] {'fsdp'}, dimensions={0} | all-to-all | bytes 3932160 | tf_op jit(solution)/shard_map/all_to_all | solution.py:313
  458.0 3.5 all-to-all-start.10
  461.5 4.7 subtract_convert_fusion
  466.2 3.9 all-to-all-done.10.got_ref
  470.9 1.8 shard_map.95
  (76 shorter events, 17.9 us)
Async XLA Ops:
  0.6 1.6 copy-start
  68.2 1.3 copy-start.3
  98.2 1.2 copy-start.6
  132.7 29.6 %copy-start.4 = (bf16[16,120,512]{2,1,0:T(8,128)(2,1)S(1)}, bf16[16,120,512]{2,1,0:T(8,128)(2,1)}, u32[]{:S(2)}) copy-start(bf16[16,120,512]{2,1,0:T(8,128)(2,1)} %copy-done.3) | copy-start | bytes 5898244
  162.2 1.3 copy-start.5
  166.4 4.4 copy-start.19
  166.4 4.5 copy-start.20
  167.3 14.5 %all-to-all-start.5 = ((bf16[8,72,512]{2,1,0:T(8,128)(2,1)}), bf16[8,72,512]{2,1,0:T(8,128)(2,1)S(1)}, u32[]{:S(2)}, u32[]{:S(2)}) async-start(bf16[8,72,512]{2,1,0:T(8,128)(2,1)} %fusion.9), calls=%async_computation.5 | async-start | bytes 1179648 | tf_op jit(solution)/shard_map/all_to_all | solution.py:285
  181.9 13.8 %copy-start.15 = (bf16[64,16,120]{2,0,1:T(8,128)(2,1)S(1)}, bf16[64,16,120]{2,0,1:T(8,128)(2,1)}, u32[]{:S(2)}) copy-start(bf16[64,16,120]{2,0,1:T(8,128)(2,1)} %copy.13) | copy-start | bytes 737284
  195.2 5.1 %copy-start.12 = (bf16[576,512]{1,0:T(8,128)(2,1)}, bf16[576,512]{1,0:T(8,128)(2,1)S(1)}, u32[]{:S(2)}) copy-start(bf16[576,512]{1,0:T(8,128)(2,1)S(1)} %all-gather) | copy-start | bytes 1769476
  196.7 18.9 %all-to-all-start.6 = ((bf16[16,192,128]{2,1,0:T(8,128)(2,1)}), bf16[16,192,128]{2,1,0:T(8,128)(2,1)S(1)}, u32[]{:S(2)}, u32[]{:S(2)}) async-start(bf16[16,192,128]{2,1,0:T(8,128)(2,1)} %fusion.8), calls=%async_computation.6 | async-start | bytes 1572864 | tf_op jit(solution)/shard_map/all_to_all | solution.py:292
  215.6 1.3 copy-start.11
  216.8 20.8 %all-to-all-start.7 = ((bf16[16,256,128]{2,1,0:T(8,128)(2,1)}), bf16[16,256,128]{2,1,0:T(8,128)(2,1)S(1)}, u32[]{:S(2)}, u32[]{:S(2)}) async-start(bf16[16,256,128]{2,1,0:T(8,128)(2,1)} %broadcast_in_dim.8), calls=%async_computation.7 | async-start | bytes 2097152 | tf_op jit(solution)/shard_map/all_to_all | solution.py:194
  221.6 2.5 copy-start.8
  237.7 1.0 copy-start.10
  240.7 182.6 %all-to-all-start.8 = ((bf16[16,120,512]{2,1,0:T(8,128)(2,1)}), bf16[16,120,512]{2,1,0:T(8,128)(2,1)}, u32[]{:S(2)}, u32[]{:S(2)}) async-start(bf16[16,120,512]{2,1,0:T(8,128)(2,1)} %bitcast.86), calls=%async_computation.8 | async-start | bytes 3932160 | tf_op jit(solution)/shard_map/all_to_all | solution.py:308
  245.3 85.4 %copy-start.13 = (bf16[1,16,4,8,4,128]{5,3,4,2,0,1:T(8,128)(2,1)S(1)}, bf16[1,16,4,8,4,128]{5,3,4,2,0,1:T(8,128)(2,1)}, u32[]{:S(2)}) copy-start(bf16[1,16,4,8,4,128]{5,3,4,2,0,1:T(8,128)(2,1)} %slice.46) | copy-start | bytes 1572868
  416.9 2.5 copy-start.1
  416.9 1.9 copy-start.18
  416.9 2.2 copy-start.17
  418.8 1.0 copy-start.9
  419.0 1.2 copy-start.7
  422.0 1.3 copy-start.2
  426.5 35.0 %copy-start.16 = (bf16[512,512]{1,0:T(8,128)(2,1)S(1)}, bf16[512,512]{1,0:T(8,128)(2,1)}, u32[]{:S(2)}) copy-start(bf16[512,512]{1,0:T(8,128)(2,1)} %fusion.4) | copy-start | bytes 1572868
  458.0 12.2 %all-to-all-start.10 = ((bf16[16,64,128]{2,1,0:T(8,128)(2,1)}), bf16[16,64,128]{2,1,0:T(8,128)(2,1)S(1)}, u32[]{:S(2)}, u32[]{:S(2)}) async-start(bf16[16,64,128]{2,1,0:T(8,128)(2,1)} %get-tuple-element.29), calls=%async_computation.10 | async-start | bytes 524288 | tf_op jit(solution)/shard_map/all_to_all | solution.py:315
  470.2 0.7 copy-start.14

commit v9 on v8

--- a/solution.py
+++ b/solution.py
@@ -204,7 +204,7 @@
     return x.reshape(n, rows // 8, 8, cols // 128, 128).transpose(0, 1, 3, 2, 4).reshape(n, -1, 128)
 
 
-def finish_kernel(scale, parts_ref, high_ref, low_ref, one_ref, two_ref, out_ref, back_ref):
+def finish_kernel(scale, parts_ref, high_ref, low_ref, one_ref, two_ref, out_ref):
     nf, rows, rank = parts_ref.shape
     share = rank // nf
     raw = parts_ref[0].astype(F32)
@@ -216,24 +216,24 @@
     one = BETA_ONE * one_ref[...] + (1.0 - BETA_ONE) * reduced
     two = BETA_TWO * two_ref[...] + (1.0 - BETA_TWO) * reduced * reduced
     direction = (one / (jnp.sqrt(two) + ADAM_EPS)).astype(BF)
-    pad = jnp.zeros((back_ref.shape[2] - rows, rank), F32)
+    pad = jnp.zeros((-rows % 128, rank), F32)
     one = jnp.concatenate([one, pad], axis=0).T
     two = jnp.concatenate([two, pad], axis=0).T
+    both = [one.astype(BF), two.astype(BF)]
     for g in range(nf):
-        out_ref[g] = direction
-        at = slice(g * share, (g + 1) * share)
-        back_ref[g, :share, :] = one[at].astype(BF)
-        back_ref[g, share:, :] = two[at].astype(BF)
+        out_ref[g, 16:, :] = direction
+        for i in range(2 * share // 16):
+            first = g * share + i * 16 % share
+            out_ref[g, :16, i * 128 : (i + 1) * 128] = both[i * 16 // share][first : first + 16]
 
 
 def finish(scale, parts, high, low, one, two):
     nf, rows, rank = parts.shape
-    back = (nf, 2 * rank // nf, rows + -rows % 128)
     return pl.pallas_call(
         functools.partial(finish_kernel, scale),
-        out_shape=[jax.ShapeDtypeStruct(parts.shape, BF), jax.ShapeDtypeStruct(back, BF)],
+        out_shape=jax.ShapeDtypeStruct((nf, 16 + rows, rank), BF),
         in_specs=[pl.BlockSpec(memory_space=pltpu.VMEM)] * 5,
-        out_specs=[pl.BlockSpec(memory_space=pltpu.VMEM)] * 2,
+        out_specs=pl.BlockSpec(memory_space=pltpu.VMEM),
         cost_estimate=pl.CostEstimate(flops=10**9, bytes_accessed=6 * 2**20, transcendentals=0),
         compiler_params=pltpu.CompilerParams(vmem_limit_bytes=32 * 2**20),
     )(parts, high, low, one, two)
@@ -242,13 +242,14 @@
 def unpack_kernel(width, got_ref, one_ref, two_ref):
     share = one_ref.shape[0]
     for ref, first in ((one_ref, 0), (two_ref, share)):
-        rows = [got_ref[g, first : first + share, :].astype(F32)[:, :width] for g in range(got_ref.shape[0])]
-        ref[...] = jnp.concatenate(rows, axis=1)
-
-
-def unpack(got, width):
-    nf, share, _ = got.shape
-    shape = jax.ShapeDtypeStruct((share // 2, nf * width), F32)
+        for i in range(share // 16):
+            lanes = slice((first // 16 + i) * 128, (first // 16 + i) * 128 + width)
+            rows = [got_ref[g].astype(F32)[:, lanes] for g in range(got_ref.shape[0])]
+            ref[i * 16 : (i + 1) * 16, :] = jnp.concatenate(rows, axis=1)
+
+
+def unpack(got, width, share):
+    shape = jax.ShapeDtypeStruct((share, got.shape[0] * width), F32)
     return pl.pallas_call(
         functools.partial(unpack_kernel, width),
         out_shape=[shape, shape],
@@ -309,10 +310,10 @@
     rotated_one, rotated_two, first_basis, new_basis = lax.optimization_barrier(
         (rotated_one, rotated_two, first_basis, new_basis)
     )
-    direction, back = finish(1.0 / M, parts, *halves(both), rotated_one, rotated_two)
-    direction = lax.all_to_all(direction, "fsdp", 0, 0, tiled=True).reshape(cols, rank)
-    direction, back = lax.optimization_barrier((direction, back))
-    moment_one, moment_two = unpack(lax.all_to_all(back, "fsdp", 0, 0, tiled=True), share_cols)
+    got = finish(1.0 / M, parts, *halves(both), rotated_one, rotated_two)
+    got = lax.all_to_all(got, "fsdp", 0, 0, tiled=True)
+    direction = got[:, 16:].reshape(cols, rank)
+    moment_one, moment_two = unpack(got[:, :16], share_cols, share_rows)
     expanded = mm(new_basis, direction, 1, 1)
     new_weight = (weight.astype(F32) - STEP_SIZE * inv_sqrt * expanded).astype(BF)
     return (first_basis, new_basis, moment_one, moment_two, new_weight)

time: 474 us -> 471 us (level)
  transfers between devices with their start and end apart: 5 -> 4, of which waited for: 4 -> 3; matrix products, arithmetic and copies ran while one was open for 4% -> 3% of each run, Pallas kernels for 36% -> 36%
where the time goes in v9:
time: 471 us; the launch traced here: 470 us
  blocking collectives  200 us (42%)
  Pallas kernels  173 us (37%)
  waiting for transfers between devices  36.6 us (8%)
  matrix products  24.6 us (5%)
  starting transfers between devices  15.4 us (3%)
  local copies, waits for them, and re-layouts  13.3 us (3%)
  other arithmetic  5.47 us (1%)
    pallas_call x2, Pallas kernels, chol_inv(): pl.pallas_call(chol_kernel, out_shape=jax.ShapeDtypeStruct((n, n), F32),...  169 us
    all_to_all x3, blocking collectives, scatter_sum(): lax.all_to_all(x.astype(BF).reshape(n, x.shape[0] // n, x.shape[1]), axis...  80.6 us
    all_to_all x2, blocking collectives, gather(): lax.all_to_all(jnp.broadcast_to(x[None], (n,) + x.shape), axis, 0, 0, til...  59 us
    all_to_all x1, blocking collectives, per_device(): got = lax.all_to_all(got, 'fsdp', 0, 0, tiled=True)  34.1 us
    dot_general x14, matrix products, mm(): lax.dot_general(a, b, (((ca,), (cb,)), ((), ())), preferred_element_type=...  19.9 us
    all_to_all x1, waiting for transfers between devices, per_device(): got = lax.all_to_all(got, 'fsdp', 0, 0, tiled=True)  15.2 us
    all_gather x1, blocking collectives, per_device(): both = lax.all_gather(both, 'tp', axis=0, tiled=False)  13.3 us
    all_gather x1, blocking collectives, per_device(): image = lax.all_gather(image, 'tp', axis=0, tiled=True)  13.1 us
  transfers between devices with their start and end apart: 4, of which 3 were waited for; matrix products, arithmetic and copies ran while one was open for 3% of the time, Pallas kernels for 36%

profile of v9, /device:TPU:0, one launch (start us, length us, event | category | flops | bytes accessed | tf_op | source)
XLA Modules:
  0.0 469.6 jit_solution(4549015773532437329)
XLA Ops:
  0.7 1.5 copy-done
  2.2 2.3 convolution_convert_fusion.2
  4.4 33.9 %all_to_all.50 = bf16[16,120,512]{2,1,0:T(8,128)(2,1)S(1)} all-to-all(bf16[16,120,512]{2,1,0:T(8,128)(2,1)S(1)} %bitcast.88), channel_id=1, replica_groups=mesh['fsdp'=16,'tp'=8] {'fsdp'}, dimensions={0} | all-to-all | bytes 3932160 | tf_op jit(solution)/shard_map/all_to_all | solution.py:189
  38.8 29.4 %all_to_all.51 = bf16[16,120,512]{2,1,0:T(8,128)(2,1)S(1)} all-to-all(bf16[16,120,512]{2,1,0:T(8,128)(2,1)S(1)} %broadcast_in_dim.6), channel_id=1, replica_groups=mesh['fsdp'=16,'tp'=8] {'fsdp'}, dimensions={0} | all-to-all | bytes 3932160 | tf_op jit(solution)/shard_map/all_to_all | solution.py:194
  69.5 15.5 %all_to_all.52 = bf16[8,64,512]{2,1,0:T(8,128)(2,1)S(1)} all-to-all(bf16[8,64,512]{2,1,0:T(8,128)(2,1)S(1)} %bitcast.93), channel_id=1, replica_groups=mesh['fsdp'=16,'tp'=8] {'tp'}, dimensions={0} | all-to-all | bytes 1048576 | tf_op jit(solution)/shard_map/all_to_all | solution.py:189
  85.1 13.1 %all_gather.9 = bf16[512,512]{1,0:T(8,128)(2,1)S(1)} all-gather(bf16[64,512]{1,0:T(8,128)(2,1)S(1)} %reduce_sum.58), channel_id=1, replica_groups=mesh['fsdp'=16,'tp'=8] {'tp'}, dimensions={0}, use_global_device_ids=true | all-gather | bytes 589824 | tf_op jit(solution)/shard_map/all_gather | solution.py:277
  99.5 31.2 %all_to_all.53 = bf16[16,120,512]{2,1,0:T(8,128)(2,1)} all-to-all(bf16[16,120,512]{2,1,0:T(8,128)(2,1)S(1)} %bitcast.89), channel_id=1, replica_groups=mesh['fsdp'=16,'tp'=8] {'fsdp'}, dimensions={0} | all-to-all | bytes 3932160 | tf_op jit(solution)/shard_map/all_to_all | solution.py:189
  130.7 1.8 reduce_sum.59
  132.7 29.6 %all_to_all.54 = bf16[16,120,512]{2,1,0:T(8,128)(2,1)S(1)} all-to-all(bf16[16,120,512]{2,1,0:T(8,128)(2,1)S(1)} %broadcast_in_dim.7), channel_id=1, replica_groups=mesh['fsdp'=16,'tp'=8] {'fsdp'}, dimensions={0} | all-to-all | bytes 3932160 | tf_op jit(solution)/shard_map/all_to_all | solution.py:194
  162.3 1.3 convolution_bitcast_fusion.1
  163.6 2.8 convolution_convert_fusion.3
  167.3 3.5 all-to-all-start.5
  172.3 9.5 %all-to-all-done.5 = bf16[8,72,512]{2,1,0:T(8,128)(2,1)S(1)} async-done(((bf16[8,72,512]{2,1,0:T(8,128)(2,1)}), bf16[8,72,512]{2,1,0:T(8,128)(2,1)S(1)}, u32[]{:S(2)}, u32[]{:S(2)}) %all-to-all-start.5) | async-done | bytes 589856 | tf_op jit(solution)/shard_map/all_to_all | solution.py:286
  181.9 13.3 %all-gather = bf16[576,512]{1,0:T(8,128)(2,1)S(1)} all-gather(bf16[72,512]{1,0:T(8,128)(2,1)S(1)} %reduce_sum.60), channel_id=2, replica_groups=mesh['fsdp'=16,'tp'=8] {'tp'}, dimensions={0}, use_global_device_ids=true | all-gather | bytes 663552 | tf_op jit(solution)/shard_map/all_gather | solution.py:287
  196.7 3.6 all-to-all-start.6
  200.4 15.2 %all-to-all-done.6 = bf16[16,192,128]{2,1,0:T(8,128)(2,1)S(1)} async-done(((bf16[16,192,128]{2,1,0:T(8,128)(2,1)}), bf16[16,192,128]{2,1,0:T(8,128)(2,1)S(1)}, u32[]{:S(2)}, u32[]{:S(2)}) %all-to-all-start.6) | async-done | bytes 786464 | tf_op jit(solution)/shard_map/all_to_all | solution.py:293
  216.9 3.7 all-to-all-start.7
  221.6 2.5 fusion
  224.1 1.7 fusion.19
  225.8 11.9 %all-to-all-done.7 = bf16[16,256,128]{2,1,0:T(8,128)(2,1)S(1)} async-done(((bf16[16,256,128]{2,1,0:T(8,128)(2,1)}), bf16[16,256,128]{2,1,0:T(8,128)(2,1)S(1)}, u32[]{:S(2)}, u32[]{:S(2)}) %all-to-all-start.7) | async-done | bytes 1048608 | tf_op jit(solution)/shard_map/all_to_all | solution.py:194
  240.7 4.6 all-to-all-start.8
  245.3 85.3 %shard_map.92 = f32[512,512]{1,0:T(8,128)S(1)} custom-call(f32[512,512]{1,0:T(8,128)S(1)} %bitcast.73), custom_call_target="tpu_custom_call" | custom-call | flops 1000000 | bytes 1024 | tf_op jit(solution)/shard_map/pallas_call | solution.py:163
  332.5 83.4 %shard_map.93 = f32[512,512]{1,0:T(8,128)S(1)} custom-call(f32[512,512]{1,0:T(8,128)S(1)} %convolution_multiply_fusion.a_ref), custom_call_target="tpu_custom_call" | custom-call | flops 1000000 | bytes 1024 | tf_op jit(solution)/shard_map/pallas_call | solution.py:163
  416.9 1.9 fusion.21
  420.8 1.3 fusion.4
  422.0 1.3 fusion.6
  423.3 2.5 shard_map.94
  425.8 34.1 %all_to_all.55 = bf16[16,136,512]{2,1,0:T(8,128)(2,1)S(1)} all-to-all(bf16[16,136,512]{2,1,0:T(8,128)(2,1)S(1)} %shard_map.94), channel_id=1, replica_groups=mesh['fsdp'=16,'tp'=8] {'fsdp'}, dimensions={0} | all-to-all | bytes 4456448 | tf_op jit(solution)/shard_map/all_to_all | solution.py:314
  459.9 1.4 copy-done.3
  462.0 1.8 shard_map.95
  463.8 1.5 slice-done
  465.4 4.2 subtract_convert_fusion
  (77 shorter events, 17.9 us)
Async XLA Ops:
  0.6 1.6 copy-start
  68.2 1.3 copy-start.4
  98.2 1.2 copy-start.7
  132.7 29.6 %copy-start.5 = (bf16[16,120,512]{2,1,0:T(8,128)(2,1)S(1)}, bf16[16,120,512]{2,1,0:T(8,128)(2,1)}, u32[]{:S(2)}) copy-start(bf16[16,120,512]{2,1,0:T(8,128)(2,1)} %copy-done.4) | copy-start | bytes 5898244
  162.3 1.3 copy-start.6
  166.4 4.4 copy-start.19
  166.4 4.5 copy-start.20
  167.3 14.5 %all-to-all-start.5 = ((bf16[8,72,512]{2,1,0:T(8,128)(2,1)}), bf16[8,72,512]{2,1,0:T(8,128)(2,1)S(1)}, u32[]{:S(2)}, u32[]{:S(2)}) async-start(bf16[8,72,512]{2,1,0:T(8,128)(2,1)} %fusion.9), calls=%async_computation.5 | async-start | bytes 1179648 | tf_op jit(solution)/shard_map/all_to_all | solution.py:286
  181.9 13.8 %copy-start.15 = (bf16[64,16,120]{2,0,1:T(8,128)(2,1)S(1)}, bf16[64,16,120]{2,0,1:T(8,128)(2,1)}, u32[]{:S(2)}) copy-start(bf16[64,16,120]{2,0,1:T(8,128)(2,1)} %copy.13) | copy-start | bytes 737284
  195.2 5.1 %copy-start.13 = (bf16[576,512]{1,0:T(8,128)(2,1)}, bf16[576,512]{1,0:T(8,128)(2,1)S(1)}, u32[]{:S(2)}) copy-start(bf16[576,512]{1,0:T(8,128)(2,1)S(1)} %all-gather) | copy-start | bytes 1769476
  196.7 18.9 %all-to-all-start.6 = ((bf16[16,192,128]{2,1,0:T(8,128)(2,1)}), bf16[16,192,128]{2,1,0:T(8,128)(2,1)S(1)}, u32[]{:S(2)}, u32[]{:S(2)}) async-start(bf16[16,192,128]{2,1,0:T(8,128)(2,1)} %fusion.8), calls=%async_computation.6 | async-start | bytes 1572864 | tf_op jit(solution)/shard_map/all_to_all | solution.py:293
  215.6 1.3 copy-start.12
  216.9 20.8 %all-to-all-start.7 = ((bf16[16,256,128]{2,1,0:T(8,128)(2,1)}), bf16[16,256,128]{2,1,0:T(8,128)(2,1)S(1)}, u32[]{:S(2)}, u32[]{:S(2)}) async-start(bf16[16,256,128]{2,1,0:T(8,128)(2,1)} %broadcast_in_dim.8), calls=%async_computation.7 | async-start | bytes 2097152 | tf_op jit(solution)/shard_map/all_to_all | solution.py:194
  221.6 2.5 copy-start.9
  237.7 1.0 copy-start.11
  240.7 182.6 %all-to-all-start.8 = ((bf16[16,120,512]{2,1,0:T(8,128)(2,1)}), bf16[16,120,512]{2,1,0:T(8,128)(2,1)}, u32[]{:S(2)}, u32[]{:S(2)}) async-start(bf16[16,120,512]{2,1,0:T(8,128)(2,1)} %bitcast.87), calls=%async_computation.8 | async-start | bytes 3932160 | tf_op jit(solution)/shard_map/all_to_all | solution.py:309
  245.3 85.4 %copy-start.14 = (bf16[1,16,4,8,4,128]{5,3,4,2,0,1:T(8,128)(2,1)S(1)}, bf16[1,16,4,8,4,128]{5,3,4,2,0,1:T(8,128)(2,1)}, u32[]{:S(2)}) copy-start(bf16[1,16,4,8,4,128]{5,3,4,2,0,1:T(8,128)(2,1)} %slice.54) | copy-start | bytes 1572868
  416.9 2.5 copy-start.1
  416.9 1.9 copy-start.18
  416.9 2.2 copy-start.17
  418.8 1.0 copy-start.10
  419.0 1.2 copy-start.8
  422.0 1.3 copy-start.2
  459.9 1.4 copy-start.3
  463.8 1.5 slice-start
  463.8 1.6 copy-start.16

commit v10 on v9

--- a/solution.py
+++ b/solution.py
@@ -289,15 +289,16 @@
     gram = both[:, rows : rows + few].reshape(1, rank // nf, rank)
     outer = (mm(wide, wide, 0, 0) / M).astype(BF).reshape(nf, -1, rank)
     raw = row_major(mm(grad, wide, 0, 0).astype(BF))
-    got = jnp.concatenate([sent, tiles(outer)], axis=1)
+    gram = jnp.broadcast_to(tiles(gram), (nf, rank * rank // nf // 128, 128))
+    got = jnp.concatenate([sent, tiles(outer), gram], axis=1)
     got = lax.all_to_all(got, "fsdp", 0, 0, tiled=True)
     first_old = got[:, :share_rows].reshape(rank, -1)
     second_old = got[:, share_rows : 2 * share_rows].reshape(rank, -1)
-    sums = jnp.sum(got[:, 2 * share_rows :].astype(F32), axis=0).astype(BF)
-    grams = gather(jnp.concatenate([sums, tiles(gram)[0]], axis=0), "fsdp", nf)
-    grams, raw = lax.optimization_barrier((grams, raw))
-    grams = grams.reshape(nf, 2, -1, rank // 128, 8, 128).transpose(1, 0, 2, 4, 3, 5).reshape(2, rank, rank)
-    outer, gram = grams[0].astype(F32), grams[1].astype(F32) / M
+    gram = got[:, 2 * share_rows + gram.shape[1] :]
+    sums = jnp.sum(got[:, 2 * share_rows : -gram.shape[1]].astype(F32), axis=0).astype(BF)
+    outer, raw = lax.optimization_barrier((gather(sums, "fsdp", nf), raw))
+    outer, gram = [x.reshape(-1, rank // 128, 8, 128).transpose(0, 2, 1, 3).reshape(rank, rank).astype(F32) for x in (outer, gram)]
+    gram = gram / M
     inverse = chol_inv(gram)
     second = chol_inv(mm_high(mm_high(inverse, outer, 1, 0), inverse, 1, 1) / M)
     both = mm_high(second, inverse, 1, 0)

time: 471 us -> 469 us (level)
  waiting for transfers between devices: 36.6 us -> 28.9 us
    all_to_all x1, waiting for transfers between devices: 11.9 us -> 0.01 us  [gather(): lax.all_to_all(jnp.broadcast_to(x[None], (n,) + x.shape), axis, 0, 0, til...]
  transfers between devices with their start and end apart: 4 -> 4, of which waited for: 3 -> 2; matrix products, arithmetic and copies ran while one was open for 3% -> 3% of each run, Pallas kernels for 36% -> 36%
where the time goes in v10:
time: 469 us; the launch traced here: 467 us
  blocking collectives  202 us (43%)
  Pallas kernels  173 us (37%)
  waiting for transfers between devices  28.9 us (6%)
  matrix products  25.6 us (5%)
  starting transfers between devices  18.6 us (4%)
  local copies, waits for them, and re-layouts  12.5 us (3%)
    pallas_call x2, Pallas kernels, chol_inv(): pl.pallas_call(chol_kernel, out_shape=jax.ShapeDtypeStruct((n, n), F32),...  169 us
    all_to_all x3, blocking collectives, scatter_sum(): lax.all_to_all(x.astype(BF).reshape(n, x.shape[0] // n, x.shape[1]), axis...  80.7 us
    all_to_all x2, blocking collectives, gather(): lax.all_to_all(jnp.broadcast_to(x[None], (n,) + x.shape), axis, 0, 0, til...  59 us
    all_to_all x1, blocking collectives, per_device(): got = lax.all_to_all(got, 'fsdp', 0, 0, tiled=True)  36.4 us
    dot_general x14, matrix products, mm(): lax.dot_general(a, b, (((ca,), (cb,)), ((), ())), preferred_element_type=...  19.9 us
    all_to_all x1, waiting for transfers between devices, per_device(): got = lax.all_to_all(got, 'fsdp', 0, 0, tiled=True)  18.7 us
    all_gather x1, blocking collectives, per_device(): both = lax.all_gather(both, 'tp', axis=0, tiled=False)  13.2 us
    all_gather x1, blocking collectives, per_device(): image = lax.all_gather(image, 'tp', axis=0, tiled=True)  13.1 us
  transfers between devices with their start and end apart: 4, of which 2 were waited for; matrix products, arithmetic and copies ran while one was open for 3% of the time, Pallas kernels for 36%

profile of v10, /device:TPU:0, one launch (start us, length us, event | category | flops | bytes accessed | tf_op | source)
XLA Modules:
  0.0 466.8 jit_solution(13640634823184772872)
XLA Ops:
  0.7 1.5 copy-done
  2.2 2.3 convolution_convert_fusion.2
  4.4 33.9 %all_to_all.50 = bf16[16,120,512]{2,1,0:T(8,128)(2,1)S(1)} all-to-all(bf16[16,120,512]{2,1,0:T(8,128)(2,1)S(1)} %bitcast.90), channel_id=1, replica_groups=mesh['fsdp'=16,'tp'=8] {'fsdp'}, dimensions={0} | all-to-all | bytes 3932160 | tf_op jit(solution)/shard_map/all_to_all | solution.py:189
  38.8 29.4 %all_to_all.51 = bf16[16,120,512]{2,1,0:T(8,128)(2,1)S(1)} all-to-all(bf16[16,120,512]{2,1,0:T(8,128)(2,1)S(1)} %broadcast_in_dim.10), channel_id=1, replica_groups=mesh['fsdp'=16,'tp'=8] {'fsdp'}, dimensions={0} | all-to-all | bytes 3932160 | tf_op jit(solution)/shard_map/all_to_all | solution.py:194
  69.5 15.5 %all_to_all.52 = bf16[8,64,512]{2,1,0:T(8,128)(2,1)S(1)} all-to-all(bf16[8,64,512]{2,1,0:T(8,128)(2,1)S(1)} %bitcast.95), channel_id=1, replica_groups=mesh['fsdp'=16,'tp'=8] {'tp'}, dimensions={0} | all-to-all | bytes 1048576 | tf_op jit(solution)/shard_map/all_to_all | solution.py:189
  85.1 13.1 %all_gather.9 = bf16[512,512]{1,0:T(8,128)(2,1)S(1)} all-gather(bf16[64,512]{1,0:T(8,128)(2,1)S(1)} %reduce_sum.58), channel_id=1, replica_groups=mesh['fsdp'=16,'tp'=8] {'tp'}, dimensions={0}, use_global_device_ids=true | all-gather | bytes 589824 | tf_op jit(solution)/shard_map/all_gather | solution.py:277
  99.5 31.2 %all_to_all.53 = bf16[16,120,512]{2,1,0:T(8,128)(2,1)} all-to-all(bf16[16,120,512]{2,1,0:T(8,128)(2,1)S(1)} %bitcast.91), channel_id=1, replica_groups=mesh['fsdp'=16,'tp'=8] {'fsdp'}, dimensions={0} | all-to-all | bytes 3932160 | tf_op jit(solution)/shard_map/all_to_all | solution.py:189
  130.7 1.8 reduce_sum.59
  132.7 29.6 %all_to_all.54 = bf16[16,120,512]{2,1,0:T(8,128)(2,1)S(1)} all-to-all(bf16[16,120,512]{2,1,0:T(8,128)(2,1)S(1)} %broadcast_in_dim.11), channel_id=1, replica_groups=mesh['fsdp'=16,'tp'=8] {'fsdp'}, dimensions={0} | all-to-all | bytes 3932160 | tf_op jit(solution)/shard_map/all_to_all | solution.py:194
  162.3 1.3 convolution_bitcast_fusion.1
  163.6 2.8 convolution_convert_fusion.3
  167.3 3.5 all-to-all-start.5
  171.6 10.2 %all-to-all-done.5 = bf16[8,72,512]{2,1,0:T(8,128)(2,1)S(1)} async-done(((bf16[8,72,512]{2,1,0:T(8,128)(2,1)}), bf16[8,72,512]{2,1,0:T(8,128)(2,1)S(1)}, u32[]{:S(2)}, u32[]{:S(2)}) %all-to-all-start.5) | async-done | bytes 589856 | tf_op jit(solution)/shard_map/all_to_all | solution.py:286
  181.9 13.2 %all-gather = bf16[576,512]{1,0:T(8,128)(2,1)S(1)} all-gather(bf16[72,512]{1,0:T(8,128)(2,1)S(1)} %reduce_sum.60), channel_id=2, replica_groups=mesh['fsdp'=16,'tp'=8] {'tp'}, dimensions={0}, use_global_device_ids=true | all-gather | bytes 663552 | tf_op jit(solution)/shard_map/all_gather | solution.py:287
  197.8 3.7 all-to-all-start.6
  203.4 2.5 fusion
  205.9 18.7 %all-to-all-done.6 = bf16[16,320,128]{2,1,0:T(8,128)(2,1)S(1)} async-done(((bf16[16,320,128]{2,1,0:T(8,128)(2,1)}), bf16[16,320,128]{2,1,0:T(8,128)(2,1)S(1)}, u32[]{:S(2)}, u32[]{:S(2)}) %all-to-all-start.6) | async-done | bytes 1310752 | tf_op jit(solution)/shard_map/all_to_all | solution.py:294
  225.7 4.4 all-to-all-start.7
  230.3 85.3 %shard_map.92 = f32[512,512]{1,0:T(8,128)S(1)} custom-call(f32[512,512]{1,0:T(8,128)S(1)} %bitcast.78), custom_call_target="tpu_custom_call" | custom-call | flops 1000000 | bytes 1024 | tf_op jit(solution)/shard_map/pallas_call | solution.py:163
  316.1 1.7 fusion.20
  317.8 1.3 fusion.8
  319.1 7.0 %all-to-all-start.8 = ((bf16[16,120,512]{2,1,0:T(8,128)(2,1)}), bf16[16,120,512]{2,1,0:T(8,128)(2,1)}, u32[]{:S(2)}, u32[]{:S(2)}) async-start(bf16[16,120,512]{2,1,0:T(8,128)(2,1)} %bitcast.89), calls=%async_computation.8 | async-start | bytes 3932160 | tf_op jit(solution)/shard_map/all_to_all | solution.py:310
  326.1 1.8 fusion.21
  328.9 83.4 %shard_map.93 = f32[512,512]{1,0:T(8,128)S(1)} custom-call(f32[512,512]{1,0:T(8,128)S(1)} %convolution_multiply_fusion.a_ref), custom_call_target="tpu_custom_call" | custom-call | flops 1000000 | bytes 1024 | tf_op jit(solution)/shard_map/pallas_call | solution.py:163
  413.5 1.9 fusion.22
  416.9 1.3 fusion.6
  418.2 2.5 shard_map.94
  420.7 36.4 %all_to_all.55 = bf16[16,136,512]{2,1,0:T(8,128)(2,1)S(1)} all-to-all(bf16[16,136,512]{2,1,0:T(8,128)(2,1)S(1)} %shard_map.94), channel_id=1, replica_groups=mesh['fsdp'=16,'tp'=8] {'fsdp'}, dimensions={0} | all-to-all | bytes 4456448 | tf_op jit(solution)/shard_map/all_to_all | solution.py:315
  457.0 1.4 copy-done.5
  459.1 1.8 shard_map.95
  461.0 1.5 slice-done
  462.6 4.2 subtract_convert_fusion
  (74 shorter events, 15.6 us)
Async XLA Ops:
  0.6 1.6 copy-start
  68.2 1.3 copy-start.6
  98.2 1.2 copy-start.10
  132.7 29.6 %copy-start.7 = (bf16[16,120,512]{2,1,0:T(8,128)(2,1)S(1)}, bf16[16,120,512]{2,1,0:T(8,128)(2,1)}, u32[]{:S(2)}) copy-start(bf16[16,120,512]{2,1,0:T(8,128)(2,1)} %copy-done.6) | copy-start | bytes 5898244
  162.3 1.3 copy-start.8
  166.4 4.4 copy-start.18
  166.4 4.5 copy-start.19
  167.3 14.5 %all-to-all-start.5 = ((bf16[8,72,512]{2,1,0:T(8,128)(2,1)}), bf16[8,72,512]{2,1,0:T(8,128)(2,1)S(1)}, u32[]{:S(2)}, u32[]{:S(2)}) async-start(bf16[8,72,512]{2,1,0:T(8,128)(2,1)} %fusion.10), calls=%async_computation.5 | async-start | bytes 1179648 | tf_op jit(solution)/shard_map/all_to_all | solution.py:286
  195.1 0.8 copy-start.14
  197.8 26.8 %all-to-all-start.6 = ((bf16[16,320,128]{2,1,0:T(8,128)(2,1)}), bf16[16,320,128]{2,1,0:T(8,128)(2,1)S(1)}, u32[]{:S(2)}, u32[]{:S(2)}) async-start(bf16[16,320,128]{2,1,0:T(8,128)(2,1)} %fusion.5), calls=%async_computation.6 | async-start | bytes 2621440 | tf_op jit(solution)/shard_map/all_to_all | solution.py:294
  202.6 0.8 copy-start.12
  224.6 5.7 %copy-start.9 = (bf16[16,320,128]{2,1,0:T(8,128)(2,1)}, bf16[16,320,128]{2,1,0:T(8,128)(2,1)S(1)}, u32[]{:S(2)}) copy-start(bf16[16,320,128]{2,1,0:T(8,128)(2,1)S(1)} %all-to-all-done.6) | copy-start | bytes 3932164
  225.7 93.4 %all-to-all-start.7 = ((bf16[16,128,128]{2,1,0:T(8,128)(2,1)}), bf16[16,128,128]{2,1,0:T(8,128)(2,1)}, u32[]{:S(2)}, u32[]{:S(2)}) async-start(bf16[16,128,128]{2,1,0:T(8,128)(2,1)} %broadcast_in_dim.14), calls=%async_computation.7 | async-start | bytes 1048576 | tf_op jit(solution)/shard_map/all_to_all | solution.py:194
  230.1 85.5 %copy-start.11 = (bf16[512,512]{1,0:T(8,128)(2,1)S(1)}, bf16[512,512]{1,0:T(8,128)(2,1)}, u32[]{:S(2)}) copy-start(bf16[512,512]{1,0:T(8,128)(2,1)} %copy-done.10) | copy-start | bytes 1572868
  230.3 85.8 %copy-start.1 = (f32[16,128,128]{2,1,0:T(8,128)}, f32[16,128,128]{2,1,0:T(8,128)S(1)}, u32[]{:S(2)}) copy-start(f32[16,128,128]{2,1,0:T(8,128)S(1)} %convert_multiply_fusion) | copy-start | bytes 3145732
  319.1 99.1 %all-to-all-start.8 = ((bf16[16,120,512]{2,1,0:T(8,128)(2,1)}), bf16[16,120,512]{2,1,0:T(8,128)(2,1)}, u32[]{:S(2)}, u32[]{:S(2)}) async-start(bf16[16,120,512]{2,1,0:T(8,128)(2,1)} %bitcast.89), calls=%async_computation.8 | async-start | bytes 3932160 | tf_op jit(solution)/shard_map/all_to_all | solution.py:310
  412.3 1.2 copy-start.2
  413.3 2.6 copy-start.3
  413.3 2.1 copy-start.17
  413.5 2.1 copy-start.16
  415.4 1.0 copy-start.13
  416.9 1.3 copy-start.4
  457.0 1.4 copy-start.5
  461.0 1.5 slice-start
  461.0 1.6 copy-start.15

commit v11 on v9

--- a/solution.py
+++ b/solution.py
@@ -244,7 +244,7 @@
     for ref, first in ((one_ref, 0), (two_ref, share)):
         for i in range(share // 16):
             lanes = slice((first // 16 + i) * 128, (first // 16 + i) * 128 + width)
-            rows = [got_ref[g].astype(F32)[:, lanes] for g in range(got_ref.shape[0])]
+            rows = [got_ref[g, :16, :].astype(F32)[:, lanes] for g in range(got_ref.shape[0])]
             ref[i * 16 : (i + 1) * 16, :] = jnp.concatenate(rows, axis=1)
 
 
@@ -313,7 +313,7 @@
     got = finish(1.0 / M, parts, *halves(both), rotated_one, rotated_two)
     got = lax.all_to_all(got, "fsdp", 0, 0, tiled=True)
     direction = got[:, 16:].reshape(cols, rank)
-    moment_one, moment_two = unpack(got[:, :16], share_cols, share_rows)
+    moment_one, moment_two = unpack(got, share_cols, share_rows)
     expanded = mm(new_basis, direction, 1, 1)
     new_weight = (weight.astype(F32) - STEP_SIZE * inv_sqrt * expanded).astype(BF)
     return (first_basis, new_basis, moment_one, moment_two, new_weight)

time: 471 us -> 469 us (level)
  no operation moved by 1% of the time
where the time goes in v11:
time: 469 us; the launch traced here: 468 us
  blocking collectives  200 us (43%)
  Pallas kernels  174 us (37%)
  waiting for transfers between devices  36.6 us (8%)
  matrix products  23 us (5%)
  starting transfers between devices  15.4 us (3%)
  local copies, waits for them, and re-layouts  12.1 us (3%)
  other arithmetic  5.47 us (1%)
    pallas_call x2, Pallas kernels, chol_inv(): pl.pallas_call(chol_kernel, out_shape=jax.ShapeDtypeStruct((n, n), F32),...  169 us
    all_to_all x3, blocking collectives, scatter_sum(): lax.all_to_all(x.astype(BF).reshape(n, x.shape[0] // n, x.shape[1]), axis...  80.7 us
    all_to_all x2, blocking collectives, gather(): lax.all_to_all(jnp.broadcast_to(x[None], (n,) + x.shape), axis, 0, 0, til...  59 us
    all_to_all x1, blocking collectives, per_device(): got = lax.all_to_all(got, 'fsdp', 0, 0, tiled=True)  34.1 us
    dot_general x14, matrix products, mm(): lax.dot_general(a, b, (((ca,), (cb,)), ((), ())), preferred_element_type=...  18.4 us
    all_to_all x1, waiting for transfers between devices, per_device(): got = lax.all_to_all(got, 'fsdp', 0, 0, tiled=True)  15.2 us
    all_gather x1, blocking collectives, per_device(): both = lax.all_gather(both, 'tp', axis=0, tiled=False)  13.3 us
    all_gather x1, blocking collectives, per_device(): image = lax.all_gather(image, 'tp', axis=0, tiled=True)  13.1 us
  transfers between devices with their start and end apart: 4, of which 3 were waited for; matrix products, arithmetic and copies ran while one was open for 3% of the time, Pallas kernels for 36%

profile of v11, /device:TPU:0, one launch (start us, length us, event | category | flops | bytes accessed | tf_op | source)
XLA Modules:
  0.0 467.6 jit_solution(9287735093629480248)
XLA Ops:
  0.7 1.5 copy-done
  2.2 2.3 convolution_convert_fusion.2
  4.4 33.9 %all_to_all.50 = bf16[16,120,512]{2,1,0:T(8,128)(2,1)S(1)} all-to-all(bf16[16,120,512]{2,1,0:T(8,128)(2,1)S(1)} %bitcast.87), channel_id=1, replica_groups=mesh['fsdp'=16,'tp'=8] {'fsdp'}, dimensions={0} | all-to-all | bytes 3932160 | tf_op jit(solution)/shard_map/all_to_all | solution.py:189
  38.8 29.4 %all_to_all.51 = bf16[16,120,512]{2,1,0:T(8,128)(2,1)S(1)} all-to-all(bf16[16,120,512]{2,1,0:T(8,128)(2,1)S(1)} %broadcast_in_dim.6), channel_id=1, replica_groups=mesh['fsdp'=16,'tp'=8] {'fsdp'}, dimensions={0} | all-to-all | bytes 3932160 | tf_op jit(solution)/shard_map/all_to_all | solution.py:194
  68.2 1.3 convolution_convert_fusion.4
  69.5 15.5 %all_to_all.52 = bf16[8,64,512]{2,1,0:T(8,128)(2,1)S(1)} all-to-all(bf16[8,64,512]{2,1,0:T(8,128)(2,1)S(1)} %bitcast.93), channel_id=1, replica_groups=mesh['fsdp'=16,'tp'=8] {'tp'}, dimensions={0} | all-to-all | bytes 1048576 | tf_op jit(solution)/shard_map/all_to_all | solution.py:189
  85.1 13.1 %all_gather.9 = bf16[512,512]{1,0:T(8,128)(2,1)S(1)} all-gather(bf16[64,512]{1,0:T(8,128)(2,1)S(1)} %reduce_sum.58), channel_id=1, replica_groups=mesh['fsdp'=16,'tp'=8] {'tp'}, dimensions={0}, use_global_device_ids=true | all-gather | bytes 589824 | tf_op jit(solution)/shard_map/all_gather | solution.py:277
  99.5 31.2 %all_to_all.53 = bf16[16,120,512]{2,1,0:T(8,128)(2,1)} all-to-all(bf16[16,120,512]{2,1,0:T(8,128)(2,1)S(1)} %bitcast.88), channel_id=1, replica_groups=mesh['fsdp'=16,'tp'=8] {'fsdp'}, dimensions={0} | all-to-all | bytes 3932160 | tf_op jit(solution)/shard_map/all_to_all | solution.py:189
  130.7 1.8 reduce_sum.59
  132.7 29.6 %all_to_all.54 = bf16[16,120,512]{2,1,0:T(8,128)(2,1)S(1)} all-to-all(bf16[16,120,512]{2,1,0:T(8,128)(2,1)S(1)} %broadcast_in_dim.7), channel_id=1, replica_groups=mesh['fsdp'=16,'tp'=8] {'fsdp'}, dimensions={0} | all-to-all | bytes 3932160 | tf_op jit(solution)/shard_map/all_to_all | solution.py:194
  162.3 1.3 convolution_bitcast_fusion.1
  163.6 2.8 convolution_convert_fusion.3
  167.3 3.5 all-to-all-start.5
  172.3 9.5 %all-to-all-done.5 = bf16[8,72,512]{2,1,0:T(8,128)(2,1)S(1)} async-done(((bf16[8,72,512]{2,1,0:T(8,128)(2,1)}), bf16[8,72,512]{2,1,0:T(8,128)(2,1)S(1)}, u32[]{:S(2)}, u32[]{:S(2)}) %all-to-all-start.5) | async-done | bytes 589856 | tf_op jit(solution)/shard_map/all_to_all | solution.py:286
  181.9 13.3 %all-gather = bf16[576,512]{1,0:T(8,128)(2,1)S(1)} all-gather(bf16[72,512]{1,0:T(8,128)(2,1)S(1)} %reduce_sum.60), channel_id=2, replica_groups=mesh['fsdp'=16,'tp'=8] {'tp'}, dimensions={0}, use_global_device_ids=true | all-gather | bytes 663552 | tf_op jit(solution)/shard_map/all_gather | solution.py:287
  196.7 3.6 all-to-all-start.6
  200.4 15.2 %all-to-all-done.6 = bf16[16,192,128]{2,1,0:T(8,128)(2,1)S(1)} async-done(((bf16[16,192,128]{2,1,0:T(8,128)(2,1)}), bf16[16,192,128]{2,1,0:T(8,128)(2,1)S(1)}, u32[]{:S(2)}, u32[]{:S(2)}) %all-to-all-start.6) | async-done | bytes 786464 | tf_op jit(solution)/shard_map/all_to_all | solution.py:293
  216.9 3.7 all-to-all-start.7
  221.6 2.5 fusion
  224.2 1.7 fusion.19
  225.8 11.9 %all-to-all-done.7 = bf16[16,256,128]{2,1,0:T(8,128)(2,1)S(1)} async-done(((bf16[16,256,128]{2,1,0:T(8,128)(2,1)}), bf16[16,256,128]{2,1,0:T(8,128)(2,1)S(1)}, u32[]{:S(2)}, u32[]{:S(2)}) %all-to-all-start.7) | async-done | bytes 1048608 | tf_op jit(solution)/shard_map/all_to_all | solution.py:194
  240.7 4.6 all-to-all-start.8
  245.4 85.3 %shard_map.92 = f32[512,512]{1,0:T(8,128)S(1)} custom-call(f32[512,512]{1,0:T(8,128)S(1)} %bitcast.73), custom_call_target="tpu_custom_call" | custom-call | flops 1000000 | bytes 1024 | tf_op jit(solution)/shard_map/pallas_call | solution.py:163
  332.5 83.4 %shard_map.93 = f32[512,512]{1,0:T(8,128)S(1)} custom-call(f32[512,512]{1,0:T(8,128)S(1)} %convolution_multiply_fusion.a_ref), custom_call_target="tpu_custom_call" | custom-call | flops 1000000 | bytes 1024 | tf_op jit(solution)/shard_map/pallas_call | solution.py:163
  416.9 1.9 fusion.21
  420.8 1.3 fusion.4
  422.1 1.3 fusion.6
  423.4 2.5 shard_map.94
  425.9 34.1 %all_to_all.55.got_ref = bf16[16,136,512]{2,1,0:T(8,128)(2,1)S(1)} all-to-all(bf16[16,136,512]{2,1,0:T(8,128)(2,1)S(1)} %shard_map.94), channel_id=1, replica_groups=mesh['fsdp'=16,'tp'=8] {'fsdp'}, dimensions={0} | all-to-all | bytes 4456448 | tf_op jit(solution)/shard_map/all_to_all | solution.py:314
  460.1 1.2 copy-done.3
  462.4 2.6 subtract_convert_fusion
  465.1 2.5 shard_map.95
  (77 shorter events, 17.1 us)
Async XLA Ops:
  0.6 1.6 copy-start
  68.2 1.3 copy-start.4
  98.2 1.2 copy-start.7
  132.7 29.6 %copy-start.5 = (bf16[16,120,512]{2,1,0:T(8,128)(2,1)S(1)}, bf16[16,120,512]{2,1,0:T(8,128)(2,1)}, u32[]{:S(2)}) copy-start(bf16[16,120,512]{2,1,0:T(8,128)(2,1)} %copy-done.4) | copy-start | bytes 5898244
  162.3 1.3 copy-start.6
  166.4 4.4 copy-start.19
  166.4 4.5 copy-start.20
  167.3 14.5 %all-to-all-start.5 = ((bf16[8,72,512]{2,1,0:T(8,128)(2,1)}), bf16[8,72,512]{2,1,0:T(8,128)(2,1)S(1)}, u32[]{:S(2)}, u32[]{:S(2)}) async-start(bf16[8,72,512]{2,1,0:T(8,128)(2,1)} %fusion.9), calls=%async_computation.5 | async-start | bytes 1179648 | tf_op jit(solution)/shard_map/all_to_all | solution.py:286
  181.9 13.8 %copy-start.15 = (bf16[64,16,120]{2,0,1:T(8,128)(2,1)S(1)}, bf16[64,16,120]{2,0,1:T(8,128)(2,1)}, u32[]{:S(2)}) copy-start(bf16[64,16,120]{2,0,1:T(8,128)(2,1)} %copy.13) | copy-start | bytes 737284
  195.2 5.1 %copy-start.13 = (bf16[576,512]{1,0:T(8,128)(2,1)}, bf16[576,512]{1,0:T(8,128)(2,1)S(1)}, u32[]{:S(2)}) copy-start(bf16[576,512]{1,0:T(8,128)(2,1)S(1)} %all-gather) | copy-start | bytes 1769476
  196.7 18.9 %all-to-all-start.6 = ((bf16[16,192,128]{2,1,0:T(8,128)(2,1)}), bf16[16,192,128]{2,1,0:T(8,128)(2,1)S(1)}, u32[]{:S(2)}, u32[]{:S(2)}) async-start(bf16[16,192,128]{2,1,0:T(8,128)(2,1)} %fusion.8), calls=%async_computation.6 | async-start | bytes 1572864 | tf_op jit(solution)/shard_map/all_to_all | solution.py:293
  215.6 1.3 copy-start.12
  216.9 20.8 %all-to-all-start.7 = ((bf16[16,256,128]{2,1,0:T(8,128)(2,1)}), bf16[16,256,128]{2,1,0:T(8,128)(2,1)S(1)}, u32[]{:S(2)}, u32[]{:S(2)}) async-start(bf16[16,256,128]{2,1,0:T(8,128)(2,1)} %broadcast_in_dim.8), calls=%async_computation.7 | async-start | bytes 2097152 | tf_op jit(solution)/shard_map/all_to_all | solution.py:194
  221.6 2.5 copy-start.9
  237.7 1.0 copy-start.11
  240.7 182.6 %all-to-all-start.8 = ((bf16[16,120,512]{2,1,0:T(8,128)(2,1)}), bf16[16,120,512]{2,1,0:T(8,128)(2,1)}, u32[]{:S(2)}, u32[]{:S(2)}) async-start(bf16[16,120,512]{2,1,0:T(8,128)(2,1)} %bitcast.86), calls=%async_computation.8 | async-start | bytes 3932160 | tf_op jit(solution)/shard_map/all_to_all | solution.py:309
  245.4 85.4 %copy-start.14 = (bf16[1,16,4,8,4,128]{5,3,4,2,0,1:T(8,128)(2,1)S(1)}, bf16[1,16,4,8,4,128]{5,3,4,2,0,1:T(8,128)(2,1)}, u32[]{:S(2)}) copy-start(bf16[1,16,4,8,4,128]{5,3,4,2,0,1:T(8,128)(2,1)} %slice.50) | copy-start | bytes 1572868
  416.9 2.5 copy-start.1
  416.9 1.9 copy-start.18
  416.9 2.2 copy-start.17
  418.8 1.0 copy-start.10
  419.1 1.2 copy-start.8
  422.1 1.3 copy-start.2
  459.9 1.4 copy-start.3
  459.9 1.4 copy-start.16
  459.9 2.5 copy-start.21

commit v12 on v11

--- a/solution.py
+++ b/solution.py
@@ -253,8 +253,9 @@
     return pl.pallas_call(
         functools.partial(unpack_kernel, width),
         out_shape=[shape, shape],
-        in_specs=[pl.BlockSpec(memory_space=pltpu.VMEM)],
-        out_specs=[pl.BlockSpec(memory_space=pltpu.VMEM)] * 2,
+        grid=(1,),
+        in_specs=[pl.BlockSpec((got.shape[0], 16, got.shape[2]), lambda i: (0, 0, 0))],
+        out_specs=[pl.BlockSpec(shape.shape, lambda i: (0, 0))] * 2,
         cost_estimate=pl.CostEstimate(flops=10**6, bytes_accessed=2**20, transcendentals=0),
     )(got)
 
@@ -301,7 +302,7 @@
     inverse = chol_inv(gram)
     second = chol_inv(mm_high(mm_high(inverse, outer, 1, 0), inverse, 1, 1) / M)
     both = mm_high(second, inverse, 1, 0)
-    margin = mm_high(gram, both, 0, 1)
+    margin = mm_split((gram * M).astype(BF), both, 0, 1) / M
     first_basis = mm_split(image, inverse, 1, 1).astype(BF)
     new_basis = (mm_split(wide, both, 1, 1) * inv_sqrt).astype(BF)
     rotated_one = mm(first_old, margin.astype(BF), 0, 0)[:share_cols]

time: 469 us -> 465 us (level)
    dot_general x14 -> x16, matrix products: 18.4 us -> 19.3 us  [mm(): lax.dot_general(a, b, (((ca,), (cb,)), ((), ())), preferred_element_type=...]
where the time goes in v12:
time: 465 us; the launch traced here: 464 us
  blocking collectives  200 us (43%)
  Pallas kernels  173 us (37%)
  waiting for transfers between devices  36.6 us (8%)
  matrix products  22.1 us (5%)
  starting transfers between devices  15.4 us (3%)
  local copies, waits for them, and re-layouts  11.3 us (2%)
    pallas_call x2, Pallas kernels, chol_inv(): pl.pallas_call(chol_kernel, out_shape=jax.ShapeDtypeStruct((n, n), F32),...  169 us
    all_to_all x3, blocking collectives, scatter_sum(): lax.all_to_all(x.astype(BF).reshape(n, x.shape[0] // n, x.shape[1]), axis...  80.6 us
    all_to_all x2, blocking collectives, gather(): lax.all_to_all(jnp.broadcast_to(x[None], (n,) + x.shape), axis, 0, 0, til...  59 us
    all_to_all x1, blocking collectives, per_device(): got = lax.all_to_all(got, 'fsdp', 0, 0, tiled=True)  34.1 us
    dot_general x16, matrix products, mm(): lax.dot_general(a, b, (((ca,), (cb,)), ((), ())), preferred_element_type=...  19.3 us
    all_to_all x1, waiting for transfers between devices, per_device(): got = lax.all_to_all(got, 'fsdp', 0, 0, tiled=True)  15.2 us
    all_gather x1, blocking collectives, per_device(): both = lax.all_gather(both, 'tp', axis=0, tiled=False)  13.3 us
    all_gather x1, blocking collectives, per_device(): image = lax.all_gather(image, 'tp', axis=0, tiled=True)  13.1 us
  transfers between devices with their start and end apart: 4, of which 3 were waited for; matrix products, arithmetic and copies ran while one was open for 3% of the time, Pallas kernels for 36%

profile of v12, /device:TPU:0, one launch (start us, length us, event | category | flops | bytes accessed | tf_op | source)
XLA Modules:
  0.0 464.2 jit_solution(13070245711571592216)
XLA Ops:
  0.7 1.5 copy-done
  2.2 2.3 convolution_convert_fusion.2
  4.4 33.9 %all_to_all.50 = bf16[16,120,512]{2,1,0:T(8,128)(2,1)S(1)} all-to-all(bf16[16,120,512]{2,1,0:T(8,128)(2,1)S(1)} %bitcast.89), channel_id=1, replica_groups=mesh['fsdp'=16,'tp'=8] {'fsdp'}, dimensions={0} | all-to-all | bytes 3932160 | tf_op jit(solution)/shard_map/all_to_all | solution.py:189
  38.8 29.4 %all_to_all.51 = bf16[16,120,512]{2,1,0:T(8,128)(2,1)S(1)} all-to-all(bf16[16,120,512]{2,1,0:T(8,128)(2,1)S(1)} %broadcast_in_dim.6), channel_id=1, replica_groups=mesh['fsdp'=16,'tp'=8] {'fsdp'}, dimensions={0} | all-to-all | bytes 3932160 | tf_op jit(solution)/shard_map/all_to_all | solution.py:194
  68.2 1.3 convolution_convert_fusion.4
  69.5 15.5 %all_to_all.52 = bf16[8,64,512]{2,1,0:T(8,128)(2,1)S(1)} all-to-all(bf16[8,64,512]{2,1,0:T(8,128)(2,1)S(1)} %bitcast.95), channel_id=1, replica_groups=mesh['fsdp'=16,'tp'=8] {'tp'}, dimensions={0} | all-to-all | bytes 1048576 | tf_op jit(solution)/shard_map/all_to_all | solution.py:189
  85.1 13.1 %all_gather.9 = bf16[512,512]{1,0:T(8,128)(2,1)S(1)} all-gather(bf16[64,512]{1,0:T(8,128)(2,1)S(1)} %reduce_sum.58), channel_id=1, replica_groups=mesh['fsdp'=16,'tp'=8] {'tp'}, dimensions={0}, use_global_device_ids=true | all-gather | bytes 589824 | tf_op jit(solution)/shard_map/all_gather | solution.py:278
  98.2 1.2 convolution_convert_fusion.1
  99.5 31.2 %all_to_all.53 = bf16[16,120,512]{2,1,0:T(8,128)(2,1)} all-to-all(bf16[16,120,512]{2,1,0:T(8,128)(2,1)S(1)} %bitcast.90), channel_id=1, replica_groups=mesh['fsdp'=16,'tp'=8] {'fsdp'}, dimensions={0} | all-to-all | bytes 3932160 | tf_op jit(solution)/shard_map/all_to_all | solution.py:189
  130.7 1.8 reduce_sum.59
  132.7 29.6 %all_to_all.54 = bf16[16,120,512]{2,1,0:T(8,128)(2,1)S(1)} all-to-all(bf16[16,120,512]{2,1,0:T(8,128)(2,1)S(1)} %broadcast_in_dim.7), channel_id=1, replica_groups=mesh['fsdp'=16,'tp'=8] {'fsdp'}, dimensions={0} | all-to-all | bytes 3932160 | tf_op jit(solution)/shard_map/all_to_all | solution.py:194
  162.3 1.3 convolution_bitcast_fusion.1
  163.6 2.8 convolution_convert_fusion.3
  167.3 3.5 all-to-all-start.5
  172.3 9.5 %all-to-all-done.5 = bf16[8,72,512]{2,1,0:T(8,128)(2,1)S(1)} async-done(((bf16[8,72,512]{2,1,0:T(8,128)(2,1)}), bf16[8,72,512]{2,1,0:T(8,128)(2,1)S(1)}, u32[]{:S(2)}, u32[]{:S(2)}) %all-to-all-start.5) | async-done | bytes 589856 | tf_op jit(solution)/shard_map/all_to_all | solution.py:287
  181.9 13.3 %all-gather = bf16[576,512]{1,0:T(8,128)(2,1)S(1)} all-gather(bf16[72,512]{1,0:T(8,128)(2,1)S(1)} %reduce_sum.60), channel_id=2, replica_groups=mesh['fsdp'=16,'tp'=8] {'tp'}, dimensions={0}, use_global_device_ids=true | all-gather | bytes 663552 | tf_op jit(solution)/shard_map/all_gather | solution.py:288
  196.7 3.6 all-to-all-start.6
  200.4 15.2 %all-to-all-done.6 = bf16[16,192,128]{2,1,0:T(8,128)(2,1)S(1)} async-done(((bf16[16,192,128]{2,1,0:T(8,128)(2,1)}), bf16[16,192,128]{2,1,0:T(8,128)(2,1)S(1)}, u32[]{:S(2)}, u32[]{:S(2)}) %all-to-all-start.6) | async-done | bytes 786464 | tf_op jit(solution)/shard_map/all_to_all | solution.py:294
  216.9 3.7 all-to-all-start.7
  221.6 2.5 fusion
  224.1 1.7 fusion.21
  225.8 11.9 %all-to-all-done.7 = bf16[16,256,128]{2,1,0:T(8,128)(2,1)S(1)} async-done(((bf16[16,256,128]{2,1,0:T(8,128)(2,1)}), bf16[16,256,128]{2,1,0:T(8,128)(2,1)S(1)}, u32[]{:S(2)}, u32[]{:S(2)}) %all-to-all-start.7) | async-done | bytes 1048608 | tf_op jit(solution)/shard_map/all_to_all | solution.py:194
  238.6 4.6 all-to-all-start.8
  243.4 85.3 %shard_map.92 = f32[512,512]{1,0:T(8,128)S(1)} custom-call(f32[512,512]{1,0:T(8,128)S(1)} %convert_multiply_fusion.a_ref), custom_call_target="tpu_custom_call" | custom-call | flops 1000000 | bytes 1024 | tf_op jit(solution)/shard_map/pallas_call | solution.py:163
  330.5 83.4 %shard_map.93 = f32[512,512]{1,0:T(8,128)S(1)} custom-call(f32[512,512]{1,0:T(8,128)S(1)} %convolution_multiply_fusion.a_ref), custom_call_target="tpu_custom_call" | custom-call | flops 1000000 | bytes 1024 | tf_op jit(solution)/shard_map/pallas_call | solution.py:163
  418.1 1.3 fusion.5
  419.4 1.3 fusion.7
  420.7 2.5 shard_map.94
  423.2 34.1 %all_to_all.55.got_ref = bf16[16,136,512]{2,1,0:T(8,128)(2,1)S(1)} all-to-all(bf16[16,136,512]{2,1,0:T(8,128)(2,1)S(1)} %shard_map.94), channel_id=1, replica_groups=mesh['fsdp'=16,'tp'=8] {'fsdp'}, dimensions={0} | all-to-all | bytes 4456448 | tf_op jit(solution)/shard_map/all_to_all | solution.py:315
  457.3 1.2 copy-done.1
  459.7 2.6 subtract_convert_fusion
  462.4 1.8 shard_map.95
  (72 shorter events, 15.1 us)
Async XLA Ops:
  0.6 1.6 copy-start
  68.2 1.3 copy-start.2
  98.2 1.2 copy-start.5
  132.7 29.6 %copy-start.3 = (bf16[16,120,512]{2,1,0:T(8,128)(2,1)S(1)}, bf16[16,120,512]{2,1,0:T(8,128)(2,1)}, u32[]{:S(2)}) copy-start(bf16[16,120,512]{2,1,0:T(8,128)(2,1)} %copy-done.2) | copy-start | bytes 5898244
  162.3 1.3 copy-start.4
  166.4 4.4 copy-start.16
  166.4 4.5 copy-start.17
  167.3 14.5 %all-to-all-start.5 = ((bf16[8,72,512]{2,1,0:T(8,128)(2,1)}), bf16[8,72,512]{2,1,0:T(8,128)(2,1)S(1)}, u32[]{:S(2)}, u32[]{:S(2)}) async-start(bf16[8,72,512]{2,1,0:T(8,128)(2,1)} %fusion.10), calls=%async_computation.5 | async-start | bytes 1179648 | tf_op jit(solution)/shard_map/all_to_all | solution.py:287
  181.9 13.8 %copy-start.12 = (bf16[64,16,120]{2,0,1:T(8,128)(2,1)S(1)}, bf16[64,16,120]{2,0,1:T(8,128)(2,1)}, u32[]{:S(2)}) copy-start(bf16[64,16,120]{2,0,1:T(8,128)(2,1)} %copy.13) | copy-start | bytes 737284
  195.2 5.1 %copy-start.10 = (bf16[576,512]{1,0:T(8,128)(2,1)}, bf16[576,512]{1,0:T(8,128)(2,1)S(1)}, u32[]{:S(2)}) copy-start(bf16[576,512]{1,0:T(8,128)(2,1)S(1)} %all-gather) | copy-start | bytes 1769476
  196.7 18.9 %all-to-all-start.6 = ((bf16[16,192,128]{2,1,0:T(8,128)(2,1)}), bf16[16,192,128]{2,1,0:T(8,128)(2,1)S(1)}, u32[]{:S(2)}, u32[]{:S(2)}) async-start(bf16[16,192,128]{2,1,0:T(8,128)(2,1)} %fusion.9), calls=%async_computation.6 | async-start | bytes 1572864 | tf_op jit(solution)/shard_map/all_to_all | solution.py:294
  215.6 1.3 copy-start.9
  216.9 20.9 %all-to-all-start.7 = ((bf16[16,256,128]{2,1,0:T(8,128)(2,1)}), bf16[16,256,128]{2,1,0:T(8,128)(2,1)S(1)}, u32[]{:S(2)}, u32[]{:S(2)}) async-start(bf16[16,256,128]{2,1,0:T(8,128)(2,1)} %broadcast_in_dim.8), calls=%async_computation.7 | async-start | bytes 2097152 | tf_op jit(solution)/shard_map/all_to_all | solution.py:194
  221.6 2.5 copy-start.7
  238.6 182.1 %all-to-all-start.8 = ((bf16[16,120,512]{2,1,0:T(8,128)(2,1)}), bf16[16,120,512]{2,1,0:T(8,128)(2,1)}, u32[]{:S(2)}, u32[]{:S(2)}) async-start(bf16[16,120,512]{2,1,0:T(8,128)(2,1)} %bitcast.88), calls=%async_computation.8 | async-start | bytes 3932160 | tf_op jit(solution)/shard_map/all_to_all | solution.py:310
  243.2 85.5 %copy-start.11 = (bf16[1,16,4,8,4,128]{5,3,4,2,0,1:T(8,128)(2,1)S(1)}, bf16[1,16,4,8,4,128]{5,3,4,2,0,1:T(8,128)(2,1)}, u32[]{:S(2)}) copy-start(bf16[1,16,4,8,4,128]{5,3,4,2,0,1:T(8,128)(2,1)} %get-tuple-element.27) | copy-start | bytes 1572868
  415.4 0.9 copy-start.15
  415.4 1.2 copy-start.14
  415.9 1.1 copy-start.8
  416.6 1.1 copy-start.6
  457.2 1.4 copy-start.1
  457.2 1.4 copy-start.13
  457.2 2.5 copy-start.18
